TPU v7x, 128 devices: a whole 4x4x4 slice. The times are simulated.
128 devices in a mesh: expert: 64 (over y, x, z), wshard: 2 (over core).
Axes of the slice: x: 4, y: 4, z: 4, core: 2. Of those that a mesh axis runs over, the one named last changes fastest.
Arguments:
- tokens: bfloat16 [16384, 768], P(('expert', 'wshard')), may hold values from -6 to 6
- lengths: int32 [32], replicated, may hold values from 1 to 1024, 16384 in all
- routes: int32 [16384, 1], P(('expert', 'wshard')), may hold values from 0 to 127; in each aligned block of 128 rows (0 to 127, 128 to 255, ...) at most 2 rows name the same one
- attn_gain: bfloat16 [768], P('wshard'), may hold values from 0.5 to 1.5
- query_weight: bfloat16 [768, 768], P('wshard'), may hold values from -0.21875 to 0.21875
- key_weight: bfloat16 [768, 768], P('wshard'), may hold values from -0.21875 to 0.21875
- value_weight: bfloat16 [768, 768], P('wshard'), may hold values from -0.21875 to 0.21875
- output_weight: bfloat16 [768, 768], P('wshard'), may hold values from -2.5 to 2.5
- bias_table: bfloat16 [32, 12], P('wshard'), may hold values from -6 to 6
- mix_gain: bfloat16 [768], P('wshard'), may hold values from 0.5 to 1.5
- router_weight: bfloat16 [768, 128], P('wshard'), may hold values from -0.109375 to 0.109375
- expert_in: bfloat16 [128, 768, 3072], P(('expert', 'wshard')), may hold values from -0.21875 to 0.21875
- expert_out: bfloat16 [128, 3072, 768], P(('expert', 'wshard')), may hold values from -14 to 14
- cotangent: bfloat16 [16384, 768], P(('expert', 'wshard')), may hold values from -6 to 6
Outputs:
- layer_out: bfloat16 [16384, 768], P(('expert', 'wshard'))
- tokens_grad: bfloat16 [16384, 768], P(('expert', 'wshard'))
- attn_gain_grad: float32 [768], P('wshard')
- query_grad: float32 [768, 768], P('wshard')
- key_grad: float32 [768, 768], P('wshard')
- value_grad: float32 [768, 768], P('wshard')
- output_grad: float32 [768, 768], P('wshard')
- bias_grad: float32 [32, 12], P('wshard')
- mix_gain_grad: float32 [768], P('wshard')
- router_grad: float32 [768, 128], P('wshard')
- expert_in_grad: bfloat16 [128, 768, 3072], P(('expert', 'wshard'))
- expert_out_grad: bfloat16 [128, 3072, 768], P(('expert', 'wshard'))
Inputs may be any that keep to these rules, and one draw needn't show every extreme that they name: `routes`: among the rows of one device (128 aligned rows) no expert is named more than 2 times, a bound that some block reaches. The lengths sum to 16384, and the longest is exactly 1024.
All inputs are finite; a program needn't handle non-finite values.
Results may differ from a plain program's by a relative error of at most 0.018.
Values may be sent and summed in bfloat16 or wider, within the bound.
A program may use at most 192 MiB of HBM per device.

v0:
```python
import math

import jax
import jax.numpy as jnp
from jax import lax
from jax.sharding import PartitionSpec as P

SPAN_DEV = 8


epsilon = 1e-06
far_edges = (12, 16, 23, 32, 46, 64, 91)


def passed_along(value, axis, steps):
    count = lax.axis_size(axis)
    initial, last = (max(0, -steps), min(count, count - steps))
    return lax.ppermute(value, axis, [(source, source + steps) for source in range(initial, last)])


def in_blocks(array, dim, length):
    shape = array.shape
    parts = array.reshape(*shape[:dim], length, shape[dim] // length, *shape[dim + 1 :])
    return jnp.moveaxis(parts, dim, 0)


def sum_at_owner(array, axis, dim):
    length = lax.axis_size(axis)
    parts = lax.all_to_all(in_blocks(array, dim, length), axis, 0, 0, tiled=True)
    return jnp.sum(parts.astype(jnp.float32), axis=0)


def side_by_side(arrays, axis, dim, along):
    widths = [math.prod(a.shape[along:]) for a in arrays]
    both = jnp.concatenate(
        [a.reshape(*a.shape[:along], w) for a, w in zip(arrays, widths)], axis=along
    )
    out = sum_at_owner(both, axis, dim)
    parts = jnp.split(out, [sum(widths[:k]) for k in range(1, len(widths))], axis=along)
    return tuple((b.reshape(*out.shape[:along], *a.shape[along:]) for a, b in zip(arrays, parts)))


def together(arrays, axis):
    ends = [0]
    for a in arrays:
        ends.append(ends[-1] + a.size)
    total = lax.psum(jnp.concatenate([a.ravel() for a in arrays]), axis)
    return tuple((total[b:e].reshape(a.shape) for a, b, e in zip(arrays, ends, ends[1:])))


def rms_scale(values, gain):
    return values * lax.rsqrt(jnp.mean(values * values, axis=-1, keepdims=True) + epsilon) * gain


def bucket_of(relative):
    distance = jnp.abs(relative)
    far_bucket = 8 + sum(((distance >= edge).astype(jnp.int32) for edge in far_edges))
    near_far = jnp.where(distance < 8, distance, far_bucket)
    return near_far + 16 * (relative > 0).astype(jnp.int32)


def segment_ids(positions, seq_ends, total_rows):
    counted = jnp.sum((seq_ends[None, :] <= positions[:, None]).astype(jnp.int32), axis=1)
    return jnp.where((positions >= 0) & (positions < total_rows), counted, -1)


def bucket_table(query_pos, key_pos, bucket_count):
    buckets = bucket_of(key_pos[None, :] - query_pos[:, None])
    return (buckets[:, :, None] == jnp.arange(bucket_count, dtype=jnp.int32)[None, None, :]).astype(
        jnp.bfloat16
    )


def masked_scores(query_rows, key_rows, table_full, bucket_onehot, allowed):
    scale = query_rows.shape[-1] ** (-0.5)
    raw = (
        jnp.einsum("qhe,khe->hqk", query_rows, key_rows, preferred_element_type=jnp.float32) * scale
    )
    raw = raw + jnp.einsum(
        "qkb,bh->hqk", bucket_onehot, table_full, preferred_element_type=jnp.float32
    )
    return jnp.where(allowed[None], raw, -1000000000.0)


def per_device(
    tokens,
    lengths,
    routes,
    attn_gain,
    query_weight,
    key_weight,
    value_weight,
    output_weight,
    bias_table,
    mix_gain,
    router_weight,
    expert_in,
    expert_out,
    cotangent,
):
    (
        gain_one,
        weight_query,
        weight_key,
        weight_value,
        weight_output,
        table_full,
        gain_two,
        weight_router,
    ) = (
        lax.all_gather(attn_gain, "wshard", axis=0, tiled=True),
        lax.all_gather(query_weight, "wshard", axis=0, tiled=True),
        lax.all_gather(key_weight, "wshard", axis=0, tiled=True),
        lax.all_gather(value_weight, "wshard", axis=0, tiled=True),
        lax.all_gather(output_weight, "wshard", axis=0, tiled=True),
        lax.all_gather(bias_table, "wshard", axis=0, tiled=True),
        lax.all_gather(mix_gain, "wshard", axis=0, tiled=True),
        lax.all_gather(router_weight, "wshard", axis=0, tiled=True),
    )
    tok_count, model_width = tokens.shape
    head_count = table_full.shape[1]
    bucket_count = table_full.shape[0]
    head_size = model_width // head_count
    scale = head_size ** (-0.5)
    expert_count = lax.axis_size("expert")
    shard_count = lax.axis_size("wshard")
    device_count = expert_count * shard_count
    my_index = lax.axis_index("expert") * shard_count + lax.axis_index("wshard")
    total_rows = device_count * tok_count
    capacity = max(2, 2 * tok_count // device_count)
    window_count = 2 * SPAN_DEV + 1
    seq_ends = jnp.cumsum(lengths)
    query_pos = my_index * tok_count + jnp.arange(tok_count, dtype=jnp.int32)
    key_pos = (my_index - SPAN_DEV) * tok_count + jnp.arange(
        window_count * tok_count, dtype=jnp.int32
    )
    allowed = (
        segment_ids(query_pos, seq_ends, total_rows)[:, None]
        == segment_ids(key_pos, seq_ends, total_rows)[None, :]
    )
    bucket_onehot = bucket_table(query_pos, key_pos, bucket_count)
    gain_first = gain_one.astype(jnp.float32)
    gain_second = gain_two.astype(jnp.float32)
    inputs = tokens.astype(jnp.float32)
    normed = rms_scale(inputs, gain_first).astype(jnp.bfloat16)
    query_rows = (
        jnp.dot(normed, weight_query, preferred_element_type=jnp.float32)
        .astype(jnp.bfloat16)
        .reshape(tok_count, head_count, head_size)
    )
    key_rows = (
        jnp.dot(normed, weight_key, preferred_element_type=jnp.float32)
        .astype(jnp.bfloat16)
        .reshape(tok_count, head_count, head_size)
    )
    value_rows = (
        jnp.dot(normed, weight_value, preferred_element_type=jnp.float32)
        .astype(jnp.bfloat16)
        .reshape(tok_count, head_count, head_size)
    )
    key_list = []
    value_list = []
    for offset in range(-SPAN_DEV, SPAN_DEV + 1):
        if offset == 0:
            key_list.append(key_rows)
            value_list.append(value_rows)
        else:
            got_keys, got_values = passed_along(
                (key_rows, value_rows), ("expert", "wshard"), -offset
            )
            key_list.append(got_keys)
            value_list.append(got_values)
    window_keys = jnp.concatenate(key_list, axis=0)
    window_values = jnp.concatenate(value_list, axis=0)
    scores = masked_scores(query_rows, window_keys, table_full, bucket_onehot, allowed)
    row_top = jnp.max(scores, axis=-1, keepdims=True)
    log_total = row_top + jnp.log(jnp.sum(jnp.exp(scores - row_top), axis=-1, keepdims=True))
    probs_low = jnp.exp(scores - log_total).astype(jnp.bfloat16)
    attended = (
        jnp.einsum("hqk,khe->qhe", probs_low, window_values, preferred_element_type=jnp.float32)
        .astype(jnp.bfloat16)
        .reshape(tok_count, model_width)
    )
    hidden = inputs + jnp.dot(attended, weight_output, preferred_element_type=jnp.float32)
    mixed = rms_scale(hidden, gain_second).astype(jnp.bfloat16)
    logits = jnp.dot(mixed, weight_router, preferred_element_type=jnp.float32)
    router = jax.nn.softmax(logits, axis=-1)
    route_ids = routes[:, 0]
    chosen = route_ids[:, None] == jnp.arange(device_count, dtype=jnp.int32)[None, :]
    chosen_float = chosen.astype(jnp.float32)
    gate_value = jnp.sum(router * chosen_float, axis=1)
    slot_rank = (
        jnp.sum(jnp.cumsum(chosen.astype(jnp.int32), axis=0) * chosen.astype(jnp.int32), axis=1) - 1
    )
    slot_index = route_ids * capacity + slot_rank
    place_matrix = (
        slot_index[None, :] == jnp.arange(device_count * capacity, dtype=jnp.int32)[:, None]
    ).astype(jnp.bfloat16)
    place_exact = place_matrix.astype(jnp.float32)
    sent_rows = jnp.dot(place_matrix, mixed, preferred_element_type=jnp.float32).astype(
        jnp.bfloat16
    )
    arrived = lax.all_to_all(
        sent_rows.reshape(device_count, capacity, model_width),
        ("expert", "wshard"),
        split_axis=0,
        concat_axis=0,
        tiled=True,
    )
    arrived = arrived.reshape(device_count * capacity, model_width)
    block_in = expert_in[0]
    block_out = expert_out[0]
    pre_act = jnp.dot(arrived, block_in, preferred_element_type=jnp.float32)
    act_rows = jax.nn.gelu(pre_act, approximate=False).astype(jnp.bfloat16)
    made_rows = jnp.dot(act_rows, block_out, preferred_element_type=jnp.float32).astype(
        jnp.bfloat16
    )
    made_home = lax.all_to_all(
        made_rows.reshape(device_count, capacity, model_width),
        ("expert", "wshard"),
        split_axis=0,
        concat_axis=0,
        tiled=True,
    )
    made_token = jnp.einsum(
        "st,sd->td",
        place_matrix,
        made_home.reshape(device_count * capacity, model_width),
        preferred_element_type=jnp.float32,
    )
    layer_out = (hidden + gate_value[:, None] * made_token).astype(jnp.bfloat16)
    out_grad = cotangent.astype(jnp.float32)
    made_grad = (gate_value[:, None] * out_grad).astype(jnp.bfloat16)
    gate_grad = jnp.sum(out_grad * made_token, axis=1)
    grad_sent = jnp.dot(place_matrix, made_grad, preferred_element_type=jnp.float32).astype(
        jnp.bfloat16
    )
    grad_rows = lax.all_to_all(
        grad_sent.reshape(device_count, capacity, model_width),
        ("expert", "wshard"),
        split_axis=0,
        concat_axis=0,
        tiled=True,
    )
    grad_rows = grad_rows.reshape(device_count * capacity, model_width)
    expert_out_grad = jnp.einsum(
        "rf,rd->fd", act_rows, grad_rows, preferred_element_type=jnp.float32
    ).astype(jnp.bfloat16)
    act_grad = jnp.einsum("rd,fd->rf", grad_rows, block_out, preferred_element_type=jnp.float32)
    gelu_back = jax.vjp(lambda value_in: jax.nn.gelu(value_in, approximate=False), pre_act)[1]
    pre_grad = gelu_back(act_grad)[0].astype(jnp.bfloat16)
    expert_in_grad = jnp.einsum(
        "rd,rf->df", arrived, pre_grad, preferred_element_type=jnp.float32
    ).astype(jnp.bfloat16)
    expert_back = jnp.einsum("rf,df->rd", pre_grad, block_in, preferred_element_type=jnp.float32)
    back_home = lax.all_to_all(
        expert_back.reshape(device_count, capacity, model_width).astype(jnp.bfloat16),
        ("expert", "wshard"),
        split_axis=0,
        concat_axis=0,
        tiled=True,
    ).astype(jnp.float32)
    expert_mixed_grad = jnp.einsum(
        "st,sd->td",
        place_exact,
        back_home.reshape(device_count * capacity, model_width),
        precision=lax.Precision.HIGHEST,
        preferred_element_type=jnp.float32,
    )
    logit_grad = ((gate_grad * gate_value)[:, None] * (chosen_float - router)).astype(jnp.bfloat16)
    router_grad = jnp.einsum("td,te->de", mixed, logit_grad, preferred_element_type=jnp.float32)
    mixed_grad = (
        jnp.einsum("te,de->td", logit_grad, weight_router, preferred_element_type=jnp.float32)
        + expert_mixed_grad
    )
    norm_two_back = jax.vjp(rms_scale, hidden, gain_second)[1]
    hidden_part, mix_gain_grad = norm_two_back(mixed_grad)
    hidden_grad = out_grad + hidden_part
    branch_grad = hidden_grad.astype(jnp.bfloat16)
    output_grad = jnp.einsum("td,te->de", attended, branch_grad, preferred_element_type=jnp.float32)
    attended_grad = (
        jnp.einsum("te,de->td", branch_grad, weight_output, preferred_element_type=jnp.float32)
        .astype(jnp.bfloat16)
        .reshape(tok_count, head_count, head_size)
    )
    again_keys = []
    again_values = []
    for offset in range(-SPAN_DEV, SPAN_DEV + 1):
        if offset == 0:
            again_keys.append(key_rows)
            again_values.append(value_rows)
        else:
            got_keys, got_values = passed_along(
                (key_rows, value_rows), ("expert", "wshard"), -offset
            )
            again_keys.append(got_keys)
            again_values.append(got_values)
    back_keys = jnp.concatenate(again_keys, axis=0)
    back_values = jnp.concatenate(again_values, axis=0)
    scores_again = masked_scores(query_rows, back_keys, table_full, bucket_onehot, allowed)
    probs = jnp.exp(scores_again - log_total)
    prob_grad = jnp.einsum(
        "qhe,khe->hqk", attended_grad, back_values, preferred_element_type=jnp.float32
    )
    row_dot = jnp.sum(probs * prob_grad, axis=-1)
    score_grad = (probs * (prob_grad - row_dot[:, :, None])).astype(jnp.bfloat16)
    bias_grad = jnp.einsum(
        "hqk,qkb->bh", score_grad, bucket_onehot, preferred_element_type=jnp.float32
    )
    query_back = (
        (
            jnp.einsum("hqk,khe->qhe", score_grad, back_keys, preferred_element_type=jnp.float32)
            * scale
        )
        .astype(jnp.bfloat16)
        .reshape(tok_count, model_width)
    )
    probs_again = probs.astype(jnp.bfloat16)
    key_part = (
        jnp.einsum("hqk,qhe->khe", score_grad, query_rows, preferred_element_type=jnp.float32)
        * scale
    )
    value_part = jnp.einsum(
        "hqk,qhe->khe", probs_again, attended_grad, preferred_element_type=jnp.float32
    )
    key_total = key_part[SPAN_DEV * tok_count : (SPAN_DEV + 1) * tok_count]
    value_total = value_part[SPAN_DEV * tok_count : (SPAN_DEV + 1) * tok_count]
    for offset in range(-SPAN_DEV, SPAN_DEV + 1):
        if offset != 0:
            lower = (offset + SPAN_DEV) * tok_count
            got_key_part, got_value_part = (
                passed_along(
                    key_part[lower : lower + tok_count].astype(jnp.bfloat16),
                    ("expert", "wshard"),
                    offset,
                ).astype(jnp.float32),
                passed_along(
                    value_part[lower : lower + tok_count].astype(jnp.bfloat16),
                    ("expert", "wshard"),
                    offset,
                ).astype(jnp.float32),
            )
            key_total = key_total + got_key_part
            value_total = value_total + got_value_part
    key_back = key_total.astype(jnp.bfloat16).reshape(tok_count, model_width)
    value_back = value_total.astype(jnp.bfloat16).reshape(tok_count, model_width)
    query_grad = jnp.einsum("td,te->de", normed, query_back, preferred_element_type=jnp.float32)
    key_grad = jnp.einsum("td,te->de", normed, key_back, preferred_element_type=jnp.float32)
    value_grad = jnp.einsum("td,te->de", normed, value_back, preferred_element_type=jnp.float32)
    normed_grad = jnp.einsum(
        "te,de->td", query_back, weight_query, preferred_element_type=jnp.float32
    )
    normed_grad = normed_grad + jnp.einsum(
        "te,de->td", key_back, weight_key, preferred_element_type=jnp.float32
    )
    normed_grad = normed_grad + jnp.einsum(
        "te,de->td", value_back, weight_value, preferred_element_type=jnp.float32
    )
    norm_one_back = jax.vjp(rms_scale, inputs, gain_first)[1]
    input_part, attn_gain_grad = norm_one_back(normed_grad)
    tokens_grad = (hidden_grad + input_part).astype(jnp.bfloat16)
    shares = (
        *side_by_side(
            (
                attn_gain_grad.astype(jnp.bfloat16),
                query_grad.astype(jnp.bfloat16),
                key_grad.astype(jnp.bfloat16),
                value_grad.astype(jnp.bfloat16),
                output_grad.astype(jnp.bfloat16),
            ),
            "wshard",
            0,
            1,
        ),
        sum_at_owner(bias_grad.astype(jnp.bfloat16), "wshard", 0),
        *side_by_side(
            (mix_gain_grad.astype(jnp.bfloat16), router_grad.astype(jnp.bfloat16)), "wshard", 0, 1
        ),
    )
    totals = together(
        (shares[0], shares[1], shares[2], shares[3], shares[4], shares[5], shares[6], shares[7]),
        "expert",
    )
    return (
        layer_out,
        tokens_grad,
        totals[0],
        totals[1],
        totals[2],
        totals[3],
        totals[4],
        totals[5],
        totals[6],
        totals[7],
        expert_in_grad[None],
        expert_out_grad[None],
    )


def solution(mesh):
    placed = (
        P(("expert", "wshard"), None),
        P(),
        P(("expert", "wshard"), None),
        P("wshard"),
        P("wshard", None),
        P("wshard", None),
        P("wshard", None),
        P("wshard", None),
        P("wshard", None),
        P("wshard"),
        P("wshard", None),
        P(("expert", "wshard"), None, None),
        P(("expert", "wshard"), None, None),
        P(("expert", "wshard"), None),
    )
    return jax.shard_map(
        per_device,
        mesh=mesh,
        in_specs=placed,
        out_specs=(
            P(("expert", "wshard"), None),
            P(("expert", "wshard"), None),
            P("wshard"),
            P("wshard", None),
            P("wshard", None),
            P("wshard", None),
            P("wshard", None),
            P("wshard", None),
            P("wshard"),
            P("wshard", None),
            P(("expert", "wshard"), None, None),
            P(("expert", "wshard"), None, None),
        ),
        check_vma=False,
    )
```

profile of v0, /device:TPU:8, one launch (start us, length us, event | category | flops | bytes accessed | tf_op | source)
XLA Modules:
  0.0 802.5 jit_solution(16977075453275256730)
XLA Ops:
  16.7 9.7 %fusion.1 = f32[128,2176,12]{0,2,1:T(8,128)} fusion(s32[128,2176]{0,1:T(8,128)S(1)} %fusion.47, bf16[32,12]{1,0:T(8,128)(2,1)S(1)} %all_gather.28), kind=kOutput, calls=%fused_computation.2 | convolution fusion | flops 222822400 | bytes 14484224 | tf_op jit(solution)/shard_map/qkb,bh->hqk/dot_general | solution.py:79
  26.4 17.2 %copy.176 = f32[128,2176,12]{1,0,2:T(8,128)} copy(f32[128,2176,12]{0,2,1:T(8,128)} %fusion.1) | data formatting | bytes 26738688 | tf_op jit(solution)/shard_map/qkb,bh->hqk/dot_general | solution.py:79
  53.8 5.2 collective-permute-start.1
  76.2 4.1 collective-permute-start.18
  80.4 3.9 collective-permute-start.19
  86.8 4.4 collective-permute-start.20
  94.8 4.1 collective-permute-done.20
  106.9 3.8 collective-permute-done.22
  119.3 10.4 %collective-permute-done.25 = bf16[128,12,64]{0,2,1:T(8,128)(2,1)S(1)} collective-permute-done((bf16[128,12,64]{0,2,1:T(8,128)(2,1)S(1)}, bf16[128,12,64]{0,2,1:T(8,128)(2,1)S(1)}, u32[]{:S(2)}, u32[]{:S(2)}) %collective-permute-start.25) | collective-permute-done | bytes 196640 | tf_op jit(solution)/shard_map/ppermute | solution.py:18
  133.6 5.7 collective-permute-done.27
  157.4 6.4 collective-permute-start.4
  163.8 7.9 fusion.120
  182.6 7.9 collective-permute-start.8
  191.5 3.9 collective-permute-start.9
  197.5 5.4 collective-permute-start.11
  211.2 8.8 %collective-permute-done.12 = bf16[128,12,64]{0,2,1:T(8,128)(2,1)S(1)} collective-permute-done((bf16[128,12,64]{0,2,1:T(8,128)(2,1)S(1)}, bf16[128,12,64]{0,2,1:T(8,128)(2,1)S(1)}, u32[]{:S(2)}, u32[]{:S(2)}) %collective-permute-start.12) | collective-permute-done | bytes 196640 | tf_op jit(solution)/shard_map/ppermute | solution.py:18
  221.3 3.9 collective-permute-done.15
  233.9 6.1 all-to-all-start
  241.6 10.3 %all-to-all-done = bf16[128,2,768]{2,1,0:T(2,128)(2,1)S(1)} async-done(((bf16[128,2,768]{2,1,0:T(2,128)(2,1)}), bf16[128,2,768]{2,1,0:T(2,128)(2,1)S(1)}, u32[]{:S(2)}, u32[]{:S(2)}) %all-to-all-start) | async-done | bytes 393248 | tf_op jit(solution)/shard_map/all_to_all | solution.py:203
  251.9 5.4 all-to-all-start.2
  257.5 11.1 %multiply_convert_fusion.1 = (bf16[256,3072]{1,0:T(8,128)(2,1)S(1)}, f32[256,3072]{1,0:T(8,128)}, f32[256,3072]{1,0:T(8,128)}) fusion(bf16[256,768]{1,0:T(8,128)(2,1)S(1)} %reshape.366, bf16[1,768,3072]{2,1,0:T(8,128)(2,1)} %param.25), kind=kOutput, calls=%fused_computation.31 | convolution fusion | flops 1259077632 | bytes 12976128 | tf_op jit(solution)/shard_map/dot_general | solution.py:213
  274.4 9.8 %all-to-all-start.1 = ((bf16[128,2,768]{2,1,0:T(2,128)(2,1)}), bf16[128,2,768]{2,1,0:T(2,128)(2,1)S(1)}, u32[]{:S(2)}, u32[]{:S(2)}) async-start(bf16[128,2,768]{2,1,0:T(2,128)(2,1)} %reshape.367), calls=%async_computation.1 | async-start | bytes 786432 | tf_op jit(solution)/shard_map/all_to_all | solution.py:218
  284.4 6.2 add_convert_fusion
  292.4 4.3 fusion.38
  297.9 10.5 %all-to-all-start.3 = ((bf16[128,2,768]{2,1,0:T(2,128)(2,1)}), bf16[128,2,768]{2,1,0:T(2,128)(2,1)}, u32[]{:S(2)}, u32[]{:S(2)}) async-start(bf16[128,2,768]{2,1,0:T(2,128)(2,1)} %copy.180), calls=%async_computation.3 | async-start | bytes 786432 | tf_op jit(solution)/shard_map/all_to_all | solution.py:256
  311.1 8.8 %all-to-all-done.3 = bf16[128,2,768]{2,1,0:T(2,128)(2,1)} async-done(((bf16[128,2,768]{2,1,0:T(2,128)(2,1)}), bf16[128,2,768]{2,1,0:T(2,128)(2,1)}, u32[]{:S(2)}, u32[]{:S(2)}) %all-to-all-start.3) | async-done | bytes 393248 | tf_op jit(solution)/shard_map/all_to_all | solution.py:256
  331.8 12.1 %multiply_reduce_fusion = (f32[12,128]{1,0:T(8,128)}, f32[12,128,2176]{2,1,0:T(8,128)}) fusion(f32[12,128,2176]{2,1,0:T(8,128)} %copy-done, f32[12,128]{1,0:T(8,128)S(1)} %log_add_fusion, bf16[128,12,64]{0,2,1:T(8,128)(2,1)} %bitcast.112, bf16[2176,12,64]{0,2,1:T(8,128)(2,1)S(1)} %copy-done.4), kind=kOutput, calls=%fused_computation.8 | convolution fusion | flops 437844480 | bytes 30289920 | tf_op jit(solution)/shard_map/qhe,khe->hqk/dot_general | solution.py:302
  345.1 6.9 multiply_convert_fusion
  355.2 3.9 fusion.122
  359.1 5.2 fusion.123
  365.8 12.9 %copy.191 = bf16[12,128,2176]{1,0,2:T(8,128)(2,1)} copy(bf16[12,128,2176]{2,1,0:T(8,128)(2,1)} %copy-done.1) | data formatting | bytes 13369344 | tf_op jit(solution)/shard_map/convert_element_type | solution.py:306
  387.5 4.6 collective-permute-start.44
  392.1 3.9 collective-permute-start.43
  399.5 8.6 %fusion.49 = bf16[32,12]{0,1:T(8,128)(2,1)} fusion(bf16[12,128,2176]{1,0,2:T(8,128)(2,1)} %copy.191, s32[128,2176]{0,1:T(8,128)} %copy-done.8), kind=kOutput, calls=%fused_computation.78 | convolution fusion | flops 222822784 | bytes 7799552 | tf_op jit(solution)/shard_map/hqk,qkb->bh/dot_general | solution.py:307
  414.6 4.5 collective-permute-start.42
  427.5 4.1 all-to-all-start.6
  434.1 7.4 collective-permute-start.39
  476.8 4.2 collective-permute-start.60
  481.7 4.6 collective-permute-start.59
  486.3 4.3 collective-permute-start.58
  498.0 7.9 collective-permute-start.55
  527.7 5.0 collective-permute-done.51
  536.3 7.1 collective-permute-done.48
  553.3 25.0 %concatenate.35 = bf16[2,384,3073]{1,2,0:T(8,128)(2,1)} concatenate(bf16[2,384,1]{1,2,0:T(2,128)(2,1)S(1)} %convert_element_type.433, bf16[2,384,768]{1,2,0:T(8,128)(2,1)S(1)} %copy-done.15, bf16[2,384,768]{1,2,0:T(8,128)(2,1)} %copy.184, bf16[2,384,768]{1,2,0:T(8,128)(2,1)} %copy.185, bf16[2,384,768]{1,2,0:T(8,128)(2,1)S(1)} %copy-done.16), dimensions={2} | concatenate | bytes 9440256 | tf_op jit(solution)/shard_map/concatenate | solution.py:35
  578.3 9.2 %all_to_all.35 = bf16[2,384,3073]{1,2,0:T(8,128)(2,1)S(1)} all-to-all(bf16[2,384,3073]{1,2,0:T(8,128)(2,1)} %concatenate.35), channel_id=1, replica_groups=mesh['expert'=64,'wshard'=2] {'wshard'}, dimensions={0} | all-to-all | bytes 9440256 | tf_op jit(solution)/shard_map/all_to_all | solution.py:29
  605.6 38.6 %concatenate.38 = f32[1229760]{0:T(1024)} concatenate(f32[384]{0:T(512)S(1)} %slice_reduce_fusion.1, f32[294912]{0:T(1024)S(1)} %reshape.377, f32[294912]{0:T(1024)S(1)} %reshape.378, f32[294912]{0:T(1024)} %reshape.379, f32[294912]{0:T(1024)} %reshape.380, f32[192]{0:T(256)S(1)} %copy-done.55, f32[384]{0:T(512)S(1)} %slice_reduce_fusion, f32[49152]{0:T(1024)S(1)} %bitcast.156), dimensions={0} | concatenate | bytes 9838080 | tf_op jit(solution)/shard_map/concatenate | solution.py:47
  645.6 5.0 fusion.14
  655.1 126.2 %all-reduce.2.cloned.1.call-done = f32[1229760]{0:T(1024)} async-done(((f32[1229760]{0:T(1024)}), f32[1229760]{0:T(1024)}) %all-reduce.2.cloned.1.call-update) | async-done | bytes 4919056 | tf_op jit(solution)/shard_map/psum | solution.py:47
  (409 shorter events, 289.5 us)
Async XLA Ops:
  7.2 41.4 %all-gather.7.cloned.1.call-start = ((), (), s32[]{:S(2)}) async-start(), calls=%async_computation.7 | async-start | bytes 1769472 | tf_op jit(solution)/shard_map/all_gather | solution.py:114
  7.9 54.7 %all-gather.11.cloned.1.call-start = ((), (), s32[]{:S(2)}) async-start(), calls=%async_computation.9 | async-start | bytes 1769472 | tf_op jit(solution)/shard_map/all_gather | solution.py:113
  8.7 62.0 %all-gather.9.cloned.1.call-start = ((), (), s32[]{:S(2)}) async-start(), calls=%async_computation.8 | async-start | bytes 1769472 | tf_op jit(solution)/shard_map/all_gather | solution.py:112
  9.4 220.6 %all-gather.13.cloned.1.call-start = ((), (), s32[]{:S(2)}) async-start(), calls=%async_computation.10 | async-start | bytes 1769472 | tf_op jit(solution)/shard_map/all_gather | solution.py:115
  50.4 123.3 %collective-permute-start = (bf16[128,12,64]{0,2,1:T(8,128)(2,1)S(1)}, bf16[128,12,64]{0,2,1:T(8,128)(2,1)}, u32[]{:S(2)}, u32[]{:S(2)}) collective-permute-start(bf16[128,12,64]{0,2,1:T(8,128)(2,1)S(1)} %bitcast.122), channel_id=1, source_target_pairs={{0,8},{1,9},{2,10},{3,11},{4,12},{5,13},{6,14},{7,15},{8,16},{9,17... | collective-permute-start | bytes 589832 | tf_op jit(solution)/shard_map/ppermute | solution.py:18
  53.8 123.0 %collective-permute-start.1 = (bf16[128,12,64]{0,2,1:T(8,128)(2,1)S(1)}, bf16[128,12,64]{0,2,1:T(8,128)(2,1)}, u32[]{:S(2)}, u32[]{:S(2)}) collective-permute-start(bf16[128,12,64]{0,2,1:T(8,128)(2,1)S(1)} %bitcast.123), channel_id=1, source_target_pairs={{0,7},{1,8},{2,9},{3,10},{4,11},{5,12},{6,13},{7,14},{8,15},{9,16}... | collective-permute-start | bytes 589832 | tf_op jit(solution)/shard_map/ppermute | solution.py:18
  59.1 120.6 %collective-permute-start.2 = (bf16[128,12,64]{0,2,1:T(8,128)(2,1)S(1)}, bf16[128,12,64]{0,2,1:T(8,128)(2,1)}, u32[]{:S(2)}, u32[]{:S(2)}) collective-permute-start(bf16[128,12,64]{0,2,1:T(8,128)(2,1)S(1)} %bitcast.124), channel_id=1, source_target_pairs={{0,6},{1,7},{2,8},{3,9},{4,10},{5,11},{6,12},{7,13},{8,14},{9,15},... | collective-permute-start | bytes 589832 | tf_op jit(solution)/shard_map/ppermute | solution.py:18
  153.2 29.4 %collective-permute-start.3 = (bf16[128,12,64]{0,2,1:T(8,128)(2,1)S(1)}, bf16[128,12,64]{0,2,1:T(8,128)(2,1)}, u32[]{:S(2)}, u32[]{:S(2)}) collective-permute-start(bf16[128,12,64]{0,2,1:T(8,128)(2,1)S(1)} %bitcast.125), channel_id=1, source_target_pairs={{0,5},{1,6},{2,7},{3,8},{4,9},{5,10},{6,11},{7,12},{8,13},{9,14},{... | collective-permute-start | bytes 589832 | tf_op jit(solution)/shard_map/ppermute | solution.py:18
  157.4 34.1 %collective-permute-start.4 = (bf16[128,12,64]{0,2,1:T(8,128)(2,1)S(1)}, bf16[128,12,64]{0,2,1:T(8,128)(2,1)S(1)}, u32[]{:S(2)}, u32[]{:S(2)}) collective-permute-start(bf16[128,12,64]{0,2,1:T(8,128)(2,1)S(1)} %bitcast.126), channel_id=1, source_target_pairs={{0,4},{1,5},{2,6},{3,7},{4,8},{5,9},{6,10},{7,11},{8,12},{9,13},{1... | collective-permute-start | bytes 589832 | tf_op jit(solution)/shard_map/ppermute | solution.py:18
  173.7 21.8 %collective-permute-start.5 = (bf16[128,12,64]{0,2,1:T(8,128)(2,1)S(1)}, bf16[128,12,64]{0,2,1:T(8,128)(2,1)S(1)}, u32[]{:S(2)}, u32[]{:S(2)}) collective-permute-start(bf16[128,12,64]{0,2,1:T(8,128)(2,1)S(1)} %bitcast.127), channel_id=1, source_target_pairs={{0,3},{1,4},{2,5},{3,6},{4,7},{5,8},{6,9},{7,10},{8,11},{9,12},{10... | collective-permute-start | bytes 589832 | tf_op jit(solution)/shard_map/ppermute | solution.py:18
  176.8 20.7 %collective-permute-start.6 = (bf16[128,12,64]{0,2,1:T(8,128)(2,1)S(1)}, bf16[128,12,64]{0,2,1:T(8,128)(2,1)S(1)}, u32[]{:S(2)}, u32[]{:S(2)}) collective-permute-start(bf16[128,12,64]{0,2,1:T(8,128)(2,1)S(1)} %bitcast.128), channel_id=1, source_target_pairs={{0,2},{1,3},{2,4},{3,5},{4,6},{5,7},{6,8},{7,9},{8,10},{9,11},{10,... | collective-permute-start | bytes 589832 | tf_op jit(solution)/shard_map/ppermute | solution.py:18
  179.7 23.3 %collective-permute-start.7 = (bf16[128,12,64]{0,2,1:T(8,128)(2,1)S(1)}, bf16[128,12,64]{0,2,1:T(8,128)(2,1)S(1)}, u32[]{:S(2)}, u32[]{:S(2)}) collective-permute-start(bf16[128,12,64]{0,2,1:T(8,128)(2,1)S(1)} %bitcast.129), channel_id=1, source_target_pairs={{0,1},{1,2},{2,3},{3,4},{4,5},{5,6},{6,7},{7,8},{8,9},{9,10},{10,1... | collective-permute-start | bytes 589832 | tf_op jit(solution)/shard_map/ppermute | solution.py:18
  182.6 22.5 %collective-permute-start.8 = (bf16[128,12,64]{0,2,1:T(8,128)(2,1)S(1)}, bf16[128,12,64]{0,2,1:T(8,128)(2,1)S(1)}, u32[]{:S(2)}, u32[]{:S(2)}) collective-permute-start(bf16[128,12,64]{0,2,1:T(8,128)(2,1)S(1)} %bitcast.130), channel_id=1, source_target_pairs={{1,0},{2,1},{3,2},{4,3},{5,4},{6,5},{7,6},{8,7},{9,8},{10,9},{11,1... | collective-permute-start | bytes 589832 | tf_op jit(solution)/shard_map/ppermute | solution.py:18
  203.0 17.0 %collective-permute-start.12 = (bf16[128,12,64]{0,2,1:T(8,128)(2,1)S(1)}, bf16[128,12,64]{0,2,1:T(8,128)(2,1)S(1)}, u32[]{:S(2)}, u32[]{:S(2)}) collective-permute-start(bf16[128,12,64]{0,2,1:T(8,128)(2,1)S(1)} %bitcast.134), channel_id=1, source_target_pairs={{5,0},{6,1},{7,2},{8,3},{9,4},{10,5},{11,6},{12,7},{13,8},{14,9},{... | collective-permute-start | bytes 589832 | tf_op jit(solution)/shard_map/ppermute | solution.py:18
  233.9 18.1 %all-to-all-start = ((bf16[128,2,768]{2,1,0:T(2,128)(2,1)}), bf16[128,2,768]{2,1,0:T(2,128)(2,1)S(1)}, u32[]{:S(2)}, u32[]{:S(2)}) async-start(bf16[128,2,768]{2,1,0:T(2,128)(2,1)} %reshape.365), calls=%async_computation | async-start | bytes 786432 | tf_op jit(solution)/shard_map/all_to_all | solution.py:203
  251.9 22.5 %all-to-all-start.2 = ((bf16[128,2,768]{2,1,0:T(2,128)(2,1)}), bf16[128,2,768]{2,1,0:T(2,128)(2,1)S(1)}, u32[]{:S(2)}, u32[]{:S(2)}) async-start(bf16[128,2,768]{2,1,0:T(2,128)(2,1)} %reshape.369), calls=%async_computation.2 | async-start | bytes 786432 | tf_op jit(solution)/shard_map/all_to_all | solution.py:238
  274.4 23.5 %all-to-all-start.1 = ((bf16[128,2,768]{2,1,0:T(2,128)(2,1)}), bf16[128,2,768]{2,1,0:T(2,128)(2,1)S(1)}, u32[]{:S(2)}, u32[]{:S(2)}) async-start(bf16[128,2,768]{2,1,0:T(2,128)(2,1)} %reshape.367), calls=%async_computation.1 | async-start | bytes 786432 | tf_op jit(solution)/shard_map/all_to_all | solution.py:218
  297.9 22.0 %all-to-all-start.3 = ((bf16[128,2,768]{2,1,0:T(2,128)(2,1)}), bf16[128,2,768]{2,1,0:T(2,128)(2,1)}, u32[]{:S(2)}, u32[]{:S(2)}) async-start(bf16[128,2,768]{2,1,0:T(2,128)(2,1)} %copy.180), calls=%async_computation.3 | async-start | bytes 786432 | tf_op jit(solution)/shard_map/all_to_all | solution.py:256
  380.6 33.9 %collective-permute-start.47 = (bf16[128,12,64]{0,2,1:T(8,128)(2,1)}, bf16[128,12,64]{0,2,1:T(8,128)(2,1)}, u32[]{:S(2)}, u32[]{:S(2)}) collective-permute-start(bf16[128,12,64]{0,2,1:T(8,128)(2,1)} %get-tuple-element.45), channel_id=1, source_target_pairs={{0,8},{1,9},{2,10},{3,11},{4,12},{5,13},{6,14},{7,15},{8,16},{9,17... | collective-permute-start | bytes 589832 | tf_op jit(solution)/shard_map/ppermute | solution.py:18
  383.3 35.8 %collective-permute-start.46 = (bf16[128,12,64]{0,2,1:T(8,128)(2,1)}, bf16[128,12,64]{0,2,1:T(8,128)(2,1)}, u32[]{:S(2)}, u32[]{:S(2)}) collective-permute-start(bf16[128,12,64]{0,2,1:T(8,128)(2,1)} %get-tuple-element.46), channel_id=1, source_target_pairs={{0,7},{1,8},{2,9},{3,10},{4,11},{5,12},{6,13},{7,14},{8,15},{9,16}... | collective-permute-start | bytes 589832 | tf_op jit(solution)/shard_map/ppermute | solution.py:18
  385.2 46.5 %collective-permute-start.45 = (bf16[128,12,64]{0,2,1:T(8,128)(2,1)}, bf16[128,12,64]{0,2,1:T(8,128)(2,1)}, u32[]{:S(2)}, u32[]{:S(2)}) collective-permute-start(bf16[128,12,64]{0,2,1:T(8,128)(2,1)} %get-tuple-element.47), channel_id=1, source_target_pairs={{0,6},{1,7},{2,8},{3,9},{4,10},{5,11},{6,12},{7,13},{8,14},{9,15},... | collective-permute-start | bytes 589832 | tf_op jit(solution)/shard_map/ppermute | solution.py:18
  387.5 46.6 %collective-permute-start.44 = (bf16[128,12,64]{0,2,1:T(8,128)(2,1)}, bf16[128,12,64]{0,2,1:T(8,128)(2,1)}, u32[]{:S(2)}, u32[]{:S(2)}) collective-permute-start(bf16[128,12,64]{0,2,1:T(8,128)(2,1)} %get-tuple-element.48), channel_id=1, source_target_pairs={{0,5},{1,6},{2,7},{3,8},{4,9},{5,10},{6,11},{7,12},{8,13},{9,14},{... | collective-permute-start | bytes 589832 | tf_op jit(solution)/shard_map/ppermute | solution.py:18
  392.1 49.4 %collective-permute-start.43 = (bf16[128,12,64]{0,2,1:T(8,128)(2,1)}, bf16[128,12,64]{0,2,1:T(8,128)(2,1)}, u32[]{:S(2)}, u32[]{:S(2)}) collective-permute-start(bf16[128,12,64]{0,2,1:T(8,128)(2,1)} %get-tuple-element.49), channel_id=1, source_target_pairs={{0,4},{1,5},{2,6},{3,7},{4,8},{5,9},{6,10},{7,11},{8,12},{9,13},{1... | collective-permute-start | bytes 589832 | tf_op jit(solution)/shard_map/ppermute | solution.py:18
  414.6 30.5 %collective-permute-start.42 = (bf16[128,12,64]{0,2,1:T(8,128)(2,1)}, bf16[128,12,64]{0,2,1:T(8,128)(2,1)}, u32[]{:S(2)}, u32[]{:S(2)}) collective-permute-start(bf16[128,12,64]{0,2,1:T(8,128)(2,1)} %get-tuple-element.50), channel_id=1, source_target_pairs={{0,3},{1,4},{2,5},{3,6},{4,7},{5,8},{6,9},{7,10},{8,11},{9,12},{10... | collective-permute-start | bytes 589832 | tf_op jit(solution)/shard_map/ppermute | solution.py:18
  419.1 27.9 %collective-permute-start.41 = (bf16[128,12,64]{0,2,1:T(8,128)(2,1)}, bf16[128,12,64]{0,2,1:T(8,128)(2,1)}, u32[]{:S(2)}, u32[]{:S(2)}) collective-permute-start(bf16[128,12,64]{0,2,1:T(8,128)(2,1)} %get-tuple-element.51), channel_id=1, source_target_pairs={{0,2},{1,3},{2,4},{3,5},{4,6},{5,7},{6,8},{7,9},{8,10},{9,11},{10,... | collective-permute-start | bytes 589832 | tf_op jit(solution)/shard_map/ppermute | solution.py:18
  427.5 40.6 %all-to-all-start.6 = ((bf16[2,384,129]{1,2,0:T(8,128)(2,1)}), bf16[2,384,129]{1,2,0:T(8,128)(2,1)}, u32[]{:S(2)}, u32[]{:S(2)}) async-start(bf16[2,384,129]{1,2,0:T(8,128)(2,1)} %pad_maximum_fusion), calls=%async_computation.6 | async-start | bytes 417792 | tf_op jit(solution)/shard_map/all_to_all | solution.py:29
  431.6 349.7 %all-reduce.2.cloned.1.call-start = ((), (), s32[]{:S(2)}) async-start(), calls=%async_computation.11 | async-start | bytes 9838592 | tf_op jit(solution)/shard_map/psum | solution.py:47
  431.7 20.6 %collective-permute-start.40 = (bf16[128,12,64]{0,2,1:T(8,128)(2,1)}, bf16[128,12,64]{0,2,1:T(8,128)(2,1)}, u32[]{:S(2)}, u32[]{:S(2)}) collective-permute-start(bf16[128,12,64]{0,2,1:T(8,128)(2,1)} %get-tuple-element.52), channel_id=1, source_target_pairs={{0,1},{1,2},{2,3},{3,4},{4,5},{5,6},{6,7},{7,8},{8,9},{9,10},{10,1... | collective-permute-start | bytes 589832 | tf_op jit(solution)/shard_map/ppermute | solution.py:18
  434.1 20.2 %collective-permute-start.39 = (bf16[128,12,64]{0,2,1:T(8,128)(2,1)}, bf16[128,12,64]{0,2,1:T(8,128)(2,1)}, u32[]{:S(2)}, u32[]{:S(2)}) collective-permute-start(bf16[128,12,64]{0,2,1:T(8,128)(2,1)} %get-tuple-element.53), channel_id=1, source_target_pairs={{1,0},{2,1},{3,2},{4,3},{5,4},{6,5},{7,6},{8,7},{9,8},{10,9},{11,1... | collective-permute-start | bytes 589832 | tf_op jit(solution)/shard_map/ppermute | solution.py:18
  441.5 16.4 %collective-permute-start.38 = (bf16[128,12,64]{0,2,1:T(8,128)(2,1)}, bf16[128,12,64]{0,2,1:T(8,128)(2,1)}, u32[]{:S(2)}, u32[]{:S(2)}) collective-permute-start(bf16[128,12,64]{0,2,1:T(8,128)(2,1)} %get-tuple-element.54), channel_id=1, source_target_pairs={{2,0},{3,1},{4,2},{5,3},{6,4},{7,5},{8,6},{9,7},{10,8},{11,9},{12,... | collective-permute-start | bytes 589832 | tf_op jit(solution)/shard_map/ppermute | solution.py:18
  445.1 16.5 %collective-permute-start.37 = (bf16[128,12,64]{0,2,1:T(8,128)(2,1)}, bf16[128,12,64]{0,2,1:T(8,128)(2,1)S(1)}, u32[]{:S(2)}, u32[]{:S(2)}) collective-permute-start(bf16[128,12,64]{0,2,1:T(8,128)(2,1)} %get-tuple-element.55), channel_id=1, source_target_pairs={{3,0},{4,1},{5,2},{6,3},{7,4},{8,5},{9,6},{10,7},{11,8},{12,9},{13... | collective-permute-start | bytes 589832 | tf_op jit(solution)/shard_map/ppermute | solution.py:18
  447.0 16.8 %collective-permute-start.36 = (bf16[128,12,64]{0,2,1:T(8,128)(2,1)}, bf16[128,12,64]{0,2,1:T(8,128)(2,1)S(1)}, u32[]{:S(2)}, u32[]{:S(2)}) collective-permute-start(bf16[128,12,64]{0,2,1:T(8,128)(2,1)} %get-tuple-element.56), channel_id=1, source_target_pairs={{4,0},{5,1},{6,2},{7,3},{8,4},{9,5},{10,6},{11,7},{12,8},{13,9},{1... | collective-permute-start | bytes 589832 | tf_op jit(solution)/shard_map/ppermute | solution.py:18
  452.3 17.7 %collective-permute-start.35 = (bf16[128,12,64]{0,2,1:T(8,128)(2,1)}, bf16[128,12,64]{0,2,1:T(8,128)(2,1)S(1)}, u32[]{:S(2)}, u32[]{:S(2)}) collective-permute-start(bf16[128,12,64]{0,2,1:T(8,128)(2,1)} %get-tuple-element.57), channel_id=1, source_target_pairs={{5,0},{6,1},{7,2},{8,3},{9,4},{10,5},{11,6},{12,7},{13,8},{14,9},{... | collective-permute-start | bytes 589832 | tf_op jit(solution)/shard_map/ppermute | solution.py:18
  454.2 18.4 %collective-permute-start.34 = (bf16[128,12,64]{0,2,1:T(8,128)(2,1)}, bf16[128,12,64]{0,2,1:T(8,128)(2,1)S(1)}, u32[]{:S(2)}, u32[]{:S(2)}) collective-permute-start(bf16[128,12,64]{0,2,1:T(8,128)(2,1)} %get-tuple-element.58), channel_id=1, source_target_pairs={{6,0},{7,1},{8,2},{9,3},{10,4},{11,5},{12,6},{13,7},{14,8},{15,9},... | collective-permute-start | bytes 589832 | tf_op jit(solution)/shard_map/ppermute | solution.py:18
  457.9 18.2 %collective-permute-start.33 = (bf16[128,12,64]{0,2,1:T(8,128)(2,1)}, bf16[128,12,64]{0,2,1:T(8,128)(2,1)S(1)}, u32[]{:S(2)}, u32[]{:S(2)}) collective-permute-start(bf16[128,12,64]{0,2,1:T(8,128)(2,1)} %get-tuple-element.59), channel_id=1, source_target_pairs={{7,0},{8,1},{9,2},{10,3},{11,4},{12,5},{13,6},{14,7},{15,8},{16,9}... | collective-permute-start | bytes 589832 | tf_op jit(solution)/shard_map/ppermute | solution.py:18
  461.6 19.4 %collective-permute-start.32 = (bf16[128,12,64]{0,2,1:T(8,128)(2,1)}, bf16[128,12,64]{0,2,1:T(8,128)(2,1)S(1)}, u32[]{:S(2)}, u32[]{:S(2)}) collective-permute-start(bf16[128,12,64]{0,2,1:T(8,128)(2,1)} %get-tuple-element.44), channel_id=1, source_target_pairs={{8,0},{9,1},{10,2},{11,3},{12,4},{13,5},{14,6},{15,7},{16,8},{17,9... | collective-permute-start | bytes 589832 | tf_op jit(solution)/shard_map/ppermute | solution.py:18
  464.5 21.8 %collective-permute-start.63 = (bf16[128,12,64]{0,2,1:T(8,128)(2,1)}, bf16[128,12,64]{0,2,1:T(8,128)(2,1)S(1)}, u32[]{:S(2)}, u32[]{:S(2)}) collective-permute-start(bf16[128,12,64]{0,2,1:T(8,128)(2,1)} %get-tuple-element.29), channel_id=1, source_target_pairs={{0,8},{1,9},{2,10},{3,11},{4,12},{5,13},{6,14},{7,15},{8,16},{9,17... | collective-permute-start | bytes 589832 | tf_op jit(solution)/shard_map/ppermute | solution.py:18
  470.1 22.4 %collective-permute-start.62 = (bf16[128,12,64]{0,2,1:T(8,128)(2,1)}, bf16[128,12,64]{0,2,1:T(8,128)(2,1)S(1)}, u32[]{:S(2)}, u32[]{:S(2)}) collective-permute-start(bf16[128,12,64]{0,2,1:T(8,128)(2,1)} %get-tuple-element.30), channel_id=1, source_target_pairs={{0,7},{1,8},{2,9},{3,10},{4,11},{5,12},{6,13},{7,14},{8,15},{9,16}... | collective-permute-start | bytes 589832 | tf_op jit(solution)/shard_map/ppermute | solution.py:18
  472.6 23.4 %collective-permute-start.61 = (bf16[128,12,64]{0,2,1:T(8,128)(2,1)}, bf16[128,12,64]{0,2,1:T(8,128)(2,1)S(1)}, u32[]{:S(2)}, u32[]{:S(2)}) collective-permute-start(bf16[128,12,64]{0,2,1:T(8,128)(2,1)} %get-tuple-element.31), channel_id=1, source_target_pairs={{0,6},{1,7},{2,8},{3,9},{4,10},{5,11},{6,12},{7,13},{8,14},{9,15},... | collective-permute-start | bytes 589832 | tf_op jit(solution)/shard_map/ppermute | solution.py:18
  476.8 21.2 %collective-permute-start.60 = (bf16[128,12,64]{0,2,1:T(8,128)(2,1)}, bf16[128,12,64]{0,2,1:T(8,128)(2,1)S(1)}, u32[]{:S(2)}, u32[]{:S(2)}) collective-permute-start(bf16[128,12,64]{0,2,1:T(8,128)(2,1)} %get-tuple-element.32), channel_id=1, source_target_pairs={{0,5},{1,6},{2,7},{3,8},{4,9},{5,10},{6,11},{7,12},{8,13},{9,14},{... | collective-permute-start | bytes 589832 | tf_op jit(solution)/shard_map/ppermute | solution.py:18
  481.7 24.1 %collective-permute-start.59 = (bf16[128,12,64]{0,2,1:T(8,128)(2,1)}, bf16[128,12,64]{0,2,1:T(8,128)(2,1)S(1)}, u32[]{:S(2)}, u32[]{:S(2)}) collective-permute-start(bf16[128,12,64]{0,2,1:T(8,128)(2,1)} %get-tuple-element.33), channel_id=1, source_target_pairs={{0,4},{1,5},{2,6},{3,7},{4,8},{5,9},{6,10},{7,11},{8,12},{9,13},{1... | collective-permute-start | bytes 589832 | tf_op jit(solution)/shard_map/ppermute | solution.py:18
  486.3 21.9 %collective-permute-start.58 = (bf16[128,12,64]{0,2,1:T(8,128)(2,1)}, bf16[128,12,64]{0,2,1:T(8,128)(2,1)S(1)}, u32[]{:S(2)}, u32[]{:S(2)}) collective-permute-start(bf16[128,12,64]{0,2,1:T(8,128)(2,1)} %get-tuple-element.34), channel_id=1, source_target_pairs={{0,3},{1,4},{2,5},{3,6},{4,7},{5,8},{6,9},{7,10},{8,11},{9,12},{10... | collective-permute-start | bytes 589832 | tf_op jit(solution)/shard_map/ppermute | solution.py:18
  492.5 20.2 %collective-permute-start.57 = (bf16[128,12,64]{0,2,1:T(8,128)(2,1)}, bf16[128,12,64]{0,2,1:T(8,128)(2,1)S(1)}, u32[]{:S(2)}, u32[]{:S(2)}) collective-permute-start(bf16[128,12,64]{0,2,1:T(8,128)(2,1)} %get-tuple-element.35), channel_id=1, source_target_pairs={{0,2},{1,3},{2,4},{3,5},{4,6},{5,7},{6,8},{7,9},{8,10},{9,11},{10,... | collective-permute-start | bytes 589832 | tf_op jit(solution)/shard_map/ppermute | solution.py:18
  496.0 19.4 %collective-permute-start.56 = (bf16[128,12,64]{0,2,1:T(8,128)(2,1)}, bf16[128,12,64]{0,2,1:T(8,128)(2,1)S(1)}, u32[]{:S(2)}, u32[]{:S(2)}) collective-permute-start(bf16[128,12,64]{0,2,1:T(8,128)(2,1)} %get-tuple-element.36), channel_id=1, source_target_pairs={{0,1},{1,2},{2,3},{3,4},{4,5},{5,6},{6,7},{7,8},{8,9},{9,10},{10,1... | collective-permute-start | bytes 589832 | tf_op jit(solution)/shard_map/ppermute | solution.py:18
  498.0 19.4 %collective-permute-start.55 = (bf16[128,12,64]{0,2,1:T(8,128)(2,1)}, bf16[128,12,64]{0,2,1:T(8,128)(2,1)S(1)}, u32[]{:S(2)}, u32[]{:S(2)}) collective-permute-start(bf16[128,12,64]{0,2,1:T(8,128)(2,1)} %get-tuple-element.37), channel_id=1, source_target_pairs={{1,0},{2,1},{3,2},{4,3},{5,4},{6,5},{7,6},{8,7},{9,8},{10,9},{11,1... | collective-permute-start | bytes 589832 | tf_op jit(solution)/shard_map/ppermute | solution.py:18
  515.4 17.3 %collective-permute-start.51 = (bf16[128,12,64]{0,2,1:T(8,128)(2,1)S(1)}, bf16[128,12,64]{0,2,1:T(8,128)(2,1)S(1)}, u32[]{:S(2)}, u32[]{:S(2)}) collective-permute-start(bf16[128,12,64]{0,2,1:T(8,128)(2,1)S(1)} %copy-done.39), channel_id=1, source_target_pairs={{5,0},{6,1},{7,2},{8,3},{9,4},{10,5},{11,6},{12,7},{13,8},{14,9},{... | collective-permute-start | bytes 589832 | tf_op jit(solution)/shard_map/ppermute | solution.py:18
  517.4 16.5 %collective-permute-start.50 = (bf16[128,12,64]{0,2,1:T(8,128)(2,1)S(1)}, bf16[128,12,64]{0,2,1:T(8,128)(2,1)S(1)}, u32[]{:S(2)}, u32[]{:S(2)}) collective-permute-start(bf16[128,12,64]{0,2,1:T(8,128)(2,1)S(1)} %copy-done.38), channel_id=1, source_target_pairs={{6,0},{7,1},{8,2},{9,3},{10,4},{11,5},{12,6},{13,7},{14,8},{15,9},... | collective-permute-start | bytes 589832 | tf_op jit(solution)/shard_map/ppermute | solution.py:18
  524.2 19.2 %collective-permute-start.48 = (bf16[128,12,64]{0,2,1:T(8,128)(2,1)S(1)}, bf16[128,12,64]{0,2,1:T(8,128)(2,1)S(1)}, u32[]{:S(2)}, u32[]{:S(2)}) collective-permute-start(bf16[128,12,64]{0,2,1:T(8,128)(2,1)S(1)} %copy-done.36), channel_id=1, source_target_pairs={{8,0},{9,1},{10,2},{11,3},{12,4},{13,5},{14,6},{15,7},{16,8},{17,9... | collective-permute-start | bytes 589832 | tf_op jit(solution)/shard_map/ppermute | solution.py:18
  (94 other events, 1549.0 us)
Sparse Core Ops, SparseCore 0:
  9.7 14.2 all-gather.6
  25.7 13.2 all-gather.10
  40.6 13.2 all-gather.8
  55.4 13.2 all-gather.12
  644.3 136.9 all-reduce.1
where the time goes:
time: 817 us; the launch traced here: 803 us
  starting transfers between devices  241 us (29%)
  waiting for transfers between devices  223 us (27%)
  local copies, waits for them, and re-layouts  169 us (21%)
  matrix products  113 us (14%)
  other arithmetic  23.6 us (3%)
  blocking collectives  16.5 us (2%)
  between operations  16.3 us (2%)
    ppermute x64, starting transfers between devices, passed_along(): lax.ppermute(value, axis, [(source, source + steps) for source in range(i...  202 us
    psum x1, waiting for transfers between devices, together(): total = lax.psum(jnp.concatenate([a.ravel() for a in arrays]), axis)  126 us
    ppermute x64, waiting for transfers between devices, passed_along(): lax.ppermute(value, axis, [(source, source + steps) for source in range(i...  74.9 us
    concatenate x1, local copies, waits for them, and re-layouts, together(): total = lax.psum(jnp.concatenate([a.ravel() for a in arrays]), axis)  38.6 us
    concatenate x6, local copies, waits for them, and re-layouts, side_by_side(): jnp.concatenate([a.reshape(*a.shape[:along], w) for a, w in zip(arrays, w...  34.3 us
    dot_general x1, local copies, waits for them, and re-layouts, masked_scores(): jnp.einsum('qkb,bh->hqk', bucket_onehot, table_full, preferred_element_ty...  17.2 us
  transfers between devices with their start and end apart: 75, of which 23 were waited for; matrix products, arithmetic and copies ran while one was open for 16% of the time, Pallas kernels for 0%

commit v1 on v0

v1 whole, which is shorter than its diff:
```python
import jax
import jax.numpy as jnp
from jax import lax
from jax.experimental import pallas as pl
from jax.experimental.pallas import tpu as pltpu
from jax.sharding import PartitionSpec as P

MESH = pl.DeviceIdType.MESH
BF = jnp.bfloat16
F32 = jnp.float32
EPSILON = 1e-06
FAR_EDGES = (12, 16, 23, 32, 46, 64, 91)

D = 768
HALF = 384
HEAD = 64
TOK = 128
CHIP = 256
REACH = 4
SLOTS = 2 * REACH + 1
WIN = SLOTS * CHIP
MID = REACH * CHIP
TOTAL = 16384
EXPERTS = 128
NB = 32
FF = 3072
NEAR = 3 * CHIP
LOOP = 1024
VMEM_BYTES = 56 * 1024 * 1024

NT = (((1,), (1,)), ((), ()))
TN = (((0,), (0,)), ((), ()))
NN = (((1,), (0,)), ((), ()))


def mm(left, right, dims=NN):
    return lax.dot_general(left, right, dims, preferred_element_type=F32)


def bucket_of(relative):
    distance = jnp.abs(relative)
    far_bucket = 8 + sum(((distance >= edge).astype(jnp.int32) for edge in FAR_EDGES))
    near_far = jnp.where(distance < 8, distance, far_bucket)
    return near_far + 16 * (relative > 0).astype(jnp.int32)


def tile(ref, rows, start, width):
    return ref[rows, pl.ds(pl.multiple_of(start, 128), width)]


def window_kernel(tok, wq, wk, wv, wo, router, misc, qkv, normed, wqkv, wo_full, router_full, misc_full, win, send, recv, fsend, frecv, wsend, wrecv, local):
    e = lax.axis_index("expert")
    j = lax.axis_index("wshard")
    jp = 1 - j
    chips = lax.axis_size("expert")
    offsets = [m for k in range(1, REACH + 1) for m in (k, -k)]
    barrier = pltpu.get_barrier_semaphore()
    for m in offsets:
        pl.semaphore_signal(barrier, inc=1, device_id=(lax.rem(e + m + chips, chips), j), device_id_type=MESH)
    pl.semaphore_signal(barrier, inc=1, device_id=(e, jp), device_id_type=MESH)
    pl.semaphore_wait(barrier, len(offsets) + 1)

    def rows_of(slot, core):
        return win.at[pl.ds(pl.multiple_of(slot * CHIP + core * TOK, TOK), TOK), :]

    def remote(src, dst, ssem, rsem, chip, core):
        return pltpu.make_async_remote_copy(src_ref=src, dst_ref=dst, send_sem=ssem, recv_sem=rsem, device_id=(chip, core), device_id_type=MESH)

    copies = []
    for n, m in enumerate(offsets):
        copies.append(remote(tok, rows_of(REACH - m, j), send.at[n], recv.at[n], lax.rem(e + m + chips, chips), j))
    for c in copies:
        c.start()
    mine = pltpu.make_async_copy(tok, rows_of(REACH, j), local.at[0])
    mine.start()
    weights = []
    kept = []
    for n, w in enumerate((wq, wk, wv)):
        rows = pl.ds(pl.multiple_of(j * HALF, HALF), HALF)
        there = w.at[:, pl.ds(pl.multiple_of(jp * HALF, 128), HALF)]
        here = w.at[:, pl.ds(pl.multiple_of(j * HALF, 128), HALF)]
        dst = wqkv.at[rows, n * HALF : (n + 1) * HALF]
        weights.append(remote(there, dst, wsend.at[n], wrecv.at[n], e, jp))
        kept.append(pltpu.make_async_copy(here, dst, local.at[1 + n]))
    for n, (src, dst, size) in enumerate(((misc, misc_full, 24), (router, router_full, HALF), (wo, wo_full, HALF))):
        rows = pl.ds(pl.multiple_of(j * size, 8), size)
        weights.append(remote(src, dst.at[rows, :], wsend.at[3 + n], wrecv.at[3 + n], e, jp))
        kept.append(pltpu.make_async_copy(src, dst.at[rows, :], local.at[4 + n]))
    swap = remote(tok, rows_of(REACH, j), fsend.at[8], frecv.at[8], e, jp)
    weights[3].start()
    for c in weights[:3]:
        c.start()
    swap.start()
    for c in weights[4:]:
        c.start()
    for c in kept:
        c.start()
    mine.wait()
    for c in kept[:4]:
        c.wait()
    for c in weights[:4]:
        c.wait_recv()
    gain = jnp.concatenate([misc_full[16:17, :], misc_full[40:41, :]], axis=1)

    def project(slot):
        rows = slice(slot * CHIP, (slot + 1) * CHIP)
        x = win[rows, :].astype(F32)
        y = (x * lax.rsqrt(jnp.mean(x * x, axis=-1, keepdims=True) + EPSILON) * gain).astype(BF)
        if slot == REACH:
            normed[...] = y
        qkv[rows, :] = mm(y, wqkv[...]).astype(BF)

    def passed(n):
        return remote(rows_of(REACH - offsets[n], j), rows_of(REACH - offsets[n], j), fsend.at[n], frecv.at[n], e, jp)

    swap.wait_recv()
    project(REACH)
    for n in range(len(offsets) + 1):
        if n < len(offsets):
            copies[n].wait_recv()
            passed(n).start()
        if n > 0:
            passed(n - 1).wait_recv()
            project(REACH - offsets[n - 1])
    for c in kept[4:]:
        c.wait()
    for c in weights[4:]:
        c.wait_recv()
    for c in weights:
        c.wait_send()
    for c in copies:
        c.wait_send()
    swap.wait_send()
    for n in range(len(offsets)):
        passed(n).wait_send()


def window(tokens, wq, wk, wv, wo, router, misc):
    any_spec = pl.BlockSpec(memory_space=pl.ANY)
    vm = pl.BlockSpec(memory_space=pltpu.VMEM)
    return pl.pallas_call(
        window_kernel,
        name="window",
        out_shape=(
            jax.ShapeDtypeStruct((WIN, 3 * HALF), BF),
            jax.ShapeDtypeStruct((CHIP, D), BF),
            jax.ShapeDtypeStruct((D, 3 * HALF), BF),
            jax.ShapeDtypeStruct((D, D), BF),
            jax.ShapeDtypeStruct((D, EXPERTS), BF),
            jax.ShapeDtypeStruct((48, HALF), F32),
        ),
        in_specs=[any_spec] * 7,
        out_specs=(vm, vm, vm, any_spec, any_spec, vm),
        scratch_shapes=[
            pltpu.VMEM((WIN, D), BF),
            pltpu.SemaphoreType.DMA((8,)),
            pltpu.SemaphoreType.DMA((8,)),
            pltpu.SemaphoreType.DMA((9,)),
            pltpu.SemaphoreType.DMA((9,)),
            pltpu.SemaphoreType.DMA((6,)),
            pltpu.SemaphoreType.DMA((6,)),
            pltpu.SemaphoreType.DMA((7,)),
        ],
        compiler_params=pltpu.CompilerParams(collective_id=1, has_side_effects=True, vmem_limit_bytes=VMEM_BYTES),
    )(tokens, wq, wk, wv, wo, router, misc)


def prepare(lengths, misc, mask, diag, ways):
    e = lax.axis_index("expert")
    row_pos = (e - REACH) * CHIP + lax.broadcasted_iota(jnp.int32, (8, WIN), 1)
    col_pos = e * CHIP + lax.broadcasted_iota(jnp.int32, (CHIP, 128), 0)

    def count(n, state):
        end, rows, cols = state
        end = end + lengths[n]
        return end, rows + (row_pos >= end).astype(jnp.int32), cols + (col_pos >= end).astype(jnp.int32)

    zero = jnp.zeros((8, WIN), jnp.int32)
    _, rows, cols = lax.fori_loop(0, 32, count, (jnp.int32(0), zero, jnp.zeros((CHIP, 128), jnp.int32)))
    rows = jnp.where((row_pos >= 0) & (row_pos < TOTAL), rows, -1)
    for c in range(SLOTS):
        part = rows[0:1, c * CHIP : (c + 1) * CHIP]
        mask[:, c * CHIP : (c + 1) * CHIP] = jnp.where(cols[:, 0:1] == part, 0.0, -1e9).astype(F32)
    table = jnp.concatenate([misc[0:16, 0:128], misc[24:40, 0:128]], axis=0).astype(BF)
    for n, sign in enumerate(ways):
        hot = diagonal_buckets(sign)
        diag[n * 16 : (n + 1) * 16, :] = mm(table, hot.astype(BF), TN)[0:16]


def diagonal_buckets(sign):
    m = lax.broadcasted_iota(jnp.int32, (NB, LOOP), 1)
    r = jnp.where(m < NEAR, m, m - LOOP) - CHIP
    b = lax.broadcasted_iota(jnp.int32, (NB, LOOP), 0)
    return (bucket_of(sign * r) == b).astype(F32)


def biased(raw, c, mask, near, left, right):
    s = raw + mask[:, c * CHIP : (c + 1) * CHIP]
    if c < REACH - 1:
        return s + left
    if c > REACH + 1:
        return s + right
    lower = (c - REACH + 1) * CHIP
    return s + near[:, lower : lower + CHIP]


def near_tile(diag, row):
    line = diag[pl.ds(row, 1), :]
    spread = pltpu.roll(jnp.broadcast_to(line, (CHIP, LOOP)), 0, 1, stride=1, stride_axis=0)
    return spread[:, 0:NEAR], line[:, 0:1], line[:, NEAR - 1 : NEAR]


def chunk(c):
    return slice(c * CHIP, (c + 1) * CHIP)


def forward_kernel(lengths, qkv, misc, att, stat, mask, diag, scores, lse_cols):
    j = lax.axis_index("wshard")
    prepare(lengths, misc, mask, diag, (1,))
    lane = lax.broadcasted_iota(jnp.int32, (CHIP, 128), 1)
    lse_cols[...] = jnp.zeros((CHIP, 128), F32)

    def pair(p, carry):
        q = tile(qkv, slice(MID, MID + CHIP), p * 128, 128).astype(F32) * 0.125
        outs = []
        for hh in range(2):
            own = (lane // HEAD) == hh
            qm = jnp.where(own, q, 0.0).astype(BF)
            near, left, right = near_tile(diag, j * 6 + 2 * p + hh)
            top = None
            for c in range(SLOTS):
                k = tile(qkv, chunk(c), HALF + p * 128, 128)
                s = biased(mm(qm, k, NT), c, mask, near, left, right)
                scores[:, chunk(c)] = s
                top = s if top is None else jnp.maximum(top, s)
            top = jnp.max(top, axis=1, keepdims=True)
            total = jnp.zeros((CHIP, CHIP), F32)
            out = jnp.zeros((CHIP, 128), F32)
            for c in range(SLOTS):
                x = jnp.exp(scores[:, chunk(c)] - top)
                total = total + x
                out = out + mm(x.astype(BF), tile(qkv, chunk(c), 2 * HALF + p * 128, 128))
            total = jnp.sum(total, axis=1, keepdims=True)
            outs.append(out / total)
            lse_cols[...] = jnp.where(lane == 2 * p + hh, top + jnp.log(total), lse_cols[...])
        att[:, pl.ds(pl.multiple_of(p * 128, 128), 128)] = jnp.where(lane < HEAD, outs[0], outs[1]).astype(BF)
        return carry

    lax.fori_loop(0, 3, pair, 0)
    stat[...] = lse_cols[...].T[0:8, :]


def attention(lengths, qkv, misc):
    vm = pl.BlockSpec(memory_space=pltpu.VMEM)
    return pl.pallas_call(
        forward_kernel,
        name="attention",
        out_shape=(jax.ShapeDtypeStruct((CHIP, HALF), BF), jax.ShapeDtypeStruct((8, CHIP), F32)),
        in_specs=[pl.BlockSpec(memory_space=pltpu.SMEM), vm, vm],
        out_specs=(vm, vm),
        scratch_shapes=[
            pltpu.VMEM((CHIP, WIN), F32),
            pltpu.VMEM((16, LOOP), F32),
            pltpu.VMEM((CHIP, WIN), F32),
            pltpu.VMEM((CHIP, 128), F32),
        ],
        compiler_params=pltpu.CompilerParams(vmem_limit_bytes=VMEM_BYTES),
    )(lengths, qkv, misc)


def backward_kernel(lengths, qkv, dout, stat, misc, dqkv, bias, mask, diag, keys):
    j = lax.axis_index("wshard")
    prepare(lengths, misc, mask, diag, (1, -1))
    lane = lax.broadcasted_iota(jnp.int32, (CHIP, 128), 1)
    line = lax.broadcasted_iota(jnp.int32, (NB, 128), 1)
    row32 = lax.broadcasted_iota(jnp.int32, (NB, 128), 0)
    hot = diagonal_buckets(1)
    mid = slice(MID, MID + CHIP)
    cols = jnp.concatenate([stat[REACH], jnp.zeros((112, CHIP), F32)], axis=0).T
    bias[...] = jnp.zeros((NB, 128), F32)

    def pair(p, carry):
        q = tile(qkv, mid, p * 128, 128).astype(F32) * 0.125
        k_own = tile(qkv, mid, HALF + p * 128, 128)
        v_own = tile(qkv, mid, 2 * HALF + p * 128, 128)
        do = tile(dout, mid, p * 128, 128)
        dqs, dks, dvs = [], [], []
        for hh in range(2):
            h = 2 * p + hh
            own = (lane // HEAD) == hh
            spare = (1 - hh) * HEAD
            qm = jnp.where(own, q, 0.0).astype(BF)
            dom = jnp.where(own, do, jnp.zeros_like(do))
            lse = jnp.sum(jnp.where(lane == h, cols, 0.0), axis=1, keepdims=True)
            delta = jnp.sum(jnp.where(lane == h + 8, cols, 0.0), axis=1, keepdims=True)
            near, left, right = near_tile(diag, j * 6 + h)
            dq = jnp.zeros((CHIP, 128), F32)
            tiles = []
            for c in range(SLOTS):
                k = tile(qkv, chunk(c), HALF + p * 128, 128)
                v = tile(qkv, chunk(c), 2 * HALF + p * 128, 128)
                s = biased(mm(qm, k, NT), c, mask, near, left, right)
                ds = jnp.exp(s - lse) * (mm(dom, v, NT) - delta)
                low = ds.astype(BF)
                if c < REACH - 1:
                    other = jnp.where(lane == spare, 1.0, 0.0).astype(BF)
                elif c > REACH + 1:
                    other = jnp.where(lane == spare + 1, 1.0, 0.0).astype(BF)
                else:
                    other = jnp.zeros((CHIP, 128), BF)
                    tiles.append(ds)
                dq = dq + mm(low, jnp.where(own, k, other))
            dqs.append(dq * 0.125)
            fold = jnp.concatenate(tiles + [jnp.zeros((CHIP, CHIP), F32)], axis=1)
            rows = CHIP
            while rows > 8:
                rows //= 2
                fold = fold[0:rows] + pltpu.roll(fold[rows : 2 * rows], LOOP - rows, 1)
            summed = fold[0:1]
            for n in range(1, 8):
                summed = summed + pltpu.roll(fold[n : n + 1], LOOP - n, 1)
            by_bucket = jnp.sum(hot * summed, axis=1, keepdims=True)
            far = jnp.sum(dq, axis=0, keepdims=True)
            far_left = far[:, spare : spare + 1]
            far_right = far[:, spare + 1 : spare + 2]
            by_bucket = by_bucket + jnp.where(row32 == 15, far_left, 0.0) + jnp.where(row32 == 31, far_right, 0.0)
            bias[...] = jnp.where(line == j * 6 + h, by_bucket, bias[...])
            km = jnp.where(own, k_own, jnp.zeros_like(k_own))
            vm = jnp.where(own, v_own, jnp.zeros_like(v_own))
            near, left, right = near_tile(diag, 16 + j * 6 + h)
            dk = jnp.zeros((CHIP, 128), F32)
            dv = jnp.zeros((CHIP, 128), F32)
            for c in range(SLOTS):
                qc = (tile(qkv, chunk(c), p * 128, 128).astype(F32) * 0.125).astype(BF)
                dc = tile(dout, chunk(c), p * 128, 128)
                s = biased(mm(km, qc, NT), c, mask, near, left, right)
                lse_row = stat[c, pl.ds(h, 1), :]
                delta_row = stat[c, pl.ds(h + 8, 1), :]
                prob = jnp.exp(s - lse_row)
                ds = prob * (mm(vm, dc, NT) - delta_row)
                dv = dv + mm(prob.astype(BF), dc)
                dk = dk + mm(ds.astype(BF), qc)
            dks.append(dk)
            dvs.append(dv)
        for n, both in enumerate((dqs, dks, dvs)):
            dqkv[:, pl.ds(pl.multiple_of(n * HALF + p * 128, 128), 128)] = jnp.where(lane < HEAD, both[0], both[1]).astype(BF)
        return carry

    lax.fori_loop(0, 3, pair, 0)


def attention_back(lengths, qkv, dout, stat, misc):
    vm = pl.BlockSpec(memory_space=pltpu.VMEM)
    return pl.pallas_call(
        backward_kernel,
        name="attention_back",
        out_shape=(jax.ShapeDtypeStruct((CHIP, 3 * HALF), BF), jax.ShapeDtypeStruct((NB, 128), F32)),
        in_specs=[pl.BlockSpec(memory_space=pltpu.SMEM), vm, vm, vm, vm],
        out_specs=(vm, vm),
        scratch_shapes=[
            pltpu.VMEM((CHIP, WIN), F32),
            pltpu.VMEM((32, LOOP), F32),
            pltpu.VMEM((8, 128), F32),
        ],
        compiler_params=pltpu.CompilerParams(vmem_limit_bytes=VMEM_BYTES),
    )(lengths, qkv, dout, stat, misc)


def spread_kernel(dout, stat, dout_win, stat_win, send, recv, local):
    e = lax.axis_index("expert")
    j = lax.axis_index("wshard")
    chips = lax.axis_size("expert")
    offsets = [m for k in range(1, REACH + 1) for m in (k, -k)]
    barrier = pltpu.get_barrier_semaphore()
    for m in offsets:
        pl.semaphore_signal(barrier, inc=1, device_id=(lax.rem(e + m + chips, chips), j), device_id_type=MESH)
    pl.semaphore_wait(barrier, len(offsets))
    copies = []
    for n, m in enumerate(offsets):
        slot = REACH - m
        for i, (src, dst) in enumerate(((dout, dout_win.at[slot * CHIP : (slot + 1) * CHIP, :]), (stat, stat_win.at[slot]))):
            copies.append(
                pltpu.make_async_remote_copy(
                    src_ref=src,
                    dst_ref=dst,
                    send_sem=send.at[2 * n + i],
                    recv_sem=recv.at[2 * n + i],
                    device_id=(lax.rem(e + m + chips, chips), j),
                    device_id_type=MESH,
                )
            )
    for c in copies:
        c.start()
    kept = [
        pltpu.make_async_copy(dout, dout_win.at[MID : MID + CHIP, :], local.at[0]),
        pltpu.make_async_copy(stat, stat_win.at[REACH], local.at[1]),
    ]
    for c in kept:
        c.start()
    for c in kept + copies:
        c.wait()


def spread(dout, stat):
    any_spec = pl.BlockSpec(memory_space=pl.ANY)
    return pl.pallas_call(
        spread_kernel,
        name="spread",
        out_shape=(jax.ShapeDtypeStruct((WIN, HALF), BF), jax.ShapeDtypeStruct((SLOTS, 16, CHIP), F32)),
        in_specs=[any_spec] * 2,
        out_specs=(any_spec, any_spec),
        scratch_shapes=[
            pltpu.SemaphoreType.DMA((16,)),
            pltpu.SemaphoreType.DMA((16,)),
            pltpu.SemaphoreType.DMA((2,)),
        ],
        compiler_params=pltpu.CompilerParams(collective_id=2, has_side_effects=True),
    )(dout, stat)


FF_TILE = 512


def expert_kernel(x, g, w_in, w_out, made, back, d_in, d_out, made_sum, back_sum):
    step = pl.program_id(0)

    @pl.when(step == 0)
    def _():
        made_sum[...] = jnp.zeros_like(made_sum)
        back_sum[...] = jnp.zeros_like(back_sum)

    pre = mm(x[...], w_in[0])
    half_erf = 0.5 * lax.erf(pre * (0.5**0.5)) + 0.5
    act = (pre * half_erf).astype(BF)
    slope = half_erf + pre * jnp.exp(-0.5 * pre * pre) * (0.5 * 0.7978845608028654)
    act_grad = mm(g[...], w_out[0], NT)
    pre_grad = (act_grad * slope).astype(BF)
    made_sum[...] += mm(act, w_out[0])
    back_sum[...] += mm(pre_grad, w_in[0], NT)
    d_out[0] = mm(act, g[...], TN).astype(BF)
    d_in[0] = mm(x[...], pre_grad, TN).astype(BF)

    @pl.when(step == pl.num_programs(0) - 1)
    def _():
        made[...] = made_sum[...].astype(BF)
        back[...] = back_sum[...].astype(BF)


def expert(x, g, w_in, w_out):
    rows = x.shape[0]
    whole = pl.BlockSpec((rows, D), lambda f: (0, 0))
    by_in = pl.BlockSpec((1, D, FF_TILE), lambda f: (0, 0, f))
    by_out = pl.BlockSpec((1, FF_TILE, D), lambda f: (0, f, 0))
    return pl.pallas_call(
        expert_kernel,
        name="expert",
        grid=(FF // FF_TILE,),
        out_shape=(
            jax.ShapeDtypeStruct((rows, D), BF),
            jax.ShapeDtypeStruct((rows, D), BF),
            jax.ShapeDtypeStruct((1, D, FF), BF),
            jax.ShapeDtypeStruct((1, FF, D), BF),
        ),
        in_specs=[whole, whole, by_in, by_out],
        out_specs=(whole, whole, by_in, by_out),
        scratch_shapes=[pltpu.VMEM((rows, D), F32), pltpu.VMEM((rows, D), F32)],
        compiler_params=pltpu.CompilerParams(vmem_limit_bytes=VMEM_BYTES, dimension_semantics=("arbitrary",)),
    )(x, g, w_in, w_out)


ORDERS = ("zxy", "xyz", "yzx")
UNITS = (4, 3, 4)


def halves(i):
    while i[0] < i[1]:
        unit, place = divmod(i[0], 64)
        n = min(64 - place, i[1] - i[0])
        yield unit, place, n
        i = (i[0] + n, i[1])


def qkv_places(c):
    if c == 8:
        return [(2, None, 0, 24, 0)]
    done, found = 0, []
    for unit, place, n in halves((24 * c, 24 * c + 24)):
        found.append((0, unit, place, n, done) if unit < 2 else (1, None, place, n, done))
        done += n
    return found


def out_places(c):
    done, found = 0, []
    for unit, place, n in halves((24 * c, 24 * c + 24)):
        found.append(((1, 2), (2, 0), (2, 3))[unit] + (place, n, done))
        done += n
    return found


def tail_kernel(dqkv, normed, wqkv, tok, hidden_grad, att, branch, mixed, logit_grad, mix_grad, bias, misc, tokens_grad, q_sum, k_sum, v_sum, out_sum, router_sum, bias_sum, gain_sum, part_a, part_b, part_c, in1a, in1b, in1c, in2a, in2b, in2c, in3a, in3b, in3c, red1a, red1b, red1c, red2a, red2b, red2c, red3a, red3b, red3c, all_a, all_b, all_c, half_out, half_in, rs_send, rs_recv, ag_send, ag_recv, core_send, core_recv):
    e = lax.axis_index("expert")
    j = lax.axis_index("wshard")
    jp = 1 - j
    parts, into = (part_a, part_b, part_c), ((in1a, in1b, in1c), (in2a, in2b, in2c), (in3a, in3b, in3c))
    reds, alls = ((red1a, red1b, red1c), (red2a, red2b, red2c), (red3a, red3b, red3c)), (all_a, all_b, all_c)
    stride = {"y": 16, "x": 4, "z": 1}
    coord = {a: lax.rem(e // s, 4) for a, s in stride.items()}

    def peer(axis, d):
        c = coord[axis]
        return e + (lax.rem(c + d, 4) - c) * stride[axis]

    barrier = pltpu.get_barrier_semaphore()
    for axis in "zxy":
        for d in (1, 2, 3):
            pl.semaphore_signal(barrier, inc=1, device_id=(peer(axis, d), j), device_id_type=MESH)
    pl.semaphore_signal(barrier, inc=1, device_id=(e, jp), device_id_type=MESH)
    pl.semaphore_wait(barrier, 10)

    def remote(src, dst, ssem, rsem, chip, core):
        return pltpu.make_async_remote_copy(src_ref=src, dst_ref=dst, send_sem=ssem, recv_sem=rsem, device_id=(chip, core), device_id_type=MESH)

    there = pl.ds(pl.multiple_of(jp * TOK, TOK), TOK)
    here = pl.ds(pl.multiple_of(j * TOK, TOK), TOK)
    half_out[...] = mm(dqkv[there, :], wqkv[...], NT).astype(BF)
    trade = remote(half_out, half_in, core_send.at[0], core_recv.at[0], e, jp)
    trade.start()

    def reduce_copies(n, phase):
        src = parts[n] if phase == 0 else reds[phase - 1][n]
        axis, size = ORDERS[n][phase], (16, 4, 1)[phase]
        copies = []
        for d in (1, 2, 3):
            place = lax.rem(coord[axis] + d, 4) * size
            copies.append(remote(src.at[:, pl.ds(place, size)], into[phase][n].at[d - 1], rs_send.at[n, phase, d - 1], rs_recv.at[n, phase, d - 1], peer(axis, d), j))
        return copies

    def gather_copies(n, phase):
        size = (1, 4, 16)[phase]
        one, two, three = (coord[a] for a in ORDERS[n])
        place = (one * 16 + two * 4 + three, one * 16 + two * 4, one * 16)[phase]
        ref = alls[n].at[:, pl.ds(place, size)]
        axis = ORDERS[n][2 - phase]
        return [remote(ref, ref, ag_send.at[n, phase, d - 1], ag_recv.at[n, phase, d - 1], peer(axis, d), j) for d in (1, 2, 3)]

    def fill(ref, unit, place, value):
        ref[unit, place : place + value.shape[0]] = value

    def tiles(value):
        return value.astype(BF).reshape(value.shape[0] // 16, 16, 128)

    for third in range(3):
        grad = mm(normed[...], dqkv[:, third * HALF : (third + 1) * HALF], TN)
        for c in range(3 * third, 3 * third + 3):
            cut = tiles(grad[:, (c % 3) * 128 : (c % 3 + 1) * 128])
            for h in range(2):
                for n, unit, place, count, first in qkv_places(c):
                    unit = (2 * h + unit if n == 0 else h if n == 1 else 1 + h)
                    fill(parts[n], unit, place, cut[24 * h + first : 24 * h + first + count])
        if third == 1:
            started = {(0, 0): reduce_copies(0, 0)}
            for c in started[0, 0]:
                c.start()
    grad = mm(att[...], branch[...], TN)
    for c in range(6):
        cut = tiles(grad[:, c * 128 : (c + 1) * 128])
        for n, unit, place, count, first in out_places(c):
            fill(parts[n], unit, place, cut[first : first + count])
    started[1, 0] = reduce_copies(1, 0)
    for c in started[1, 0]:
        c.start()
    grad = tiles(mm(mixed[...], logit_grad[...], TN))
    for h in range(2):
        fill(part_c, 1 + h, 24, grad[24 * h : 24 * h + 24])
        part_c[1 + h, 50:64] = jnp.zeros((14, 16, 128), BF)
    fill(part_c, 1, 48, tiles(bias[0:16, :]))
    fill(part_c, 2, 48, tiles(bias[16:32, :]))
    part_c[3, 16:64] = jnp.zeros((48, 16, 128), BF)

    own_half = mm(dqkv[here, :], wqkv[...], NT)
    trade.wait_recv()
    grad = own_half + half_in[...].astype(F32)
    x = tok[...].astype(F32)
    gain = jnp.concatenate([misc[16:17, :], misc[40:41, :]], axis=1)
    r = lax.rsqrt(jnp.mean(x * x, axis=-1, keepdims=True) + EPSILON)
    w = grad * gain
    tokens_grad[...] = (hidden_grad[...] + r * w - x * (r * r * r * jnp.mean(w * x, axis=-1, keepdims=True))).astype(BF)
    attn_gain = jnp.sum(grad * x * r, axis=0, keepdims=True)
    for h in range(2):
        lines = [v[:, h * HALF + 128 * n : h * HALF + 128 * n + 128] for v in (attn_gain, mix_grad[0:1, :]) for n in range(3)]
        fill(part_c, 1 + h, 49, tiles(jnp.concatenate(lines + [jnp.zeros((10, 128), F32)], axis=0)))
    started[2, 0] = reduce_copies(2, 0)
    for c in started[2, 0]:
        c.start()

    for phase in range(3):
        for n in range(3):
            for c in started[n, phase]:
                c.wait_recv()
            size = (16, 4, 1)[phase]
            src = parts[n] if phase == 0 else reds[phase - 1][n]
            place = coord[ORDERS[n][phase]] * size
            for u in range(UNITS[n]):
                total = src[u, pl.ds(place, size)].astype(F32)
                for d in range(3):
                    total = total + into[phase][n][d, u].astype(F32)
                reds[phase][n][u] = total.astype(BF)
            if phase < 2:
                started[n, phase + 1] = reduce_copies(n, phase + 1)
                for c in started[n, phase + 1]:
                    c.start()

    spots = [lax.rem(e // stride[o[0]], 4) * 16 + lax.rem(e // stride[o[1]], 4) * 4 + lax.rem(e // stride[o[2]], 4) for o in ORDERS]
    swaps = [
        remote(red3a.at[pl.ds(2 * jp, 2)], all_a.at[2:4, pl.ds(spots[0], 1)], core_send.at[1], core_recv.at[1], e, jp),
        remote(red3b.at[pl.ds(jp, 1)], all_b.at[1:2, pl.ds(spots[1], 1)], core_send.at[2], core_recv.at[2], e, jp),
        remote(red3c.at[pl.ds(1 + jp, 1)], all_c.at[2:3, pl.ds(spots[2], 1)], core_send.at[3], core_recv.at[3], e, jp),
    ]
    for c in swaps:
        c.start()
    all_a[0:2, pl.ds(spots[0], 1)] = red3a[pl.ds(2 * j, 2)]
    all_b[0:1, pl.ds(spots[1], 1)] = red3b[pl.ds(j, 1)]
    all_b[2:3, pl.ds(spots[1], 1)] = red3b[2:3]
    all_c[0:1, pl.ds(spots[2], 1)] = red3c[0:1]
    all_c[1:2, pl.ds(spots[2], 1)] = red3c[pl.ds(1 + j, 1)]
    all_c[3:4, pl.ds(spots[2], 1)] = red3c[3:4]
    gathers = {}
    for n in range(3):
        swaps[n].wait_recv()
        gathers[n, 0] = gather_copies(n, 0)
        for c in gathers[n, 0]:
            c.start()
    for phase in range(2):
        for n in range(3):
            for c in gathers[n, phase]:
                c.wait_recv()
            gathers[n, phase + 1] = gather_copies(n, phase + 1)
            for c in gathers[n, phase + 1]:
                c.start()
    for n in range(3):
        for c in gathers[n, 2]:
            c.wait_recv()

    def rows(value):
        return value.reshape(value.shape[0] * 16, 128)

    sums = (q_sum, k_sum, v_sum)
    for c in range(9):
        for who, core in ((0, j), (1, jp)):
            column = pl.ds(pl.multiple_of(core * HALF + (c % 3) * 128, 128), 128)
            for n, unit, place, count, first in qkv_places(c):
                unit = (2 * who + unit if n == 0 else who if n == 1 else 1 + who)
                sums[c // 3][16 * first : 16 * (first + count), column] = rows(alls[n][unit, place : place + count])
    for c in range(6):
        for n, unit, place, count, first in out_places(c):
            out_sum[16 * first : 16 * (first + count), c * 128 : (c + 1) * 128] = rows(alls[n][unit, place : place + count])
    both = all_c[1, 24:50].astype(F32) + all_c[2, 24:50].astype(F32)
    router_sum[...] = rows(both[0:24])
    bias_sum[...] = both[24]
    gain_sum[...] = both[25]

    trade.wait_send()
    for c in swaps:
        c.wait_send()
    for copies in list(started.values()) + list(gathers.values()):
        for c in copies:
            c.wait_send()


def tail(*operands):
    vm = pl.BlockSpec(memory_space=pltpu.VMEM)

    def tiled(*lead):
        return [pltpu.VMEM(lead[:1] + (u,) + lead[1:] + (16, 128), BF) if len(lead) == 2 else pltpu.VMEM((u,) + lead + (16, 128), BF) for u in UNITS]

    return pl.pallas_call(
        tail_kernel,
        name="tail",
        out_shape=(
            jax.ShapeDtypeStruct((TOK, D), BF),
            jax.ShapeDtypeStruct((HALF, D), BF),
            jax.ShapeDtypeStruct((HALF, D), BF),
            jax.ShapeDtypeStruct((HALF, D), BF),
            jax.ShapeDtypeStruct((HALF, D), BF),
            jax.ShapeDtypeStruct((HALF, EXPERTS), F32),
            jax.ShapeDtypeStruct((16, 128), F32),
            jax.ShapeDtypeStruct((16, 128), F32),
        ),
        in_specs=[vm] * 12,
        out_specs=(vm,) * 8,
        scratch_shapes=[
            *tiled(64),
            *tiled(3, 16),
            *tiled(3, 4),
            *tiled(3, 1),
            *tiled(16),
            *tiled(4),
            *tiled(1),
            *tiled(64),
            pltpu.VMEM((TOK, D), BF),
            pltpu.VMEM((TOK, D), BF),
            pltpu.SemaphoreType.DMA((3, 3, 3)),
            pltpu.SemaphoreType.DMA((3, 3, 3)),
            pltpu.SemaphoreType.DMA((3, 3, 3)),
            pltpu.SemaphoreType.DMA((3, 3, 3)),
            pltpu.SemaphoreType.DMA((4,)),
            pltpu.SemaphoreType.DMA((4,)),
        ],
        compiler_params=pltpu.CompilerParams(collective_id=3, has_side_effects=True, vmem_limit_bytes=VMEM_BYTES),
    )(*operands)


def swapped(value):
    return lax.ppermute(value, "wshard", [(0, 1), (1, 0)])


def part(value, index, size, axis=0):
    return lax.dynamic_slice_in_dim(value, index * size, size, axis)


def rms_scale(values, gain):
    return values * lax.rsqrt(jnp.mean(values * values, axis=-1, keepdims=True) + EPSILON) * gain


def to_all(rows):
    return lax.all_to_all(rows, ("expert", "wshard"), split_axis=0, concat_axis=0, tiled=True)


def per_device(tokens, lengths, routes, attn_gain, query_weight, key_weight, value_weight, output_weight, bias_table, mix_gain, router_weight, expert_in, expert_out, cotangent):
    j = lax.axis_index("wshard")
    jp = 1 - j
    misc = jnp.zeros((24, HALF), F32)
    misc = misc.at[0:16, 0:12].set(bias_table.astype(F32))
    misc = misc.at[16].set(attn_gain.astype(F32)).at[17].set(mix_gain.astype(F32))
    qkv, normed, wqkv, wo_full, router_full, misc_full = window(tokens, query_weight, key_weight, value_weight, output_weight, router_weight, misc)
    gain_second = jnp.concatenate([misc_full[17], misc_full[41]])
    att, lse = attention(lengths, qkv, misc_full)
    got = swapped(part(att, jp, TOK))
    mine = part(att, j, TOK)
    att_row = jnp.where(j == 0, jnp.concatenate([mine, got], axis=1), jnp.concatenate([got, mine], axis=1))
    inputs = tokens.astype(F32)
    hidden = inputs + mm(att_row, wo_full)
    mixed = rms_scale(hidden, gain_second).astype(BF)
    router = jax.nn.softmax(mm(mixed, router_full), axis=-1)
    experts = jnp.arange(EXPERTS, dtype=jnp.int32)
    chosen = routes == experts[None, :]
    chosen_float = chosen.astype(F32)
    gate = jnp.sum(router * chosen_float, axis=1)
    out_grad = cotangent.astype(F32)
    made_grad = (gate[:, None] * out_grad).astype(BF)
    earlier = (jnp.arange(TOK)[:, None] > jnp.arange(TOK)[None, :]) & (routes == routes[:, 0][None, :])
    second = jnp.any(earlier, axis=1)
    place = [(chosen & (second == bool(r))[:, None]).astype(BF) for r in range(2)]
    sent = jnp.stack([mm(place[r], rows, TN).astype(BF) for rows in (mixed, made_grad) for r in range(2)], axis=1)
    arrived = to_all(sent)
    x = arrived[:, 0:2].reshape(2 * EXPERTS, D)
    g = arrived[:, 2:4].reshape(2 * EXPERTS, D)
    made, back, expert_in_grad, expert_out_grad = expert(x, g, expert_in, expert_out)
    home = to_all(jnp.concatenate([made.reshape(EXPERTS, 2, D), back.reshape(EXPERTS, 2, D)], axis=1))
    made_token = mm(place[0], home[:, 0]) + mm(place[1], home[:, 1])
    expert_mixed_grad = mm(place[0], home[:, 2]) + mm(place[1], home[:, 3])
    layer_out = (hidden + gate[:, None] * made_token).astype(BF)
    gate_grad = jnp.sum(out_grad * made_token, axis=1)
    logit_grad = ((gate_grad * gate)[:, None] * (chosen_float - router)).astype(BF)
    mixed_grad = mm(logit_grad, router_full, NT) + expert_mixed_grad
    hidden_part, mix_gain_grad = jax.vjp(rms_scale, hidden, gain_second)[1](mixed_grad)
    hidden_grad = out_grad + hidden_part
    branch_grad = hidden_grad.astype(BF)
    got = swapped(branch_grad)
    branch_chip = jnp.where(j == 0, jnp.concatenate([branch_grad, got]), jnp.concatenate([got, branch_grad]))
    att_grad = mm(branch_chip, output_weight, NT).astype(BF)
    delta = jnp.sum((att_grad.astype(F32) * att.astype(F32)).reshape(CHIP, 6, HEAD), axis=2)
    stat = jnp.concatenate([lse, jnp.pad(delta.T, ((0, 2), (0, 0)))], axis=0)
    dout_win, stat_win = spread(att_grad, stat)
    dqkv, bias_part = attention_back(lengths, qkv, dout_win, stat_win, misc_full)
    mix_row = jnp.broadcast_to(mix_gain_grad[None], (8, D))
    tokens_grad, q_sum, k_sum, v_sum, out_sum, router_sum, bias_sum, gain_sum = tail(
        dqkv, normed, wqkv, tokens, hidden_grad, att, branch_chip, mixed, logit_grad, mix_row, bias_part, misc_full
    )
    return (
        layer_out,
        tokens_grad,
        gain_sum[0:3].reshape(HALF),
        q_sum.astype(F32),
        k_sum.astype(F32),
        v_sum.astype(F32),
        out_sum.astype(F32),
        bias_sum[:, 0:12],
        gain_sum[3:6].reshape(HALF),
        router_sum,
        expert_in_grad,
        expert_out_grad,
    )


def solution(mesh):
    by_token = P(("expert", "wshard"), None)
    by_row = P("wshard", None)
    by_expert = P(("expert", "wshard"), None, None)
    return jax.shard_map(
        per_device,
        mesh=mesh,
        in_specs=(
            by_token,
            P(),
            by_token,
            P("wshard"),
            by_row,
            by_row,
            by_row,
            by_row,
            by_row,
            P("wshard"),
            by_row,
            by_expert,
            by_expert,
            by_token,
        ),
        out_specs=(
            by_token,
            by_token,
            P("wshard"),
            by_row,
            by_row,
            by_row,
            by_row,
            by_row,
            P("wshard"),
            by_row,
            by_expert,
            by_expert,
        ),
        check_vma=False,
    )
```

time: 817 us -> 252 us (0.31); the launches traced: 803 us -> 250 us
  starting transfers between devices: 241 us -> 0.64 us
  waiting for transfers between devices: 223 us -> 1.44 us
  Pallas kernels: 0 us -> 172 us
  local copies, waits for them, and re-layouts: 169 us -> 13.6 us
  matrix products: 113 us -> 4.53 us
  blocking collectives: 16.5 us -> 46.8 us
  between operations: 16.3 us -> 1.09 us
  other arithmetic: 23.6 us -> 9.68 us
    ppermute x64 -> x2, starting transfers between devices: 202 us -> 0.64 us  [swapped(): return lax.ppermute(value, 'wshard', [(0, 1), (1, 0)])]
    pallas_call x0 -> x6, Pallas kernels: none -> 172 us  [the longest x1 59.3 us: tail(): pl.pallas_call(tail_kernel, name='tail', out_shape=(jax.ShapeDtypeStruct(...]
    psum x1 -> x0, waiting for transfers between devices: 126 us -> none  [together(): total = lax.psum(jnp.concatenate([a.ravel() for a in arrays]), axis)]
    dot_general x33 -> x12, matrix products: 113 us -> 4.53 us  [mm(): return lax.dot_general(left, right, dims, preferred_element_type=F32)]
    ppermute x64 -> x2, waiting for transfers between devices: 74.9 us -> 1.44 us  [swapped(): return lax.ppermute(value, 'wshard', [(0, 1), (1, 0)])]
    concatenate x9 -> x0, local copies, waits for them, and re-layouts: 73 us -> none  [the longest x1 38.6 us: together(): total = lax.psum(jnp.concatenate([a.ravel() for a in arrays]), axis)]
    all_to_all x6 -> x0, starting transfers between devices: 39.1 us -> none  [the longest x1 10.5 us: per_device(): lax.all_to_all(expert_back.reshape(device_count, capacity, model_width).a...]
    all_to_all x1 -> x2, blocking collectives: 9.19 us -> 46.8 us  [to_all(): lax.all_to_all(rows, ('expert', 'wshard'), split_axis=0, concat_axis=0, t...]
  transfers between devices with their start and end apart: 75 -> 2, of which waited for: 23 -> 1; matrix products, arithmetic and copies ran while one was open for 16% -> 0% of each run, Pallas kernels for 0% -> 0%
where the time goes in v1:
time: 252 us; the launch traced here: 250 us
  Pallas kernels  172 us (68%)
  blocking collectives  46.8 us (19%)
  local copies, waits for them, and re-layouts  13.6 us (5%)
  other arithmetic  9.68 us (4%)
  matrix products  4.53 us (2%)
    pallas_call x1, Pallas kernels, tail(): pl.pallas_call(tail_kernel, name='tail', out_shape=(jax.ShapeDtypeStruct(...  59.3 us
    all_to_all x2, blocking collectives, to_all(): lax.all_to_all(rows, ('expert', 'wshard'), split_axis=0, concat_axis=0, t...  46.8 us
    pallas_call x1, Pallas kernels, window(): pl.pallas_call(window_kernel, name='window', out_shape=(jax.ShapeDtypeStr...  33.4 us
    pallas_call x1, Pallas kernels, spread(): pl.pallas_call(spread_kernel, name='spread', out_shape=(jax.ShapeDtypeStr...  27.3 us
    pallas_call x1, Pallas kernels, attention_back(): pl.pallas_call(backward_kernel, name='attention_back', out_shape=(jax.Sha...  27.2 us
    pallas_call x1, Pallas kernels, expert(): pl.pallas_call(expert_kernel, name='expert', grid=(FF // FF_TILE,), out_s...  13 us
    pallas_call x1, Pallas kernels, attention(): pl.pallas_call(forward_kernel, name='attention', out_shape=(jax.ShapeDtyp...  12.2 us
  transfers between devices with their start and end apart: 2, of which 1 were waited for; matrix products, arithmetic and copies ran while one was open for 0% of the time, Pallas kernels for 0%

profile of v1, /device:TPU:8, one launch (start us, length us, event | category | flops | bytes accessed | tf_op | source)
XLA Modules:
  0.0 250.2 jit_solution(15314700222327115887)
XLA Ops:
  0.6 0.7 pad_convert_fusion
  1.3 0.7 reshape.170
  2.0 0.7 reshape.171
  2.8 0.6 copy-done.13
  3.4 33.4 %window.1 = (bf16[2304,1152]{1,0:T(8,128)(2,1)}, bf16[256,768]{1,0:T(8,128)(2,1)}, bf16[768,1152]{1,0:T(8,128)(2,1)}, bf16[768,768]{1,0:T(8,128)(2,1)}, bf16[768,128]{1,0:T(8,128)(2,1)}, /*index=5*/f32[48,384]{1,0:T(8,128)}) custom-call(bf16[128,768]{1,0:T(8,128)(2,1)} %tok.3, bf16[384,768]{1,0:T(8,128)(2,1)} %wq.1, bf16[384,768]{1,0:T(8,128)(2,1)} %wk.1, ...), custom_call_target="tpu_custom_call" | custom-call | tf_op jit(solution)/shard_map/window/pallas_call | solution.py:141
  36.8 12.2 %attention.1 = (bf16[256,384]{1,0:T(8,128)(2,1)}, f32[8,256]{1,0:T(8,128)}) custom-call(s32[32]{0:T(128)} %lengths.3, bf16[2304,1152]{1,0:T(8,128)(2,1)} %get-tuple-element.72.qkv, f32[48,384]{1,0:T(8,128)} %get-tuple-element.73.misc), custom_call_target="tpu_custom_call" | custom-call | tf_op jit(solution)/shard_map/attention/pallas_call | solution.py:255
  49.1 1.0 constant_dynamic-slice_fusion.1
  50.1 0.6 collective-permute-start
  50.7 0.7 slice_reduce_fusion.1
  51.7 0.4 multiply_reduce_fusion.2
  52.3 0.3 fusion.51
  52.8 0.2 select_reduce_fusion
  53.1 0.3 fusion.3
  53.4 0.3 fusion.2
  53.7 0.3 fusion
  54.1 0.3 fusion.1
  54.5 0.6 copy.36
  55.1 26.2 %all_to_all.10 = bf16[128,4,768]{2,1,0:T(4,128)(2,1)S(1)} all-to-all(bf16[128,4,768]{2,1,0:T(4,128)(2,1)S(1)} %copy.36), channel_id=1, replica_groups=mesh['expert'=64,'wshard'=2] {'expert','wshard'}, dimensions={0} | all-to-all | bytes 1572864 | tf_op jit(solution)/shard_map/all_to_all | solution.py:727
  81.3 0.5 fusion.50
  81.9 0.9 reshape.163.x
  82.8 0.9 reshape.164.g
  83.7 13.0 %expert.1 = (bf16[256,768]{1,0:T(8,128)(2,1)}, bf16[256,768]{1,0:T(8,128)(2,1)}, bf16[1,768,3072]{2,1,0:T(8,128)(2,1)}, bf16[1,3072,768]{2,1,0:T(8,128)(2,1)}) custom-call(bf16[256,768]{1,0:T(8,128)(2,1)} %reshape.163.x, bf16[256,768]{1,0:T(8,128)(2,1)} %reshape.164.g, bf16[1,768,3072]{2,1,0:T(8,128)(2,1)} %w_in.1, bf16[1,3072,768]{2,1,0:T(8,128)(2,1)} %w_out.1), custom_call_target="tpu_custom_call" | custom-call | tf_op jit(solution)/shard_map/expert/pallas_call | solution.py:454
  96.7 1.1 reshape.165
  97.8 1.1 reshape.166
  98.9 0.8 pad_maximum_fusion.1
  99.8 20.7 %all_to_all.11 = bf16[128,4,768]{2,1,0:T(4,128)(2,1)S(1)} all-to-all(bf16[128,4,768]{2,1,0:T(4,128)(2,1)S(1)} %pad_maximum_fusion.1), channel_id=1, replica_groups=mesh['expert'=64,'wshard'=2] {'expert','wshard'}, dimensions={0} | all-to-all | bytes 1572864 | tf_op jit(solution)/shard_map/all_to_all | solution.py:727
  120.4 1.1 fusion.49
  121.6 0.3 fusion.12
  121.8 0.3 fusion.5
  122.3 0.3 fusion.11
  122.6 0.3 convolution_add_fusion
  122.9 0.3 multiply_reduce_fusion
  123.3 1.0 fusion.48
  124.2 1.4 collective-permute-done.1
  125.8 1.1 convert_multiply_fusion.2
  127.1 0.6 select_maximum_fusion.stat
  127.7 27.3 %spread.1 = (bf16[2304,384]{1,0:T(8,128)(2,1)}, f32[9,16,256]{2,1,0:T(8,128)}) custom-call(bf16[256,384]{1,0:T(8,128)(2,1)} %get-tuple-element.121.dout, f32[16,256]{1,0:T(8,128)} %select_maximum_fusion.stat), custom_call_target="tpu_custom_call" | custom-call | tf_op jit(solution)/shard_map/spread/pallas_call | solution.py:406
  155.0 27.2 %attention_back.1 = (bf16[256,1152]{1,0:T(8,128)(2,1)}, f32[32,128]{1,0:T(8,128)}) custom-call(s32[32]{0:T(128)} %lengths.3, bf16[2304,1152]{1,0:T(8,128)(2,1)} %get-tuple-element.72.qkv, bf16[2304,384]{1,0:T(8,128)(2,1)} %get-tuple-element.80.dout, f32[9,16,256]{2,1,0:T(8,128)} %get-tuple-element.81.stat, f32[48,384]{1,0:T(8,128)} %get-tuple-element.73.misc), custom_call_target="tpu_custom_call" | custom-call | tf_op jit(solution)/shard_map/attention_back/pallas_call | solution.py:354
  182.2 0.6 broadcast_in_dim.5.mix_grad
  182.8 59.3 %tail.1 = (bf16[128,768]{1,0:T(8,128)(2,1)}, bf16[384,768]{1,0:T(8,128)(2,1)}, bf16[384,768]{1,0:T(8,128)(2,1)}, bf16[384,768]{1,0:T(8,128)(2,1)}, bf16[384,768]...) custom-call(bf16[256,1152]{1,0:T(8,128)(2,1)} %get-tuple-element.82.dqkv, ...), custom_call_target="tpu_custom_call" | custom-call | tf_op jit(solution)/shard_map/tail/pallas_call | solution.py:677
  242.1 2.2 convert_element_type.79
  244.4 1.1 convert_element_type.80
  245.5 1.1 convert_element_type.81
  246.6 1.1 convert_element_type.82
  247.7 0.6 slice_bitcast_fusion
  248.3 0.7 copy.61
  248.9 0.6 copy.62
  249.5 0.7 copy.63
  (55 shorter events, 1.3 us)
Async XLA Ops:
  2.8 0.6 copy-start.13
  36.8 14.6 %copy-start.14 = (s32[128,1]{0,1:T(1,128)S(1)}, s32[128,1]{0,1:T(1,128)}, u32[]{:S(2)}) copy-start(s32[128,1]{0,1:T(1,128)} %param.22) | copy-start | bytes 1540
  36.8 14.9 %copy-start.5 = (bf16[128,768]{1,0:T(8,128)(2,1)S(1)}, bf16[128,768]{1,0:T(8,128)(2,1)}, u32[]{:S(2)}) copy-start(bf16[128,768]{1,0:T(8,128)(2,1)} %tok.3) | copy-start | bytes 589828
  36.8 14.9 %copy-start.18 = (bf16[768,768]{1,0:T(8,128)(2,1)S(1)}, bf16[768,768]{1,0:T(8,128)(2,1)}, u32[]{:S(2)}) copy-start(bf16[768,768]{1,0:T(8,128)(2,1)} %get-tuple-element.75) | copy-start | bytes 3538948
  49.1 3.2 %copy-start.6 = (bf16[768,128]{1,0:T(8,128)(2,1)S(1)}, bf16[768,128]{1,0:T(8,128)(2,1)}, u32[]{:S(2)}) copy-start(bf16[768,128]{1,0:T(8,128)(2,1)} %get-tuple-element.76) | copy-start | bytes 589828
  50.1 1.6 collective-permute-start
  51.7 1.4 copy-start.2
  52.3 2.3 copy-start
  122.3 1.9 copy-start.10
  123.2 2.5 %copy-start.3 = (bf16[384,768]{1,0:T(8,128)(2,1)S(1)}, bf16[384,768]{1,0:T(8,128)(2,1)}, u32[]{:S(2)}) copy-start(bf16[384,768]{1,0:T(8,128)(2,1)} %wo.1) | copy-start | bytes 1769476
  123.2 2.5 %copy-start.4 = (bf16[256,384]{1,0:T(8,128)(2,1)S(1)}, bf16[256,384]{1,0:T(8,128)(2,1)}, u32[]{:S(2)}) copy-start(bf16[256,384]{1,0:T(8,128)(2,1)} %get-tuple-element.74.att) | copy-start | bytes 589828
  124.2 1.4 collective-permute-start.1
  125.8 29.2 %copy-start.1 = (bf16[256,768]{1,0:T(8,128)(2,1)}, bf16[256,768]{1,0:T(8,128)(2,1)S(1)}, u32[]{:S(2)}) copy-start(bf16[256,768]{1,0:T(8,128)(2,1)S(1)} %maximum_select_fusion.branch) | copy-start | bytes 1179652
  125.8 1.3 copy-start.16
  242.1 2.3 copy-start.9
  242.1 3.4 %copy-start.8 = (bf16[384,768]{1,0:T(8,128)(2,1)S(1)}, bf16[384,768]{1,0:T(8,128)(2,1)}, u32[]{:S(2)}) copy-start(bf16[384,768]{1,0:T(8,128)(2,1)} %get-tuple-element.90) | copy-start | bytes 1769476
  244.4 2.2 copy-start.7
  245.5 2.2 copy-start.17
  245.5 2.8 %copy-start.12 = (bf16[128,768]{1,0:T(8,128)(2,1)S(1)}, bf16[128,768]{1,0:T(8,128)(2,1)}, u32[]{:S(2)}) copy-start(bf16[128,768]{1,0:T(8,128)(2,1)} %get-tuple-element.135) | copy-start | bytes 589828
  245.5 3.5 %copy-start.15 = (f32[16,128]{1,0:T(8,128)S(1)}, f32[16,128]{1,0:T(8,128)}, u32[]{:S(2)}) copy-start(f32[16,128]{1,0:T(8,128)} %get-tuple-element.92) | copy-start | bytes 24580
  245.5 4.1 %copy-start.11 = (f32[384,128]{1,0:T(8,128)S(1)}, f32[384,128]{1,0:T(8,128)}, u32[]{:S(2)}) copy-start(f32[384,128]{1,0:T(8,128)} %get-tuple-element.143) | copy-start | bytes 589828

commit v2 on v1

v2 whole, which is shorter than its diff:
```python
import functools

import jax
import jax.numpy as jnp
from jax import lax
from jax.experimental import pallas as pl
from jax.experimental.pallas import tpu as pltpu
from jax.sharding import PartitionSpec as P

MESH = pl.DeviceIdType.MESH
BF = jnp.bfloat16
F32 = jnp.float32
EPSILON = 1e-06
FAR_EDGES = (12, 16, 23, 32, 46, 64, 91)

D = 768
HALF = 384
HEAD = 64
TOK = 128
CHIP = 256
REACH = 4
SLOTS = 2 * REACH + 1
WIN = SLOTS * CHIP
MID = REACH * CHIP
TOTAL = 16384
EXPERTS = 128
NB = 32
FF = 3072
NEAR = 3 * CHIP
LOOP = 1024
VMEM_BYTES = 56 * 1024 * 1024

NT = (((1,), (1,)), ((), ()))
TN = (((0,), (0,)), ((), ()))
NN = (((1,), (0,)), ((), ()))


def mm(left, right, dims=NN):
    return lax.dot_general(left, right, dims, preferred_element_type=F32)


def bucket_of(relative):
    distance = jnp.abs(relative)
    far_bucket = 8 + sum(((distance >= edge).astype(jnp.int32) for edge in FAR_EDGES))
    near_far = jnp.where(distance < 8, distance, far_bucket)
    return near_far + 16 * (relative > 0).astype(jnp.int32)


def tile(ref, rows, start, width):
    return ref[rows, pl.ds(pl.multiple_of(start, 128), width)]


OFFSETS = (1, -1, 4, -4, 3, -3, 2, -2)
DIRECT = 6
AXES = {"y": 16, "x": 4, "z": 1}


def remote(src, dst, ssem, rsem, chip, core):
    return pltpu.make_async_remote_copy(src_ref=src, dst_ref=dst, send_sem=ssem, recv_sem=rsem, device_id=(chip, core), device_id_type=MESH)


def chip_at(e, m):
    chips = lax.axis_size("expert")
    return lax.rem(e + m + chips, chips)


def signal(barrier, chip, core):
    pl.semaphore_signal(barrier, inc=1, device_id=(chip, core), device_id_type=MESH)


def chunk(c):
    return slice(c * CHIP, (c + 1) * CHIP)


def both_gains(misc, row):
    return jnp.concatenate([misc[row : row + 1, :], misc[row + 24 : row + 25, :]], axis=1)


def placing(routes_row):
    lane = lax.broadcasted_iota(jnp.int32, (TOK, EXPERTS), 1)
    row = lax.broadcasted_iota(jnp.int32, (TOK, EXPERTS), 0)
    across = jnp.broadcast_to(routes_row[0:1, :], (TOK, TOK))
    down = across.T
    chosen = (down == lane).astype(F32)
    earlier = ((down == across) & (lane < row)).astype(F32)
    second = jnp.max(earlier, axis=1, keepdims=True)
    return chosen, (chosen * (1.0 - second)).astype(BF), (chosen * second).astype(BF)


def prepare(lengths, mask):
    e = lax.axis_index("expert")
    row_pos = (e - REACH) * CHIP + lax.broadcasted_iota(jnp.int32, (8, WIN), 1)
    col_pos = e * CHIP + lax.broadcasted_iota(jnp.int32, (CHIP, 128), 0)

    def count(n, state):
        end, rows, cols = state
        end = end + lengths[n]
        return end, rows + (row_pos >= end).astype(jnp.int32), cols + (col_pos >= end).astype(jnp.int32)

    zero = jnp.zeros((8, WIN), jnp.int32)
    _, rows, cols = lax.fori_loop(0, 32, count, (jnp.int32(0), zero, jnp.zeros((CHIP, 128), jnp.int32)))
    rows = jnp.where((row_pos >= 0) & (row_pos < TOTAL), rows, -1)
    for c in range(SLOTS):
        part = rows[0:1, c * CHIP : (c + 1) * CHIP]
        mask[:, c * CHIP : (c + 1) * CHIP] = jnp.where(cols[:, 0:1] == part, 0.0, -1e9).astype(F32)


def prepare_biases(misc, diag, ways):
    table = jnp.concatenate([misc[0:16, 0:128], misc[24:40, 0:128]], axis=0).astype(BF)
    for n, sign in enumerate(ways):
        hot = diagonal_buckets(sign)
        diag[n * 16 : (n + 1) * 16, :] = mm(table, hot.astype(BF), TN)[0:16]


def diagonal_buckets(sign):
    m = lax.broadcasted_iota(jnp.int32, (NB, LOOP), 1)
    r = jnp.where(m < NEAR, m, m - LOOP) - CHIP
    b = lax.broadcasted_iota(jnp.int32, (NB, LOOP), 0)
    return (bucket_of(sign * r) == b).astype(F32)


def biased(raw, c, mask, near, left, right):
    s = raw + mask[:, c * CHIP : (c + 1) * CHIP]
    if c < REACH - 1:
        return s + left
    if c > REACH + 1:
        return s + right
    lower = (c - REACH + 1) * CHIP
    return s + near[:, lower : lower + CHIP]


def near_tile(diag, row):
    line = diag[pl.ds(row, 1), :]
    spread = pltpu.roll(jnp.broadcast_to(line, (CHIP, LOOP)), 0, 1, stride=1, stride_axis=0)
    return spread[:, 0:NEAR], line[:, 0:1], line[:, NEAR - 1 : NEAR]


def front_kernel(lengths, tok_any, wq, wk, wv, wo_any, router_any, misc_any, tok, wo, routes_row, cot, qkv_any, normed_any, wqkv_any, router_full, misc, att, lse, hidden, mixed, router, sent, qkv, normed, wqkv, win, wo_other, att_other, mask, diag, scores, lse_cols, send, recv, fsend, frecv, wsend, wrecv, local, store):
    e = lax.axis_index("expert")
    j = lax.axis_index("wshard")
    jp = 1 - j
    barrier = pltpu.get_barrier_semaphore()
    for m in OFFSETS:
        signal(barrier, chip_at(e, m), j)
    signal(barrier, e, jp)

    def rows_of(slot, core):
        return win.at[pl.ds(pl.multiple_of(slot * CHIP + core * TOK, TOK), TOK), :]

    weights = []
    kept = []
    for n, w in enumerate((wq, wk, wv)):
        rows = pl.ds(pl.multiple_of(j * HALF, HALF), HALF)
        there = w.at[:, pl.ds(pl.multiple_of(jp * HALF, 128), HALF)]
        here = w.at[:, pl.ds(pl.multiple_of(j * HALF, 128), HALF)]
        dst = wqkv.at[rows, n * HALF : (n + 1) * HALF]
        weights.append(remote(there, dst, wsend.at[n], wrecv.at[n], e, jp))
        kept.append(pltpu.make_async_copy(here, dst, local.at[1 + n]))
    for n, (src, dst, size) in enumerate(((misc_any, misc, 24), (router_any, router_full, HALF))):
        rows = pl.ds(pl.multiple_of(j * size, 8), size)
        weights.append(remote(src, dst.at[rows, :], wsend.at[3 + n], wrecv.at[3 + n], e, jp))
        kept.append(pltpu.make_async_copy(src, dst.at[rows, :], local.at[4 + n]))
    weights.append(remote(wo_any, wo_other, wsend.at[5], wrecv.at[5], e, jp))
    mine = pltpu.make_async_copy(tok_any, rows_of(REACH, j), local.at[0])
    mine.start()
    for c in kept:
        c.start()

    copies = []
    for n, m in enumerate(OFFSETS):
        src = tok_any if n < DIRECT else rows_of(REACH - m // 2, j)
        to = chip_at(e, m if n < DIRECT else m // 2)
        copies.append(remote(src, rows_of(REACH - m, j), send.at[n], recv.at[n], to, j))
    passed = [remote(rows_of(REACH - m, j), rows_of(REACH - m, j), fsend.at[n], frecv.at[n], e, jp) for n, m in enumerate(OFFSETS)]
    swap = remote(tok_any, rows_of(REACH, j), fsend.at[8], frecv.at[8], e, jp)

    pl.semaphore_wait(barrier, len(OFFSETS) + 1)
    for c in copies[:DIRECT]:
        c.start()
    weights[3].start()
    for c in weights[:3]:
        c.start()
    swap.start()
    for c in weights[4:]:
        c.start()
    prepare(lengths, mask)
    mine.wait()
    for c in kept:
        c.wait()
    for c in weights[:4]:
        c.wait_recv()
    prepare_biases(misc, diag, (1,))
    gain = both_gains(misc, 16)

    def project(slot):
        x = win[chunk(slot), :].astype(F32)
        y = (x * lax.rsqrt(jnp.mean(x * x, axis=-1, keepdims=True) + EPSILON) * gain).astype(BF)
        if slot == REACH:
            normed[...] = y
        qkv[chunk(slot), :] = mm(y, wqkv[...]).astype(BF)

    for n in range(2):
        copies[n].wait_recv()
        copies[DIRECT + n].start()
        passed[n].start()
    swap.wait_recv()
    project(REACH)
    for n in range(2, len(OFFSETS) + 2):
        if n < len(OFFSETS):
            copies[n].wait_recv()
            passed[n].start()
        passed[n - 2].wait_recv()
        project(REACH - OFFSETS[n - 2])

    stores = [pltpu.make_async_copy(src, dst, store.at[n]) for n, (src, dst) in enumerate(((qkv, qkv_any), (normed, normed_any), (wqkv, wqkv_any)))]
    for c in stores:
        c.start()
    lane = lax.broadcasted_iota(jnp.int32, (CHIP, 128), 1)
    lse_cols[...] = jnp.zeros((CHIP, 128), F32)

    def pair(p, carry):
        q = tile(qkv, slice(MID, MID + CHIP), p * 128, 128).astype(F32) * 0.125
        outs = []
        for hh in range(2):
            own = (lane // HEAD) == hh
            qm = jnp.where(own, q, 0.0).astype(BF)
            near, left, right = near_tile(diag, j * 6 + 2 * p + hh)
            top = None
            for c in range(SLOTS):
                k = tile(qkv, chunk(c), HALF + p * 128, 128)
                s = biased(mm(qm, k, NT), c, mask, near, left, right)
                scores[:, chunk(c)] = s
                top = s if top is None else jnp.maximum(top, s)
            top = jnp.max(top, axis=1, keepdims=True)
            total = jnp.zeros((CHIP, CHIP), F32)
            out = jnp.zeros((CHIP, 128), F32)
            for c in range(SLOTS):
                x = jnp.exp(scores[:, chunk(c)] - top)
                total = total + x
                out = out + mm(x.astype(BF), tile(qkv, chunk(c), 2 * HALF + p * 128, 128))
            total = jnp.sum(total, axis=1, keepdims=True)
            outs.append(out / total)
            lse_cols[...] = jnp.where(lane == 2 * p + hh, top + jnp.log(total), lse_cols[...])
        att[:, pl.ds(pl.multiple_of(p * 128, 128), 128)] = jnp.where(lane < HEAD, outs[0], outs[1]).astype(BF)
        return carry

    lax.fori_loop(0, 3, pair, 0)
    lse[...] = lse_cols[...].T[0:8, :]

    here = pl.ds(pl.multiple_of(j * TOK, TOK), TOK)
    there = pl.ds(pl.multiple_of(jp * TOK, TOK), TOK)
    trade = remote(att.at[there, :], att_other, wsend.at[6], wrecv.at[6], e, jp)
    trade.start()
    chosen, first, second = placing(routes_row)
    branch = mm(att[here, :], wo[...])
    for c in weights[4:]:
        c.wait_recv()
    trade.wait_recv()
    total = tok[...].astype(F32) + (branch + mm(att_other[...], wo_other[...]))
    hidden[...] = total
    low = (total * lax.rsqrt(jnp.mean(total * total, axis=-1, keepdims=True) + EPSILON) * both_gains(misc, 17)).astype(BF)
    mixed[...] = low
    logits = mm(low, router_full[...])
    powers = jnp.exp(logits - jnp.max(logits, axis=1, keepdims=True))
    probs = powers / jnp.sum(powers, axis=1, keepdims=True)
    router[...] = probs
    gate = jnp.sum(probs * chosen, axis=1, keepdims=True)
    made_grad = (gate * cot[...].astype(F32)).astype(BF)
    for n, (place, rows) in enumerate(((first, low), (second, low), (first, made_grad), (second, made_grad))):
        sent[n] = mm(place, rows, TN).astype(BF)

    trade.wait_send()
    swap.wait_send()
    for c in weights + copies + passed:
        c.wait_send()
    for c in stores:
        c.wait()


def front(lengths, tokens, wq, wk, wv, wo, router, misc, row, cotangent):
    smem = pl.BlockSpec(memory_space=pltpu.SMEM)
    hbm = pl.BlockSpec(memory_space=pl.ANY)
    vm = pl.BlockSpec(memory_space=pltpu.VMEM)
    return pl.pallas_call(
        front_kernel,
        name="front",
        out_shape=(
            jax.ShapeDtypeStruct((WIN, 3 * HALF), BF),
            jax.ShapeDtypeStruct((CHIP, D), BF),
            jax.ShapeDtypeStruct((D, 3 * HALF), BF),
            jax.ShapeDtypeStruct((D, EXPERTS), BF),
            jax.ShapeDtypeStruct((48, HALF), F32),
            jax.ShapeDtypeStruct((CHIP, HALF), BF),
            jax.ShapeDtypeStruct((8, CHIP), F32),
            jax.ShapeDtypeStruct((TOK, D), F32),
            jax.ShapeDtypeStruct((TOK, D), BF),
            jax.ShapeDtypeStruct((TOK, EXPERTS), F32),
            jax.ShapeDtypeStruct((4, EXPERTS, D), BF),
        ),
        in_specs=[smem] + [hbm] * 7 + [vm] * 4,
        out_specs=(hbm,) * 3 + (vm,) * 8,
        scratch_shapes=[
            pltpu.VMEM((WIN, 3 * HALF), BF),
            pltpu.VMEM((CHIP, D), BF),
            pltpu.VMEM((D, 3 * HALF), BF),
            pltpu.VMEM((WIN, D), BF),
            pltpu.VMEM((HALF, D), BF),
            pltpu.VMEM((TOK, HALF), BF),
            pltpu.VMEM((CHIP, WIN), F32),
            pltpu.VMEM((16, LOOP), F32),
            pltpu.VMEM((CHIP, WIN), F32),
            pltpu.VMEM((CHIP, 128), F32),
            pltpu.SemaphoreType.DMA((8,)),
            pltpu.SemaphoreType.DMA((8,)),
            pltpu.SemaphoreType.DMA((9,)),
            pltpu.SemaphoreType.DMA((9,)),
            pltpu.SemaphoreType.DMA((7,)),
            pltpu.SemaphoreType.DMA((7,)),
            pltpu.SemaphoreType.DMA((6,)),
            pltpu.SemaphoreType.DMA((3,)),
        ],
        compiler_params=pltpu.CompilerParams(collective_id=1, has_side_effects=True, vmem_limit_bytes=VMEM_BYTES),
    )(lengths, tokens, wq, wk, wv, wo, router, misc, tokens, wo, row, cotangent)


FF_TILE = 512


def expert_kernel(x, g, w_in, w_out, made_back, d_in, d_out, made_sum, back_sum):
    step = pl.program_id(0)

    @pl.when(step == 0)
    def _():
        made_sum[...] = jnp.zeros_like(made_sum)
        back_sum[...] = jnp.zeros_like(back_sum)

    pre = mm(x[...], w_in[0])
    half_erf = 0.5 * lax.erf(pre * (0.5**0.5)) + 0.5
    act = (pre * half_erf).astype(BF)
    slope = half_erf + pre * jnp.exp(-0.5 * pre * pre) * (0.5 * 0.7978845608028654)
    act_grad = mm(g[...], w_out[0], NT)
    pre_grad = (act_grad * slope).astype(BF)
    made_sum[...] += mm(act, w_out[0])
    back_sum[...] += mm(pre_grad, w_in[0], NT)
    d_out[0] = mm(act, g[...], TN).astype(BF)
    d_in[0] = mm(x[...], pre_grad, TN).astype(BF)

    @pl.when(step == pl.num_programs(0) - 1)
    def _():
        made_back[0 : 2 * EXPERTS, :] = made_sum[...].astype(BF)
        made_back[2 * EXPERTS :, :] = back_sum[...].astype(BF)


def expert(arrived, w_in, w_out):
    rows = 2 * EXPERTS
    forward = pl.BlockSpec((rows, D), lambda f: (0, 0))
    backward = pl.BlockSpec((rows, D), lambda f: (1, 0))
    whole = pl.BlockSpec((2 * rows, D), lambda f: (0, 0))
    by_in = pl.BlockSpec((1, D, FF_TILE), lambda f: (0, 0, f))
    by_out = pl.BlockSpec((1, FF_TILE, D), lambda f: (0, f, 0))
    return pl.pallas_call(
        expert_kernel,
        name="expert",
        grid=(FF // FF_TILE,),
        out_shape=(
            jax.ShapeDtypeStruct((2 * rows, D), BF),
            jax.ShapeDtypeStruct((1, D, FF), BF),
            jax.ShapeDtypeStruct((1, FF, D), BF),
        ),
        in_specs=[forward, backward, by_in, by_out],
        out_specs=(whole, by_in, by_out),
        scratch_shapes=[pltpu.VMEM((rows, D), F32), pltpu.VMEM((rows, D), F32)],
        compiler_params=pltpu.CompilerParams(vmem_limit_bytes=VMEM_BYTES, dimension_semantics=("arbitrary",)),
    )(arrived, arrived, w_in, w_out)


ORDERS = ("zxy", "xyz", "yzx")
RING = 16
PLANE = [(d, f) for d in range(4) for f in range(4) if d + f > 0]


class Sum:
    def __init__(self, e, j, order, part, ring, plane, ring_sum, plane_sum, all_, ring_sems, plane_sems):
        self.e, self.j, self.order = e, j, order
        self.part, self.ring, self.plane, self.ring_sum, self.plane_sum, self.all = part, ring, plane, ring_sum, plane_sum, all_
        self.ring_sems, self.plane_sems = ring_sems, plane_sems
        self.coord = [lax.rem(e // AXES[a], 4) for a in order]

    def peer(self, *steps):
        to = self.e
        for axis, at, d in zip(self.order, self.coord, steps):
            to = to + (lax.rem(at + d, 4) - at) * AXES[axis]
        return to

    def block(self, d, first, count):
        return pl.ds(lax.rem(self.coord[0] + d + 4, 4) * RING + first, count)

    def copy(self, src, dst, sems, n, to):
        return remote(src, dst, sems[0].at[n], sems[1].at[n], to, self.j)

    def reduce_copies(self, which):
        h = RING // 2
        up, down = self.peer(1), self.peer(3)
        pieces = [
            (lambda: self.part.at[:, self.block(2, 0, h)], up),
            (lambda: self.part.at[:, self.block(2, h, h)], down),
            (lambda: self.part.at[:, self.block(1, h, h)], up),
            (lambda: self.part.at[:, self.block(3, 0, h)], down),
            (lambda: self.ring.at[6], up),
            (lambda: self.ring.at[7], down),
        ]
        return [self.copy(pieces[n][0](), self.ring.at[n], self.ring_sems, n, pieces[n][1]) for n in which]

    def gather_copies(self, which):
        h = RING // 2
        up, down = self.peer(1), self.peer(3)
        pieces = [(0, 0, RING, up), (0, 0, RING, down), (-1, 0, h, up), (1, h, h, down)]
        found = []
        for n in which:
            d, first, count, to = pieces[n]
            ref = self.all.at[:, self.block(d, first, count)]
            found.append(self.copy(ref, ref, self.ring_sems, 6 + n, to))
        return found

    def plane_copies(self, back):
        found = []
        for n, (d, f) in enumerate(PLANE):
            to = self.peer(0, d, f)
            if back:
                ref = self.all.at[:, pl.ds(self.coord[0] * RING + self.coord[1] * 4 + self.coord[2], 1)]
                found.append(self.copy(ref, ref, self.plane_sems, 15 + n, to))
            else:
                place = lax.rem(self.coord[1] + d, 4) * 4 + lax.rem(self.coord[2] + f, 4)
                found.append(self.copy(self.ring_sum.at[:, pl.ds(place, 1)], self.plane.at[n], self.plane_sems, n, to))
        return found

    def start_ring(self):
        for c in self.reduce_copies(range(4)):
            c.start()

    def pass_ring(self):
        h = RING // 2
        for n, where in ((0, self.block(1, 0, h)), (1, self.block(3, h, h))):
            came, goes = self.reduce_copies((n, 4 + n))
            came.wait_recv()
            self.ring[6 + n] = (self.part[:, where].astype(F32) + self.ring[n].astype(F32)).astype(BF)
            goes.start()

    def ring_to_plane(self):
        h = RING // 2
        for c in self.reduce_copies(range(2, 6)):
            c.wait_recv()
        for first, others in ((0, (4, 3)), (h, (5, 2))):
            total = self.part[:, self.block(0, first, h)].astype(F32)
            for n in others:
                total = total + self.ring[n].astype(F32)
            self.ring_sum[:, first : first + h] = total.astype(BF)
        for c in self.plane_copies(False):
            c.start()

    def plane_back(self):
        own = self.coord[1] * 4 + self.coord[2]
        total = self.ring_sum[:, pl.ds(own, 1)].astype(F32)
        for n, c in enumerate(self.plane_copies(False)):
            c.wait_recv()
            total = total + self.plane[n].astype(F32)
        self.all[:, pl.ds(self.coord[0] * RING + own, 1)] = total.astype(BF)
        for c in self.plane_copies(True):
            c.start()

    def plane_to_ring(self):
        for c in self.plane_copies(True):
            c.wait_recv()
        for c in self.gather_copies((0, 1)):
            c.start()

    def pass_back(self):
        for n in range(2):
            came, goes = self.gather_copies((n, 2 + n))
            came.wait_recv()
            goes.start()

    def end(self):
        for c in self.gather_copies((2, 3)):
            c.wait_recv()

    def end_sends(self):
        for c in self.reduce_copies(range(6)) + self.plane_copies(False) + self.plane_copies(True) + self.gather_copies(range(4)):
            c.wait_send()


def sum_scratch(units):
    return [
        pltpu.VMEM((units, 64, 16, 128), BF),
        pltpu.VMEM((8, units, RING // 2, 16, 128), BF),
        pltpu.VMEM((15, units, 1, 16, 128), BF),
        pltpu.VMEM((units, RING, 16, 128), BF),
        pltpu.VMEM((units, 1, 16, 128), BF),
        pltpu.VMEM((units, 64, 16, 128), BF),
        pltpu.SemaphoreType.DMA((10,)),
        pltpu.SemaphoreType.DMA((10,)),
        pltpu.SemaphoreType.DMA((30,)),
        pltpu.SemaphoreType.DMA((30,)),
    ]


def sums_of(e, j, scratch):
    found = []
    for n, order in enumerate(ORDERS):
        s = scratch[10 * n : 10 * n + 10]
        found.append(Sum(e, j, order, *s[:6], s[6:8], s[8:10]))
    return found


LATE = (3, 2, 2)
EARLY = (1, 1, 1)
OWN = 216


def spots(units, first, count):
    table = [(n, u) for n in range(3) for u in range(units[n])]
    done = 0
    while done < count:
        unit, place = divmod(first + done, 64)
        n = min(64 - place, count - done)
        yield table[unit] + (place, n, done)
        done += n


def tiles(value):
    return value.astype(BF).reshape(value.shape[0] // 16, 16, 128)


def rows_of_tiles(value):
    return value.reshape(value.shape[0] * 16, 128)


def back_kernel(lengths, home, hidden, mixed, router, routes_row, cot, tok, router_full, misc, wo, att, lse, qkv_any, normed_any, wqkv_any, layer_out, tokens_grad, q_sum, k_sum, v_sum, out_sum, router_sum, bias_sum, gain_sum, qkv, normed, wqkv, mask, diag, dout, stat, cols, dqkv, bias, branch, hidden_grad, half_out, half_in, grads, router_grad, stage, small, send, recv, core_send, core_recv, local, acc, *scratch):
    e = lax.axis_index("expert")
    j = lax.axis_index("wshard")
    jp = 1 - j
    here = pl.ds(pl.multiple_of(j * TOK, TOK), TOK)
    there = pl.ds(pl.multiple_of(jp * TOK, TOK), TOK)
    barrier = pltpu.get_barrier_semaphore()
    early, late = sums_of(e, j, scratch[:30]), sums_of(e, j, scratch[30:])
    for m in OFFSETS:
        signal(barrier, chip_at(e, m), j)
    for n in range(1, 64):
        steps = (n // 16, n // 4 % 4, n % 4)
        if 0 in steps:
            signal(barrier, early[0].peer(*steps), j)
    signal(barrier, e, jp)

    loads = [pltpu.make_async_copy(src, dst, local.at[n]) for n, (src, dst) in enumerate(((qkv_any, qkv), (normed_any, normed), (wqkv_any, wqkv)))]
    for c in loads:
        c.start()

    chosen, first, second = placing(routes_row)
    probs = router[...]
    gate = jnp.sum(probs * chosen, axis=1, keepdims=True)
    made = mm(first, home[0]) + mm(second, home[1])
    expert_back = mm(first, home[2]) + mm(second, home[3])
    total = hidden[...]
    layer_out[...] = (total + gate * made).astype(BF)
    dy = cot[...].astype(F32)
    gate_grad = jnp.sum(dy * made, axis=1, keepdims=True)
    logit_grad = ((gate_grad * gate) * (chosen - probs)).astype(BF)
    mixed_grad = mm(logit_grad, router_full[...], NT) + expert_back
    r = lax.rsqrt(jnp.mean(total * total, axis=-1, keepdims=True) + EPSILON)
    w = mixed_grad * both_gains(misc, 17)
    mix_gain = jnp.sum(mixed_grad * total * r, axis=0, keepdims=True)
    rest = dy + (r * w - total * (r * r * r * jnp.mean(w * total, axis=-1, keepdims=True)))
    hidden_grad[...] = rest
    branch[here, :] = rest.astype(BF)

    pl.semaphore_wait(barrier, len(OFFSETS) + 37)
    trade = remote(branch.at[here, :], branch.at[here, :], core_send.at[0], core_recv.at[0], e, jp)
    trade.start()
    router_grad[...] = tiles(mm(mixed[...], logit_grad, TN))
    router_rows = lambda core: router_grad.at[pl.ds(core * 24, 24)]
    router_trade = remote(router_rows(jp), early[2].part.at[0, 40:64], core_send.at[1], core_recv.at[1], e, jp)
    router_trade.start()
    early[2].part[0, 16:40] = router_grad[pl.ds(j * 24, 24)]
    prepare(lengths, mask)
    prepare_biases(misc, diag, (1, -1))
    trade.wait_recv()

    lane = lax.broadcasted_iota(jnp.int32, (CHIP, 128), 1)
    mid = slice(MID, MID + CHIP)
    att_grad = mm(branch[...], wo[...], NT).astype(BF)
    dout[mid, :] = att_grad
    both = att_grad.astype(F32) * att[...].astype(F32)
    dots = jnp.zeros((CHIP, 128), F32)
    for h in range(6):
        own = (lane // HEAD) == h % 2
        dot = jnp.sum(jnp.where(own, both[:, (h // 2) * 128 : (h // 2) * 128 + 128], 0.0), axis=1, keepdims=True)
        dots = jnp.where(lane == h, dot, dots)
    stat[REACH, 0:8] = lse[...]
    stat[REACH, 8:16] = dots.T[0:8, :]
    cols[...] = jnp.concatenate([stat[REACH], jnp.zeros((112, CHIP), F32)], axis=0).T

    def window_copies(n):
        m = OFFSETS[n]
        slot = REACH if n < DIRECT else REACH - m // 2
        to = chip_at(e, m if n < DIRECT else m // 2)
        return [
            remote(dout.at[chunk(slot), :], dout.at[chunk(REACH - m), :], send.at[n, 0], recv.at[n, 0], to, j),
            remote(stat.at[slot], stat.at[REACH - m], send.at[n, 1], recv.at[n, 1], to, j),
        ]

    for n in range(DIRECT):
        for c in window_copies(n):
            c.start()
    grad = mm(att[...], branch[...], TN)
    for c in range(6):
        cut = tiles(grad[:, c * 128 : (c + 1) * 128])
        for n, unit, place, count, done in spots(EARLY, 24 * c, 24):
            early[n].part[unit, place : place + count] = cut[done : done + count]
    router_trade.wait_recv()
    for s in early:
        s.start_ring()
    for c in loads:
        c.wait()

    def forward_window():
        for n in range(2):
            for c in window_copies(n):
                c.wait_recv()
            for c in window_copies(DIRECT + n):
                c.start()

    def pass_early():
        for s in early:
            s.pass_ring()

    line = lax.broadcasted_iota(jnp.int32, (NB, 128), 1)
    row32 = lax.broadcasted_iota(jnp.int32, (NB, 128), 0)
    hot = diagonal_buckets(1)
    bias[...] = jnp.zeros((NB, 128), F32)

    def by_queries(p, carry):
        q = tile(qkv, mid, p * 128, 128).astype(F32) * 0.125
        do = tile(dout, mid, p * 128, 128)
        found = []
        for hh in range(2):
            h = 2 * p + hh
            own = (lane // HEAD) == hh
            spare = (1 - hh) * HEAD
            qm = jnp.where(own, q, 0.0).astype(BF)
            dom = jnp.where(own, do, jnp.zeros_like(do))
            log_sum = jnp.sum(jnp.where(lane == h, cols[...], 0.0), axis=1, keepdims=True)
            dot = jnp.sum(jnp.where(lane == h + 8, cols[...], 0.0), axis=1, keepdims=True)
            near, left, right = near_tile(diag, j * 6 + h)
            dq = jnp.zeros((CHIP, 128), F32)
            near_grads = []
            for c in range(SLOTS):
                k = tile(qkv, chunk(c), HALF + p * 128, 128)
                v = tile(qkv, chunk(c), 2 * HALF + p * 128, 128)
                s = biased(mm(qm, k, NT), c, mask, near, left, right)
                ds = jnp.exp(s - log_sum) * (mm(dom, v, NT) - dot)
                if c < REACH - 1:
                    other = jnp.where(lane == spare, 1.0, 0.0).astype(BF)
                elif c > REACH + 1:
                    other = jnp.where(lane == spare + 1, 1.0, 0.0).astype(BF)
                else:
                    other = jnp.zeros((CHIP, 128), BF)
                    near_grads.append(ds)
                dq = dq + mm(ds.astype(BF), jnp.where(own, k, other))
            found.append(dq * 0.125)
            fold = jnp.concatenate(near_grads + [jnp.zeros((CHIP, CHIP), F32)], axis=1)
            rows = CHIP
            while rows > 8:
                rows //= 2
                fold = fold[0:rows] + pltpu.roll(fold[rows : 2 * rows], LOOP - rows, 1)
            summed = fold[0:1]
            for n in range(1, 8):
                summed = summed + pltpu.roll(fold[n : n + 1], LOOP - n, 1)
            by_bucket = jnp.sum(hot * summed, axis=1, keepdims=True)
            far = jnp.sum(dq, axis=0, keepdims=True)
            by_bucket = by_bucket + jnp.where(row32 == 15, far[:, spare : spare + 1], 0.0) + jnp.where(row32 == 31, far[:, spare + 1 : spare + 2], 0.0)
            bias[...] = jnp.where(line == j * 6 + h, by_bucket, bias[...])
            if hh == 0:
                pl.when(p == 0)(forward_window)
                pl.when(p == 2)(pass_early)
        dqkv[:, pl.ds(pl.multiple_of(p * 128, 128), 128)] = jnp.where(lane < HEAD, found[0], found[1]).astype(BF)
        return carry

    lax.fori_loop(0, 3, by_queries, 0)

    def by_keys(slots, p, carry):
        k_own = tile(qkv, mid, HALF + p * 128, 128)
        v_own = tile(qkv, mid, 2 * HALF + p * 128, 128)
        found = []
        for hh in range(2):
            h = 2 * p + hh
            own = (lane // HEAD) == hh
            km = jnp.where(own, k_own, jnp.zeros_like(k_own))
            vm = jnp.where(own, v_own, jnp.zeros_like(v_own))
            if REACH in slots:
                near, left, right = near_tile(diag, 16 + j * 6 + h)
            else:
                ends = diag[pl.ds(16 + j * 6 + h, 1), :]
                near, left, right = None, ends[:, 0:1], ends[:, NEAR - 1 : NEAR]
            dk = jnp.zeros((CHIP, 128), F32)
            dv = jnp.zeros((CHIP, 128), F32)
            for c in slots:
                qc = (tile(qkv, chunk(c), p * 128, 128).astype(F32) * 0.125).astype(BF)
                dc = tile(dout, chunk(c), p * 128, 128)
                s = biased(mm(km, qc, NT), c, mask, near, left, right)
                prob = jnp.exp(s - stat[c, pl.ds(h, 1), :])
                ds = prob * (mm(vm, dc, NT) - stat[c, pl.ds(h + 8, 1), :])
                dv = dv + mm(prob.astype(BF), dc)
                dk = dk + mm(ds.astype(BF), qc)
            found.append((dk, dv))
        for n in range(2):
            where = pl.ds(pl.multiple_of(n * HALF + p * 128, 128), 128)
            both = jnp.where(lane < HEAD, found[0][n], found[1][n])
            acc[:, where] = both if REACH in slots else acc[:, where] + both
        return carry

    for n, slots in ((1, (REACH, 3, 5)), (2, (0, 8)), (4, (1, 7)), (6, (2, 6))):
        if n > 1:
            for c in window_copies(n) + window_copies(n + 1):
                c.wait_recv()
        lax.fori_loop(0, 3, functools.partial(by_keys, slots), 0)
        if n == 1:
            for s in early:
                s.ring_to_plane()
        elif n == 4:
            for s in early:
                s.plane_back()
    dqkv[:, HALF:] = acc[...].astype(BF)

    half_out[...] = mm(dqkv[there, :], wqkv[...], NT).astype(BF)
    half_trade = remote(half_out, half_in, core_send.at[2], core_recv.at[2], e, jp)
    half_trade.start()
    whole = tuple(s.part for s in late)
    swaps = []
    for n, unit, place, count, done in spots(LATE, OWN, OWN):
        swaps.append((done + count, remote(stage.at[done : done + count], whole[n].at[unit, place : place + count], core_send.at[4 + len(swaps)], core_recv.at[4 + len(swaps)], e, jp)))
    sent = 0
    for third in range(3):
        grad = mm(normed[...], dqkv[:, third * HALF : (third + 1) * HALF], TN)
        for c in range(3 * third, 3 * third + 3):
            grads[c % 3] = tiles(grad[:, (c % 3) * 128 : (c % 3 + 1) * 128])
            stage[24 * c : 24 * c + 24] = grads[c % 3, pl.ds(24 * jp, 24)]
            for n, unit, place, count, done in spots(LATE, 24 * c, 24):
                whole[n][unit, place : place + count] = grads[c % 3, pl.ds(24 * j + done, count)]
        while sent < len(swaps) and swaps[sent][0] <= 72 * (third + 1):
            swaps[sent][1].start()
            sent += 1
    late[0].start_ring()
    for s in early:
        s.plane_to_ring()

    half = mm(dqkv[here, :], wqkv[...], NT)
    half_trade.wait_recv()
    grad = half + half_in[...].astype(F32)
    x = tok[...].astype(F32)
    r = lax.rsqrt(jnp.mean(x * x, axis=-1, keepdims=True) + EPSILON)
    w = grad * both_gains(misc, 16)
    tokens_grad[...] = (hidden_grad[...] + (r * w - x * (r * r * r * jnp.mean(w * x, axis=-1, keepdims=True)))).astype(BF)
    attn_gain = jnp.sum(grad * x * r, axis=0, keepdims=True)
    for h in range(2):
        lines = [v[:, h * HALF + 128 * n : h * HALF + 128 * n + 128] for v in (attn_gain, mix_gain) for n in range(3)]
        small[2 * h] = bias[16 * h : 16 * h + 16, :].astype(BF)
        small[2 * h + 1] = jnp.concatenate(lines + [jnp.zeros((10, 128), F32)], axis=0).astype(BF)
    last = whole[2]
    last[1, 52:64] = jnp.zeros((12, 16, 128), BF)
    last[1, 48:50] = small[pl.ds(2 * j, 2)]
    small_trade = remote(small.at[pl.ds(2 * jp, 2)], last.at[1, 50:52], core_send.at[3], core_recv.at[3], e, jp)
    small_trade.start()
    late[0].pass_ring()
    for _, c in swaps:
        c.wait_recv()
    late[1].start_ring()
    small_trade.wait_recv()
    late[2].start_ring()
    for s in early:
        s.pass_back()
    for s in late[1:]:
        s.pass_ring()
    for s in late:
        s.ring_to_plane()

    for s in early:
        s.end()
    for c in range(6):
        for n, unit, place, count, done in spots(EARLY, 24 * c, 24):
            out_sum[16 * done : 16 * (done + count), c * 128 : (c + 1) * 128] = rows_of_tiles(early[n].all[unit, place : place + count])
    router_sum[...] = rows_of_tiles(early[2].all[0, 16:40].astype(F32) + early[2].all[0, 40:64].astype(F32))

    for step in ("plane_back", "plane_to_ring", "pass_back", "end"):
        for s in late:
            getattr(s, step)()
    sums = (q_sum, k_sum, v_sum)
    for c in range(9):
        for first_tile, core in ((24 * c, j), (OWN + 24 * c, jp)):
            column = pl.ds(pl.multiple_of(core * HALF + (c % 3) * 128, 128), 128)
            for n, unit, place, count, done in spots(LATE, first_tile, 24):
                sums[c // 3][16 * done : 16 * (done + count), column] = rows_of_tiles(late[n].all[unit, place : place + count])
    smalls = late[2].all[1, 48:50].astype(F32) + late[2].all[1, 50:52].astype(F32)
    bias_sum[...] = smalls[0]
    gain_sum[...] = smalls[1]

    for c in (trade, router_trade, half_trade, small_trade):
        c.wait_send()
    for _, c in swaps:
        c.wait_send()
    for n in range(len(OFFSETS)):
        for c in window_copies(n):
            c.wait_send()
    for s in early + late:
        s.end_sends()


def back(lengths, *operands):
    vm = pl.BlockSpec(memory_space=pltpu.VMEM)
    return pl.pallas_call(
        back_kernel,
        name="back",
        out_shape=(
            jax.ShapeDtypeStruct((TOK, D), BF),
            jax.ShapeDtypeStruct((TOK, D), BF),
            jax.ShapeDtypeStruct((HALF, D), BF),
            jax.ShapeDtypeStruct((HALF, D), BF),
            jax.ShapeDtypeStruct((HALF, D), BF),
            jax.ShapeDtypeStruct((HALF, D), BF),
            jax.ShapeDtypeStruct((HALF, EXPERTS), F32),
            jax.ShapeDtypeStruct((16, 128), F32),
            jax.ShapeDtypeStruct((16, 128), F32),
        ),
        in_specs=[pl.BlockSpec(memory_space=pltpu.SMEM)] + [vm] * 12 + [pl.BlockSpec(memory_space=pl.ANY)] * 3,
        out_specs=(vm,) * 9,
        scratch_shapes=[
            pltpu.VMEM((WIN, 3 * HALF), BF),
            pltpu.VMEM((CHIP, D), BF),
            pltpu.VMEM((D, 3 * HALF), BF),
            pltpu.VMEM((CHIP, WIN), F32),
            pltpu.VMEM((32, LOOP), F32),
            pltpu.VMEM((WIN, HALF), BF),
            pltpu.VMEM((SLOTS, 16, CHIP), F32),
            pltpu.VMEM((CHIP, 128), F32),
            pltpu.VMEM((CHIP, 3 * HALF), BF),
            pltpu.VMEM((NB, 128), F32),
            pltpu.VMEM((CHIP, D), BF),
            pltpu.VMEM((TOK, D), F32),
            pltpu.VMEM((TOK, D), BF),
            pltpu.VMEM((TOK, D), BF),
            pltpu.VMEM((3, 48, 16, 128), BF),
            pltpu.VMEM((48, 16, 128), BF),
            pltpu.VMEM((OWN, 16, 128), BF),
            pltpu.VMEM((4, 16, 128), BF),
            pltpu.SemaphoreType.DMA((8, 2)),
            pltpu.SemaphoreType.DMA((8, 2)),
            pltpu.SemaphoreType.DMA((8,)),
            pltpu.SemaphoreType.DMA((8,)),
            pltpu.SemaphoreType.DMA((3,)),
            pltpu.VMEM((CHIP, 2 * HALF), F32),
            *[s for units in EARLY + LATE for s in sum_scratch(units)],
        ],
        compiler_params=pltpu.CompilerParams(collective_id=2, has_side_effects=True, vmem_limit_bytes=VMEM_BYTES),
    )(lengths, *operands)


def finish_kernel(*refs):
    for src, dst in zip(refs[:8], refs[8:]):
        dst[...] = src[:, 0 : dst.shape[1]].astype(dst.dtype)


def finish(*results):
    vm = pl.BlockSpec(memory_space=pltpu.VMEM)
    kinds = ((TOK, D, BF), (TOK, D, BF)) + ((HALF, D, F32),) * 4 + ((HALF, EXPERTS, F32), (16, 12, F32))
    return pl.pallas_call(
        finish_kernel,
        name="finish",
        out_shape=tuple(jax.ShapeDtypeStruct((rows, columns), kind) for rows, columns, kind in kinds),
        in_specs=[vm] * 8,
        out_specs=(vm,) * 8,
        compiler_params=pltpu.CompilerParams(vmem_limit_bytes=VMEM_BYTES),
    )(*results)


def to_all(rows):
    return lax.all_to_all(rows, ("expert", "wshard"), split_axis=1, concat_axis=1, tiled=True)


def per_device(tokens, lengths, routes, attn_gain, query_weight, key_weight, value_weight, output_weight, bias_table, mix_gain, router_weight, expert_in, expert_out, cotangent):
    misc = jnp.zeros((24, HALF), F32)
    misc = misc.at[0:16, 0:12].set(bias_table.astype(F32))
    misc = misc.at[16].set(attn_gain.astype(F32)).at[17].set(mix_gain.astype(F32))
    row = routes.reshape(1, TOK)
    qkv, normed, wqkv, router_full, misc_full, att, lse, hidden, mixed, router, sent = front(
        lengths, tokens, query_weight, key_weight, value_weight, output_weight, router_weight, misc, row, cotangent
    )

    arrived = to_all(sent).reshape(4 * EXPERTS, D)
    made_back, expert_in_grad, expert_out_grad = expert(arrived, expert_in, expert_out)
    home = to_all(made_back.reshape(4, EXPERTS, D))
    *results, gain_sum = back(lengths, home, hidden, mixed, router, row, cotangent, tokens, router_full, misc_full, output_weight, att, lse, qkv, normed, wqkv)
    layer_out, tokens_grad, query_grad, key_grad, value_grad, output_grad, router_grad, bias_grad = finish(*results)
    return (
        layer_out,
        tokens_grad,
        gain_sum[0:3].reshape(HALF),
        query_grad,
        key_grad,
        value_grad,
        output_grad,
        bias_grad,
        gain_sum[3:6].reshape(HALF),
        router_grad,
        expert_in_grad,
        expert_out_grad,
    )


def solution(mesh):
    by_token = P(("expert", "wshard"), None)
    by_row = P("wshard", None)
    by_expert = P(("expert", "wshard"), None, None)
    return jax.shard_map(
        per_device,
        mesh=mesh,
        in_specs=(
            by_token,
            P(),
            by_token,
            P("wshard"),
            by_row,
            by_row,
            by_row,
            by_row,
            by_row,
            P("wshard"),
            by_row,
            by_expert,
            by_expert,
            by_token,
        ),
        out_specs=(
            by_token,
            by_token,
            P("wshard"),
            by_row,
            by_row,
            by_row,
            by_row,
            by_row,
            P("wshard"),
            by_row,
            by_expert,
            by_expert,
        ),
        check_vma=False,
    )
```

time: 252 us -> 202 us (0.80)
  Pallas kernels: 172 us -> 145 us
  other arithmetic: 9.68 us -> 0.69 us
  local copies, waits for them, and re-layouts: 13.6 us -> 8.8 us
  matrix products: 4.53 us -> 0 us
    pallas_call x5 -> x3, Pallas kernels: 159 us -> 132 us  [the longest x1 86.9 us: back(): pl.pallas_call(back_kernel, name='back', out_shape=(jax.ShapeDtypeStruct(...]
    convert_element_type x7 -> x0, other arithmetic: 6.75 us -> none  [the longest x1 2.25 us: per_device(): q_sum.astype(F32)]
    dot_general x12 -> x0, matrix products: 4.53 us -> none  [mm(): return lax.dot_general(left, right, dims, preferred_element_type=F32)]
  transfers between devices with their start and end apart: 2 -> 0, of which waited for: 1 -> 0; matrix products, arithmetic and copies ran while one was open for 0% -> 0% of each run, Pallas kernels for 0% -> 0%
where the time goes in v2:
time: 202 us; the launch traced here: 201 us
  Pallas kernels  145 us (72%)
  blocking collectives  45.9 us (23%)
  local copies, waits for them, and re-layouts  8.8 us (4%)
    pallas_call x1, Pallas kernels, back(): pl.pallas_call(back_kernel, name='back', out_shape=(jax.ShapeDtypeStruct(...  86.9 us
    all_to_all x2, blocking collectives, to_all(): lax.all_to_all(rows, ('expert', 'wshard'), split_axis=1, concat_axis=1, t...  45.9 us
    pallas_call x1, Pallas kernels, front(): pl.pallas_call(front_kernel, name='front', out_shape=(jax.ShapeDtypeStruc...  40.7 us
    pallas_call x1, Pallas kernels, expert(): pl.pallas_call(expert_kernel, name='expert', grid=(FF // FF_TILE,), out_s...  13 us
    pallas_call x1, Pallas kernels, finish(): pl.pallas_call(finish_kernel, name='finish', out_shape=tuple((jax.ShapeDt...  4.2 us

profile of v2, /device:TPU:8, one launch (start us, length us, event | category | flops | bytes accessed | tf_op | source)
XLA Modules:
  0.0 200.9 jit_solution(7276834844229179877)
XLA Ops:
  0.6 0.7 reshape.128
  1.3 0.7 reshape.129
  2.0 0.7 pad_convert_fusion
  2.7 0.1 scatter.20.misc_any
  2.8 0.0 copy-start
  2.8 0.6 copy-done
  3.4 40.7 %front.1 = (bf16[2304,1152]{1,0:T(8,128)(2,1)}, bf16[256,768]{1,0:T(8,128)(2,1)}, bf16[768,1152]{1,0:T(8,128)(2,1)}, bf16[768,128]{1,0:T(8,128)(2,1)}, f32[48,38...) custom-call(s32[32]{0:T(128)} %lengths.3, ...), custom_call_target="tpu_custom_call" | custom-call | tf_op jit(solution)/shard_map/front/pallas_call | solution.py:284
  44.1 1.7 copy.26
  45.9 25.3 %all_to_all.10 = bf16[4,128,768]{2,0,1:T(4,128)(2,1)S(1)} all-to-all(bf16[4,128,768]{2,0,1:T(4,128)(2,1)S(1)} %copy.26), channel_id=1, replica_groups=mesh['expert'=64,'wshard'=2] {'expert','wshard'}, dimensions={1} | all-to-all | bytes 1572864 | tf_op jit(solution)/shard_map/all_to_all | solution.py:885
  71.2 1.0 copy.27
  72.1 13.0 %expert.1 = (bf16[512,768]{1,0:T(8,128)(2,1)}, bf16[1,768,3072]{2,1,0:T(8,128)(2,1)}, bf16[1,3072,768]{2,1,0:T(8,128)(2,1)}) custom-call(bf16[512,768]{1,0:T(8,128)(2,1)} %bitcast.7, bf16[512,768]{1,0:T(8,128)(2,1)} %bitcast.8, bf16[1,768,3072]{2,1,0:T(8,128)(2,1)} %w_in.1, bf16[1,3072,768]{2,1,0:T(8,128)(2,1)} %w_out.1), custom_call_target="tpu_custom_call" | custom-call | tf_op jit(solution)/shard_map/expert/pallas_call | solution.py:361
  85.1 1.7 copy.28
  86.9 20.7 %all_to_all.11 = bf16[4,128,768]{2,0,1:T(4,128)(2,1)S(1)} all-to-all(bf16[4,128,768]{2,0,1:T(4,128)(2,1)S(1)} %copy.28), channel_id=1, replica_groups=mesh['expert'=64,'wshard'=2] {'expert','wshard'}, dimensions={1} | all-to-all | bytes 1572864 | tf_op jit(solution)/shard_map/all_to_all | solution.py:885
  107.5 1.0 copy.29.home
  108.5 86.9 %back.1 = (bf16[128,768]{1,0:T(8,128)(2,1)}, bf16[128,768]{1,0:T(8,128)(2,1)}, bf16[384,768]{1,0:T(8,128)(2,1)}, bf16[384,768]{1,0:T(8,128)(2,1)}, bf16[384,768]...) custom-call(s32[32]{0:T(128)} %lengths.3, ...), custom_call_target="tpu_custom_call" | custom-call | tf_op jit(solution)/shard_map/back/pallas_call | solution.py:819
  195.4 1.3 slice_bitcast_fusion
  196.7 4.2 %finish.1 = (bf16[128,768]{1,0:T(8,128)(2,1)}, bf16[128,768]{1,0:T(8,128)(2,1)}, f32[384,768]{1,0:T(8,128)}, f32[384,768]{1,0:T(8,128)}, f32[384,768]{1,0:T(8,12...) custom-call(bf16[128,768]{1,0:T(8,128)(2,1)} %get-tuple-element.91.refs_0_, ...), custom_call_target="tpu_custom_call" | custom-call | tf_op jit(solution)/shard_map/finish/pallas_call | solution.py:874
  (1 shorter events, 0.0 us)
Async XLA Ops:
  2.8 0.6 copy-start

commit v3 on v2

--- a/solution.py
+++ b/solution.py
@@ -131,11 +131,15 @@
 
 def near_tile(diag, row):
     line = diag[pl.ds(row, 1), :]
-    spread = pltpu.roll(jnp.broadcast_to(line, (CHIP, LOOP)), 0, 1, stride=1, stride_axis=0)
+    spread = pltpu.roll(jnp.broadcast_to(line, (8, LOOP)), 0, 1, stride=1, stride_axis=0)
+    rows = 8
+    while rows < CHIP:
+        spread = jnp.concatenate([spread, pltpu.roll(spread, rows, 1)], axis=0)
+        rows *= 2
     return spread[:, 0:NEAR], line[:, 0:1], line[:, NEAR - 1 : NEAR]
 
 
-def front_kernel(lengths, tok_any, wq, wk, wv, wo_any, router_any, misc_any, tok, wo, routes_row, cot, qkv_any, normed_any, wqkv_any, router_full, misc, att, lse, hidden, mixed, router, sent, qkv, normed, wqkv, win, wo_other, att_other, mask, diag, scores, lse_cols, send, recv, fsend, frecv, wsend, wrecv, local, store):
+def front_kernel(lengths, tok_any, wq, wk, wv, wo_any, router_any, gain_one, gain_two, bias_rows, tok, wo, routes_row, cot, qkv_any, normed_any, wqkv_any, router_full, misc, att, lse, hidden, mixed, router, sent, qkv, normed, wqkv, misc_mine, win, wo_other, att_other, mask, diag, scores, lse_cols, send, recv, fsend, frecv, wsend, wrecv, local, store):
     e = lax.axis_index("expert")
     j = lax.axis_index("wshard")
     jp = 1 - j
@@ -147,6 +151,10 @@
     def rows_of(slot, core):
         return win.at[pl.ds(pl.multiple_of(slot * CHIP + core * TOK, TOK), TOK), :]
 
+    misc_mine[...] = jnp.zeros((24, HALF), F32)
+    misc_mine[16:17, :] = gain_one[...].astype(F32).reshape(1, HALF)
+    misc_mine[17:18, :] = gain_two[...].astype(F32).reshape(1, HALF)
+    misc_mine[0:16, 0:12] = bias_rows[...].astype(F32)
     weights = []
     kept = []
     for n, w in enumerate((wq, wk, wv)):
@@ -156,7 +164,7 @@
         dst = wqkv.at[rows, n * HALF : (n + 1) * HALF]
         weights.append(remote(there, dst, wsend.at[n], wrecv.at[n], e, jp))
         kept.append(pltpu.make_async_copy(here, dst, local.at[1 + n]))
-    for n, (src, dst, size) in enumerate(((misc_any, misc, 24), (router_any, router_full, HALF))):
+    for n, (src, dst, size) in enumerate(((misc_mine, misc, 24), (router_any, router_full, HALF))):
         rows = pl.ds(pl.multiple_of(j * size, 8), size)
         weights.append(remote(src, dst.at[rows, :], wsend.at[3 + n], wrecv.at[3 + n], e, jp))
         kept.append(pltpu.make_async_copy(src, dst.at[rows, :], local.at[4 + n]))
@@ -277,7 +285,7 @@
         c.wait()
 
 
-def front(lengths, tokens, wq, wk, wv, wo, router, misc, row, cotangent):
+def front(lengths, tokens, wq, wk, wv, wo, router, gain_one, gain_two, bias, row, cotangent):
     smem = pl.BlockSpec(memory_space=pltpu.SMEM)
     hbm = pl.BlockSpec(memory_space=pl.ANY)
     vm = pl.BlockSpec(memory_space=pltpu.VMEM)
@@ -297,12 +305,13 @@
             jax.ShapeDtypeStruct((TOK, EXPERTS), F32),
             jax.ShapeDtypeStruct((4, EXPERTS, D), BF),
         ),
-        in_specs=[smem] + [hbm] * 7 + [vm] * 4,
+        in_specs=[smem] + [hbm] * 6 + [vm] * 7,
         out_specs=(hbm,) * 3 + (vm,) * 8,
         scratch_shapes=[
             pltpu.VMEM((WIN, 3 * HALF), BF),
             pltpu.VMEM((CHIP, D), BF),
             pltpu.VMEM((D, 3 * HALF), BF),
+            pltpu.VMEM((24, HALF), F32),
             pltpu.VMEM((WIN, D), BF),
             pltpu.VMEM((HALF, D), BF),
             pltpu.VMEM((TOK, HALF), BF),
@@ -320,19 +329,20 @@
             pltpu.SemaphoreType.DMA((3,)),
         ],
         compiler_params=pltpu.CompilerParams(collective_id=1, has_side_effects=True, vmem_limit_bytes=VMEM_BYTES),
-    )(lengths, tokens, wq, wk, wv, wo, router, misc, tokens, wo, row, cotangent)
+    )(lengths, tokens, wq, wk, wv, wo, router, gain_one, gain_two, bias, tokens, wo, row, cotangent)
 
 
 FF_TILE = 512
 
 
-def expert_kernel(x, g, w_in, w_out, made_back, d_in, d_out, made_sum, back_sum):
+def expert_kernel(x, g, w_in, w_out, made_back, d_in, d_out, made_sum, back_sum, across):
     step = pl.program_id(0)
 
     @pl.when(step == 0)
     def _():
         made_sum[...] = jnp.zeros_like(made_sum)
         back_sum[...] = jnp.zeros_like(back_sum)
+        across[...] = x[...].T
 
     pre = mm(x[...], w_in[0])
     half_erf = 0.5 * lax.erf(pre * (0.5**0.5)) + 0.5
@@ -343,7 +353,7 @@
     made_sum[...] += mm(act, w_out[0])
     back_sum[...] += mm(pre_grad, w_in[0], NT)
     d_out[0] = mm(act, g[...], TN).astype(BF)
-    d_in[0] = mm(x[...], pre_grad, TN).astype(BF)
+    d_in[0] = mm(across[...], pre_grad).astype(BF)
 
     @pl.when(step == pl.num_programs(0) - 1)
     def _():
@@ -369,12 +379,13 @@
         ),
         in_specs=[forward, backward, by_in, by_out],
         out_specs=(whole, by_in, by_out),
-        scratch_shapes=[pltpu.VMEM((rows, D), F32), pltpu.VMEM((rows, D), F32)],
+        scratch_shapes=[pltpu.VMEM((rows, D), F32), pltpu.VMEM((rows, D), F32), pltpu.VMEM((D, rows), BF)],
         compiler_params=pltpu.CompilerParams(vmem_limit_bytes=VMEM_BYTES, dimension_semantics=("arbitrary",)),
     )(arrived, arrived, w_in, w_out)
 
 
 ORDERS = ("zxy", "xyz", "yzx")
+EARLY_ORDERS = ("yxz",)
 RING = 16
 PLANE = [(d, f) for d in range(4) for f in range(4) if d + f > 0]
 
@@ -504,21 +515,21 @@
     ]
 
 
-def sums_of(e, j, scratch):
+def sums_of(e, j, orders, scratch):
     found = []
-    for n, order in enumerate(ORDERS):
+    for n, order in enumerate(orders):
         s = scratch[10 * n : 10 * n + 10]
         found.append(Sum(e, j, order, *s[:6], s[6:8], s[8:10]))
     return found
 
 
 LATE = (3, 2, 2)
-EARLY = (1, 1, 1)
+EARLY = (3,)
 OWN = 216
 
 
 def spots(units, first, count):
-    table = [(n, u) for n in range(3) for u in range(units[n])]
+    table = [(n, u) for n in range(len(units)) for u in range(units[n])]
     done = 0
     while done < count:
         unit, place = divmod(first + done, 64)
@@ -542,7 +553,7 @@
     here = pl.ds(pl.multiple_of(j * TOK, TOK), TOK)
     there = pl.ds(pl.multiple_of(jp * TOK, TOK), TOK)
     barrier = pltpu.get_barrier_semaphore()
-    early, late = sums_of(e, j, scratch[:30]), sums_of(e, j, scratch[30:])
+    early, late = sums_of(e, j, EARLY_ORDERS, scratch[:10]), sums_of(e, j, ORDERS, scratch[10:])
     for m in OFFSETS:
         signal(barrier, chip_at(e, m), j)
     for n in range(1, 64):
@@ -578,9 +589,9 @@
     trade.start()
     router_grad[...] = tiles(mm(mixed[...], logit_grad, TN))
     router_rows = lambda core: router_grad.at[pl.ds(core * 24, 24)]
-    router_trade = remote(router_rows(jp), early[2].part.at[0, 40:64], core_send.at[1], core_recv.at[1], e, jp)
+    router_trade = remote(router_rows(jp), early[0].part.at[2, 40:64], core_send.at[1], core_recv.at[1], e, jp)
     router_trade.start()
-    early[2].part[0, 16:40] = router_grad[pl.ds(j * 24, 24)]
+    early[0].part[2, 16:40] = router_grad[pl.ds(j * 24, 24)]
     prepare(lengths, mask)
     prepare_biases(misc, diag, (1, -1))
     trade.wait_recv()
@@ -788,7 +799,7 @@
     for c in range(6):
         for n, unit, place, count, done in spots(EARLY, 24 * c, 24):
             out_sum[16 * done : 16 * (done + count), c * 128 : (c + 1) * 128] = rows_of_tiles(early[n].all[unit, place : place + count])
-    router_sum[...] = rows_of_tiles(early[2].all[0, 16:40].astype(F32) + early[2].all[0, 40:64].astype(F32))
+    router_sum[...] = rows_of_tiles(early[0].all[2, 16:40].astype(F32) + early[0].all[2, 40:64].astype(F32))
 
     for step in ("plane_back", "plane_to_ring", "pass_back", "end"):
         for s in late:
@@ -886,12 +897,9 @@
 
 
 def per_device(tokens, lengths, routes, attn_gain, query_weight, key_weight, value_weight, output_weight, bias_table, mix_gain, router_weight, expert_in, expert_out, cotangent):
-    misc = jnp.zeros((24, HALF), F32)
-    misc = misc.at[0:16, 0:12].set(bias_table.astype(F32))
-    misc = misc.at[16].set(attn_gain.astype(F32)).at[17].set(mix_gain.astype(F32))
     row = routes.reshape(1, TOK)
     qkv, normed, wqkv, router_full, misc_full, att, lse, hidden, mixed, router, sent = front(
-        lengths, tokens, query_weight, key_weight, value_weight, output_weight, router_weight, misc, row, cotangent
+        lengths, tokens, query_weight, key_weight, value_weight, output_weight, router_weight, attn_gain, mix_gain, bias_table, row, cotangent
     )
 
     arrived = to_all(sent).reshape(4 * EXPERTS, D)

time: 202 us -> 201 us (level)
  local copies, waits for them, and re-layouts: 8.8 us -> 6.74 us
    pallas_call x1, Pallas kernels: 86.9 us -> 89.2 us  [back(): pl.pallas_call(back_kernel, name='back', out_shape=(jax.ShapeDtypeStruct(...]
where the time goes in v3:
time: 201 us
  Pallas kernels  147 us (73%)
  blocking collectives  45.9 us (23%)
  local copies, waits for them, and re-layouts  6.74 us (3%)
    pallas_call x1, Pallas kernels, back(): pl.pallas_call(back_kernel, name='back', out_shape=(jax.ShapeDtypeStruct(...  89.2 us
    all_to_all x2, blocking collectives, to_all(): lax.all_to_all(rows, ('expert', 'wshard'), split_axis=1, concat_axis=1, t...  45.9 us
    pallas_call x1, Pallas kernels, front(): pl.pallas_call(front_kernel, name='front', out_shape=(jax.ShapeDtypeStruc...  40.8 us
    pallas_call x1, Pallas kernels, expert(): pl.pallas_call(expert_kernel, name='expert', grid=(FF // FF_TILE,), out_s...  13.1 us
    pallas_call x1, Pallas kernels, finish(): pl.pallas_call(finish_kernel, name='finish', out_shape=tuple((jax.ShapeDt...  4.2 us

profile of v3, /device:TPU:8, one launch (start us, length us, event | category | flops | bytes accessed | tf_op | source)
XLA Modules:
  0.0 200.7 jit_solution(16280837759268223905)
XLA Ops:
  0.6 40.8 %front.1 = (bf16[2304,1152]{1,0:T(8,128)(2,1)}, bf16[256,768]{1,0:T(8,128)(2,1)}, bf16[768,1152]{1,0:T(8,128)(2,1)}, bf16[768,128]{1,0:T(8,128)(2,1)}, f32[48,38...) custom-call(s32[32]{0:T(128)} %lengths.3, ...), custom_call_target="tpu_custom_call" | custom-call | tf_op jit(solution)/shard_map/front/pallas_call | solution.py:292
  41.5 1.7 copy.26
  43.2 25.3 %all_to_all.10 = bf16[4,128,768]{2,0,1:T(4,128)(2,1)S(1)} all-to-all(bf16[4,128,768]{2,0,1:T(4,128)(2,1)S(1)} %copy.26), channel_id=1, replica_groups=mesh['expert'=64,'wshard'=2] {'expert','wshard'}, dimensions={1} | all-to-all | bytes 1572864 | tf_op jit(solution)/shard_map/all_to_all | solution.py:896
  68.5 1.0 copy.27
  69.5 13.1 %expert.1 = (bf16[512,768]{1,0:T(8,128)(2,1)}, bf16[1,768,3072]{2,1,0:T(8,128)(2,1)}, bf16[1,3072,768]{2,1,0:T(8,128)(2,1)}) custom-call(bf16[512,768]{1,0:T(8,128)(2,1)} %bitcast.7, bf16[512,768]{1,0:T(8,128)(2,1)} %bitcast.8, bf16[1,768,3072]{2,1,0:T(8,128)(2,1)} %w_in.1, bf16[1,3072,768]{2,1,0:T(8,128)(2,1)} %w_out.1), custom_call_target="tpu_custom_call" | custom-call | tf_op jit(solution)/shard_map/expert/pallas_call | solution.py:371
  82.6 1.7 copy.28
  84.3 20.7 %all_to_all.11 = bf16[4,128,768]{2,0,1:T(4,128)(2,1)S(1)} all-to-all(bf16[4,128,768]{2,0,1:T(4,128)(2,1)S(1)} %copy.28), channel_id=1, replica_groups=mesh['expert'=64,'wshard'=2] {'expert','wshard'}, dimensions={1} | all-to-all | bytes 1572864 | tf_op jit(solution)/shard_map/all_to_all | solution.py:896
  105.0 1.0 copy.29.home
  105.9 89.2 %back.1 = (bf16[128,768]{1,0:T(8,128)(2,1)}, bf16[128,768]{1,0:T(8,128)(2,1)}, bf16[384,768]{1,0:T(8,128)(2,1)}, bf16[384,768]{1,0:T(8,128)(2,1)}, bf16[384,768]...) custom-call(s32[32]{0:T(128)} %lengths.3, ...), custom_call_target="tpu_custom_call" | custom-call | tf_op jit(solution)/shard_map/back/pallas_call | solution.py:830
  195.2 1.3 slice_bitcast_fusion
  196.5 4.2 %finish.1 = (bf16[128,768]{1,0:T(8,128)(2,1)}, bf16[128,768]{1,0:T(8,128)(2,1)}, f32[384,768]{1,0:T(8,128)}, f32[384,768]{1,0:T(8,128)}, f32[384,768]{1,0:T(8,12...) custom-call(bf16[128,768]{1,0:T(8,128)(2,1)} %get-tuple-element.55.refs_0_, ...), custom_call_target="tpu_custom_call" | custom-call | tf_op jit(solution)/shard_map/finish/pallas_call | solution.py:885

commit v4 on v3

--- a/solution.py
+++ b/solution.py
@@ -26,8 +26,8 @@
 EXPERTS = 128
 NB = 32
 FF = 3072
-NEAR = 3 * CHIP
-LOOP = 1024
+NEAR = 3 * TOK
+LOOP = 512
 VMEM_BYTES = 56 * 1024 * 1024
 
 NT = (((1,), (1,)), ((), ()))
@@ -114,32 +114,45 @@
 
 def diagonal_buckets(sign):
     m = lax.broadcasted_iota(jnp.int32, (NB, LOOP), 1)
-    r = jnp.where(m < NEAR, m, m - LOOP) - CHIP
+    r = jnp.where(m < NEAR, m, m - LOOP) - TOK
     b = lax.broadcasted_iota(jnp.int32, (NB, LOOP), 0)
     return (bucket_of(sign * r) == b).astype(F32)
 
 
-def biased(raw, c, mask, near, left, right):
+def biased(raw, c, mask, near, ends):
     s = raw + mask[:, c * CHIP : (c + 1) * CHIP]
+    left, right = ends
     if c < REACH - 1:
         return s + left
     if c > REACH + 1:
         return s + right
-    lower = (c - REACH + 1) * CHIP
-    return s + near[:, lower : lower + CHIP]
-
-
-def near_tile(diag, row):
+    t = [near[:, n * TOK : (n + 1) * TOK] for n in range(3)]
+    added = {REACH - 1: (left, t[0], left, left), REACH: (t[1], t[2], t[0], t[1]), REACH + 1: (right, right, t[2], right)}[c]
+    return jnp.concatenate(
+        [jnp.concatenate([s[i * TOK : (i + 1) * TOK, n * TOK : (n + 1) * TOK] + added[2 * i + n] for n in range(2)], axis=1) for i in range(2)], axis=0
+    )
+
+
+def fill_near(diag, near, j, ways):
+    def one(n, carry):
+        line = diag[pl.ds(n // 6 * 16 + j * 6 + lax.rem(n, 6), 1), :]
+        spread = pltpu.roll(jnp.broadcast_to(line, (8, LOOP)), 0, 1, stride=1, stride_axis=0)
+        rows = 8
+        while rows < TOK:
+            spread = jnp.concatenate([spread, pltpu.roll(spread, rows, 1)], axis=0)
+            rows *= 2
+        near[n] = spread[:, 0:NEAR]
+        return carry
+
+    lax.fori_loop(0, 6 * ways, one, 0)
+
+
+def far_ends(diag, row):
     line = diag[pl.ds(row, 1), :]
-    spread = pltpu.roll(jnp.broadcast_to(line, (8, LOOP)), 0, 1, stride=1, stride_axis=0)
-    rows = 8
-    while rows < CHIP:
-        spread = jnp.concatenate([spread, pltpu.roll(spread, rows, 1)], axis=0)
-        rows *= 2
-    return spread[:, 0:NEAR], line[:, 0:1], line[:, NEAR - 1 : NEAR]
-
-
-def front_kernel(lengths, tok_any, wq, wk, wv, wo_any, router_any, gain_one, gain_two, bias_rows, tok, wo, routes_row, cot, qkv_any, normed_any, wqkv_any, router_full, misc, att, lse, hidden, mixed, router, sent, qkv, normed, wqkv, misc_mine, win, wo_other, att_other, mask, diag, scores, lse_cols, send, recv, fsend, frecv, wsend, wrecv, local, store):
+    return line[:, 0:1], line[:, NEAR - 1 : NEAR]
+
+
+def front_kernel(lengths, tok_any, wq, wk, wv, wo_any, router_any, gain_one, gain_two, bias_rows, tok, wo, routes_row, cot, qkv_any, normed_any, wqkv_any, router_full, misc, att, lse, hidden, mixed, router, sent, qkv, normed, wqkv, misc_mine, win, wo_other, att_other, mask, diag, near, scores, tops, lse_cols, send, recv, fsend, frecv, wsend, wrecv, local, store):
     e = lax.axis_index("expert")
     j = lax.axis_index("wshard")
     jp = 1 - j
@@ -198,7 +211,10 @@
     for c in weights[:4]:
         c.wait_recv()
     prepare_biases(misc, diag, (1,))
+    fill_near(diag, near, j, 1)
     gain = both_gains(misc, 16)
+
+    lane = lax.broadcasted_iota(jnp.int32, (CHIP, 128), 1)
 
     def project(slot):
         x = win[chunk(slot), :].astype(F32)
@@ -206,6 +222,20 @@
         if slot == REACH:
             normed[...] = y
         qkv[chunk(slot), :] = mm(y, wqkv[...]).astype(BF)
+
+        def score(p, carry):
+            q = tile(qkv, slice(MID, MID + CHIP), p * 128, 128).astype(F32) * 0.125
+            k = tile(qkv, chunk(slot), HALF + p * 128, 128)
+            for hh in range(2):
+                h = 2 * p + hh
+                qm = jnp.where((lane // HEAD) == hh, q, 0.0).astype(BF)
+                s = biased(mm(qm, k, NT), slot, mask, near.at[h], far_ends(diag, j * 6 + h))
+                scores[h, :, chunk(slot)] = s
+                top = jnp.maximum(s[:, 0:128], s[:, 128:256])
+                tops[h] = top if slot == REACH else jnp.maximum(tops[h], top)
+            return carry
+
+        lax.fori_loop(0, 3, score, 0)
 
     for n in range(2):
         copies[n].wait_recv()
@@ -223,32 +253,22 @@
     stores = [pltpu.make_async_copy(src, dst, store.at[n]) for n, (src, dst) in enumerate(((qkv, qkv_any), (normed, normed_any), (wqkv, wqkv_any)))]
     for c in stores:
         c.start()
-    lane = lax.broadcasted_iota(jnp.int32, (CHIP, 128), 1)
     lse_cols[...] = jnp.zeros((CHIP, 128), F32)
 
     def pair(p, carry):
-        q = tile(qkv, slice(MID, MID + CHIP), p * 128, 128).astype(F32) * 0.125
         outs = []
         for hh in range(2):
-            own = (lane // HEAD) == hh
-            qm = jnp.where(own, q, 0.0).astype(BF)
-            near, left, right = near_tile(diag, j * 6 + 2 * p + hh)
-            top = None
-            for c in range(SLOTS):
-                k = tile(qkv, chunk(c), HALF + p * 128, 128)
-                s = biased(mm(qm, k, NT), c, mask, near, left, right)
-                scores[:, chunk(c)] = s
-                top = s if top is None else jnp.maximum(top, s)
-            top = jnp.max(top, axis=1, keepdims=True)
+            h = 2 * p + hh
+            top = jnp.max(tops[h], axis=1, keepdims=True)
             total = jnp.zeros((CHIP, CHIP), F32)
             out = jnp.zeros((CHIP, 128), F32)
             for c in range(SLOTS):
-                x = jnp.exp(scores[:, chunk(c)] - top)
+                x = jnp.exp(scores[h, :, chunk(c)] - top)
                 total = total + x
                 out = out + mm(x.astype(BF), tile(qkv, chunk(c), 2 * HALF + p * 128, 128))
             total = jnp.sum(total, axis=1, keepdims=True)
             outs.append(out / total)
-            lse_cols[...] = jnp.where(lane == 2 * p + hh, top + jnp.log(total), lse_cols[...])
+            lse_cols[...] = jnp.where(lane == h, top + jnp.log(total), lse_cols[...])
         att[:, pl.ds(pl.multiple_of(p * 128, 128), 128)] = jnp.where(lane < HEAD, outs[0], outs[1]).astype(BF)
         return carry
 
@@ -317,7 +337,9 @@
             pltpu.VMEM((TOK, HALF), BF),
             pltpu.VMEM((CHIP, WIN), F32),
             pltpu.VMEM((16, LOOP), F32),
-            pltpu.VMEM((CHIP, WIN), F32),
+            pltpu.VMEM((6, TOK, NEAR), F32),
+            pltpu.VMEM((6, CHIP, WIN), F32),
+            pltpu.VMEM((6, CHIP, 128), F32),
             pltpu.VMEM((CHIP, 128), F32),
             pltpu.SemaphoreType.DMA((8,)),
             pltpu.SemaphoreType.DMA((8,)),
@@ -385,7 +407,6 @@
 
 
 ORDERS = ("zxy", "xyz", "yzx")
-EARLY_ORDERS = ("yxz",)
 RING = 16
 PLANE = [(d, f) for d in range(4) for f in range(4) if d + f > 0]
 
@@ -515,16 +536,16 @@
     ]
 
 
-def sums_of(e, j, orders, scratch):
+def sums_of(e, j, scratch):
     found = []
-    for n, order in enumerate(orders):
+    for n, order in enumerate(ORDERS):
         s = scratch[10 * n : 10 * n + 10]
         found.append(Sum(e, j, order, *s[:6], s[6:8], s[8:10]))
     return found
 
 
 LATE = (3, 2, 2)
-EARLY = (3,)
+EARLY = (1, 1, 1)
 OWN = 216
 
 
@@ -546,14 +567,14 @@
     return value.reshape(value.shape[0] * 16, 128)
 
 
-def back_kernel(lengths, home, hidden, mixed, router, routes_row, cot, tok, router_full, misc, wo, att, lse, qkv_any, normed_any, wqkv_any, layer_out, tokens_grad, q_sum, k_sum, v_sum, out_sum, router_sum, bias_sum, gain_sum, qkv, normed, wqkv, mask, diag, dout, stat, cols, dqkv, bias, branch, hidden_grad, half_out, half_in, grads, router_grad, stage, small, send, recv, core_send, core_recv, local, acc, *scratch):
+def back_kernel(lengths, home, hidden, mixed, router, routes_row, cot, tok, router_full, misc, wo, att, lse, qkv_any, normed_any, wqkv_any, layer_out, tokens_grad, q_sum, k_sum, v_sum, out_sum, router_sum, bias_sum, gain_sum, qkv, normed, wqkv, mask, diag, near, dout, stat, cols, dqkv, bias, branch, hidden_grad, half_out, half_in, grads, router_grad, stage, small, send, recv, core_send, core_recv, local, acc, *scratch):
     e = lax.axis_index("expert")
     j = lax.axis_index("wshard")
     jp = 1 - j
     here = pl.ds(pl.multiple_of(j * TOK, TOK), TOK)
     there = pl.ds(pl.multiple_of(jp * TOK, TOK), TOK)
     barrier = pltpu.get_barrier_semaphore()
-    early, late = sums_of(e, j, EARLY_ORDERS, scratch[:10]), sums_of(e, j, ORDERS, scratch[10:])
+    early, late = sums_of(e, j, scratch[:30]), sums_of(e, j, scratch[30:])
     for m in OFFSETS:
         signal(barrier, chip_at(e, m), j)
     for n in range(1, 64):
@@ -589,14 +610,16 @@
     trade.start()
     router_grad[...] = tiles(mm(mixed[...], logit_grad, TN))
     router_rows = lambda core: router_grad.at[pl.ds(core * 24, 24)]
-    router_trade = remote(router_rows(jp), early[0].part.at[2, 40:64], core_send.at[1], core_recv.at[1], e, jp)
+    router_trade = remote(router_rows(jp), early[2].part.at[0, 40:64], core_send.at[1], core_recv.at[1], e, jp)
     router_trade.start()
-    early[0].part[2, 16:40] = router_grad[pl.ds(j * 24, 24)]
+    early[2].part[0, 16:40] = router_grad[pl.ds(j * 24, 24)]
     prepare(lengths, mask)
     prepare_biases(misc, diag, (1, -1))
+    fill_near(diag, near, j, 2)
     trade.wait_recv()
 
     lane = lax.broadcasted_iota(jnp.int32, (CHIP, 128), 1)
+    low = lax.broadcasted_iota(jnp.int32, (CHIP, 128), 0) < TOK
     mid = slice(MID, MID + CHIP)
     att_grad = mm(branch[...], wo[...], NT).astype(BF)
     dout[mid, :] = att_grad
@@ -640,10 +663,6 @@
             for c in window_copies(DIRECT + n):
                 c.start()
 
-    def pass_early():
-        for s in early:
-            s.pass_ring()
-
     line = lax.broadcasted_iota(jnp.int32, (NB, 128), 1)
     row32 = lax.broadcasted_iota(jnp.int32, (NB, 128), 0)
     hot = diagonal_buckets(1)
@@ -661,25 +680,40 @@
             dom = jnp.where(own, do, jnp.zeros_like(do))
             log_sum = jnp.sum(jnp.where(lane == h, cols[...], 0.0), axis=1, keepdims=True)
             dot = jnp.sum(jnp.where(lane == h + 8, cols[...], 0.0), axis=1, keepdims=True)
-            near, left, right = near_tile(diag, j * 6 + h)
+            ends = far_ends(diag, j * 6 + h)
             dq = jnp.zeros((CHIP, 128), F32)
             near_grads = []
             for c in range(SLOTS):
                 k = tile(qkv, chunk(c), HALF + p * 128, 128)
                 v = tile(qkv, chunk(c), 2 * HALF + p * 128, 128)
-                s = biased(mm(qm, k, NT), c, mask, near, left, right)
+                s = biased(mm(qm, k, NT), c, mask, near.at[h], ends)
                 ds = jnp.exp(s - log_sum) * (mm(dom, v, NT) - dot)
                 if c < REACH - 1:
-                    other = jnp.where(lane == spare, 1.0, 0.0).astype(BF)
+                    other = lane == spare
                 elif c > REACH + 1:
-                    other = jnp.where(lane == spare + 1, 1.0, 0.0).astype(BF)
+                    other = lane == spare + 1
+                elif c == REACH - 1:
+                    other = lane == jnp.where(low, spare, spare + 2)
+                elif c == REACH + 1:
+                    other = lane == jnp.where(low, spare + 3, spare + 1)
                 else:
-                    other = jnp.zeros((CHIP, 128), BF)
+                    other = lane < 0
+                other = jnp.where(other, 1.0, 0.0).astype(BF)
+                if abs(c - REACH) < 2:
                     near_grads.append(ds)
                 dq = dq + mm(ds.astype(BF), jnp.where(own, k, other))
             found.append(dq * 0.125)
-            fold = jnp.concatenate(near_grads + [jnp.zeros((CHIP, CHIP), F32)], axis=1)
-            rows = CHIP
+            before, same, after = near_grads
+            fold = jnp.concatenate(
+                [
+                    before[0:TOK, TOK:] + same[TOK:, 0:TOK],
+                    same[0:TOK, 0:TOK] + same[TOK:, TOK:],
+                    same[0:TOK, TOK:] + after[TOK:, 0:TOK],
+                    jnp.zeros((TOK, TOK), F32),
+                ],
+                axis=1,
+            )
+            rows = TOK
             while rows > 8:
                 rows //= 2
                 fold = fold[0:rows] + pltpu.roll(fold[rows : 2 * rows], LOOP - rows, 1)
@@ -687,12 +721,15 @@
             for n in range(1, 8):
                 summed = summed + pltpu.roll(fold[n : n + 1], LOOP - n, 1)
             by_bucket = jnp.sum(hot * summed, axis=1, keepdims=True)
-            far = jnp.sum(dq, axis=0, keepdims=True)
-            by_bucket = by_bucket + jnp.where(row32 == 15, far[:, spare : spare + 1], 0.0) + jnp.where(row32 == 31, far[:, spare + 1 : spare + 2], 0.0)
+            far_low = jnp.sum(dq[0:TOK], axis=0, keepdims=True)
+            far_high = jnp.sum(dq[TOK:], axis=0, keepdims=True)
+            far = far_low + far_high
+            far_left = far[:, spare : spare + 1] + far_high[:, spare + 2 : spare + 3]
+            far_right = far[:, spare + 1 : spare + 2] + far_low[:, spare + 3 : spare + 4]
+            by_bucket = by_bucket + jnp.where(row32 == 15, far_left, 0.0) + jnp.where(row32 == 31, far_right, 0.0)
             bias[...] = jnp.where(line == j * 6 + h, by_bucket, bias[...])
             if hh == 0:
                 pl.when(p == 0)(forward_window)
-                pl.when(p == 2)(pass_early)
         dqkv[:, pl.ds(pl.multiple_of(p * 128, 128), 128)] = jnp.where(lane < HEAD, found[0], found[1]).astype(BF)
         return carry
 
@@ -707,17 +744,13 @@
             own = (lane // HEAD) == hh
             km = jnp.where(own, k_own, jnp.zeros_like(k_own))
             vm = jnp.where(own, v_own, jnp.zeros_like(v_own))
-            if REACH in slots:
-                near, left, right = near_tile(diag, 16 + j * 6 + h)
-            else:
-                ends = diag[pl.ds(16 + j * 6 + h, 1), :]
-                near, left, right = None, ends[:, 0:1], ends[:, NEAR - 1 : NEAR]
+            ends = far_ends(diag, 16 + j * 6 + h)
             dk = jnp.zeros((CHIP, 128), F32)
             dv = jnp.zeros((CHIP, 128), F32)
             for c in slots:
                 qc = (tile(qkv, chunk(c), p * 128, 128).astype(F32) * 0.125).astype(BF)
                 dc = tile(dout, chunk(c), p * 128, 128)
-                s = biased(mm(km, qc, NT), c, mask, near, left, right)
+                s = biased(mm(km, qc, NT), c, mask, near.at[6 + h], ends)
                 prob = jnp.exp(s - stat[c, pl.ds(h, 1), :])
                 ds = prob * (mm(vm, dc, NT) - stat[c, pl.ds(h + 8, 1), :])
                 dv = dv + mm(prob.astype(BF), dc)
@@ -734,12 +767,12 @@
             for c in window_copies(n) + window_copies(n + 1):
                 c.wait_recv()
         lax.fori_loop(0, 3, functools.partial(by_keys, slots), 0)
-        if n == 1:
+        if n == 2:
+            for s in early:
+                s.pass_ring()
+        elif n == 6:
             for s in early:
                 s.ring_to_plane()
-        elif n == 4:
-            for s in early:
-                s.plane_back()
     dqkv[:, HALF:] = acc[...].astype(BF)
 
     half_out[...] = mm(dqkv[there, :], wqkv[...], NT).astype(BF)
@@ -762,7 +795,7 @@
             sent += 1
     late[0].start_ring()
     for s in early:
-        s.plane_to_ring()
+        s.plane_back()
 
     half = mm(dqkv[here, :], wqkv[...], NT)
     half_trade.wait_recv()
@@ -788,20 +821,26 @@
     small_trade.wait_recv()
     late[2].start_ring()
     for s in early:
-        s.pass_back()
+        s.plane_to_ring()
     for s in late[1:]:
         s.pass_ring()
     for s in late:
         s.ring_to_plane()
+    for s in early:
+        s.pass_back()
+    for s in late:
+        s.plane_back()
+    for s in late:
+        s.plane_to_ring()
 
     for s in early:
         s.end()
     for c in range(6):
         for n, unit, place, count, done in spots(EARLY, 24 * c, 24):
             out_sum[16 * done : 16 * (done + count), c * 128 : (c + 1) * 128] = rows_of_tiles(early[n].all[unit, place : place + count])
-    router_sum[...] = rows_of_tiles(early[0].all[2, 16:40].astype(F32) + early[0].all[2, 40:64].astype(F32))
-
-    for step in ("plane_back", "plane_to_ring", "pass_back", "end"):
+    router_sum[...] = rows_of_tiles(early[2].all[0, 16:40].astype(F32) + early[2].all[0, 40:64].astype(F32))
+
+    for step in ("pass_back", "end"):
         for s in late:
             getattr(s, step)()
     sums = (q_sum, k_sum, v_sum)
@@ -849,6 +888,7 @@
             pltpu.VMEM((D, 3 * HALF), BF),
             pltpu.VMEM((CHIP, WIN), F32),
             pltpu.VMEM((32, LOOP), F32),
+            pltpu.VMEM((12, TOK, NEAR), F32),
             pltpu.VMEM((WIN, HALF), BF),
             pltpu.VMEM((SLOTS, 16, CHIP), F32),
             pltpu.VMEM((CHIP, 128), F32),

time: 201 us -> 201 us (level)
  no operation moved by 1% of the time
where the time goes in v4:
time: 201 us
  Pallas kernels  148 us (74%)
  blocking collectives  45.7 us (23%)
  local copies, waits for them, and re-layouts  6.74 us (3%)
    pallas_call x1, Pallas kernels, back(): pl.pallas_call(back_kernel, name='back', out_shape=(jax.ShapeDtypeStruct(...  90.4 us
    all_to_all x2, blocking collectives, to_all(): lax.all_to_all(rows, ('expert', 'wshard'), split_axis=1, concat_axis=1, t...  45.7 us
    pallas_call x1, Pallas kernels, front(): pl.pallas_call(front_kernel, name='front', out_shape=(jax.ShapeDtypeStruc...  40.1 us
    pallas_call x1, Pallas kernels, expert(): pl.pallas_call(expert_kernel, name='expert', grid=(FF // FF_TILE,), out_s...  13.1 us
    pallas_call x1, Pallas kernels, finish(): pl.pallas_call(finish_kernel, name='finish', out_shape=tuple((jax.ShapeDt...  4.2 us

profile of v4, /device:TPU:8, one launch (start us, length us, event | category | flops | bytes accessed | tf_op | source)
XLA Modules:
  0.0 200.9 jit_solution(17726254011532585251)
XLA Ops:
  0.6 40.1 %front.1 = (bf16[2304,1152]{1,0:T(8,128)(2,1)}, bf16[256,768]{1,0:T(8,128)(2,1)}, bf16[768,1152]{1,0:T(8,128)(2,1)}, bf16[768,128]{1,0:T(8,128)(2,1)}, f32[48,38...) custom-call(s32[32]{0:T(128)} %lengths.3, ...), custom_call_target="tpu_custom_call" | custom-call | tf_op jit(solution)/shard_map/front/pallas_call | solution.py:312
  40.7 1.7 copy.26
  42.5 25.0 %all_to_all.10 = bf16[4,128,768]{2,0,1:T(4,128)(2,1)S(1)} all-to-all(bf16[4,128,768]{2,0,1:T(4,128)(2,1)S(1)} %copy.26), channel_id=1, replica_groups=mesh['expert'=64,'wshard'=2] {'expert','wshard'}, dimensions={1} | all-to-all | bytes 1572864 | tf_op jit(solution)/shard_map/all_to_all | solution.py:936
  67.5 1.0 copy.27
  68.4 13.1 %expert.1 = (bf16[512,768]{1,0:T(8,128)(2,1)}, bf16[1,768,3072]{2,1,0:T(8,128)(2,1)}, bf16[1,3072,768]{2,1,0:T(8,128)(2,1)}) custom-call(bf16[512,768]{1,0:T(8,128)(2,1)} %bitcast.7, bf16[512,768]{1,0:T(8,128)(2,1)} %bitcast.8, bf16[1,768,3072]{2,1,0:T(8,128)(2,1)} %w_in.1, bf16[1,3072,768]{2,1,0:T(8,128)(2,1)} %w_out.1), custom_call_target="tpu_custom_call" | custom-call | tf_op jit(solution)/shard_map/expert/pallas_call | solution.py:393
  81.5 1.7 copy.28
  83.3 20.7 %all_to_all.11 = bf16[4,128,768]{2,0,1:T(4,128)(2,1)S(1)} all-to-all(bf16[4,128,768]{2,0,1:T(4,128)(2,1)S(1)} %copy.28), channel_id=1, replica_groups=mesh['expert'=64,'wshard'=2] {'expert','wshard'}, dimensions={1} | all-to-all | bytes 1572864 | tf_op jit(solution)/shard_map/all_to_all | solution.py:936
  103.9 1.0 copy.29.home
  104.9 90.4 %back.1 = (bf16[128,768]{1,0:T(8,128)(2,1)}, bf16[128,768]{1,0:T(8,128)(2,1)}, bf16[384,768]{1,0:T(8,128)(2,1)}, bf16[384,768]{1,0:T(8,128)(2,1)}, bf16[384,768]...) custom-call(s32[32]{0:T(128)} %lengths.3, ...), custom_call_target="tpu_custom_call" | custom-call | tf_op jit(solution)/shard_map/back/pallas_call | solution.py:869
  195.3 1.3 slice_bitcast_fusion
  196.7 4.2 %finish.1 = (bf16[128,768]{1,0:T(8,128)(2,1)}, bf16[128,768]{1,0:T(8,128)(2,1)}, f32[384,768]{1,0:T(8,128)}, f32[384,768]{1,0:T(8,128)}, f32[384,768]{1,0:T(8,12...) custom-call(bf16[128,768]{1,0:T(8,128)(2,1)} %get-tuple-element.55.refs_0_, ...), custom_call_target="tpu_custom_call" | custom-call | tf_op jit(solution)/shard_map/finish/pallas_call | solution.py:925
